TPU v7x, 128 devices: a whole 4x4x4 slice. The times are simulated.
128 devices in a mesh: replica: 8 (over x, y_hi), fsdp: 16 (over z, y_lo, core).
Axes of the slice: x: 4, y: 4 (y_hi: 2, y_lo: 2; y = y_hi * 2 + y_lo), z: 4, core: 2. Of those that a mesh axis runs over, the one named last changes fastest.
Arguments:
- hidden_in: bfloat16 [8, 8192, 8192], P('replica', 'fsdp'), may hold values from -6 to 6
- value_cot: bfloat16 [8, 8192, 1024], P('replica', 'fsdp'), may hold values from -6 to 6
- proj_weight: bfloat16 [8, 8192, 1024], P('replica', 'fsdp'), may hold values from -0.0625 to 0.0625
- norm_gain: float32 [8, 8192], P('replica'), may hold values from 0.5 to 1.5
- anchor: float32 [8, 16, 512, 128], P(None, 'fsdp', 'replica'), may hold values from -0.0625 to 0.0625
- momentum: float32 [8, 16, 512, 128], P(None, 'fsdp', 'replica'), may hold values from -0.078125 to 0.078125
- excluded: int32 [8, 1024], P('replica'), may hold values from 0 to 8191
- fragment: int32 [1], replicated, may hold values from 0 to 7
Outputs:
- values_out: bfloat16 [8, 8192, 1024], P('replica', 'fsdp')
- hidden_grad: bfloat16 [8, 8192, 8192], P('replica', 'fsdp')
- weight_out: bfloat16 [8, 8192, 1024], P('replica', 'fsdp')
- gain_out: float32 [8, 8192], P('replica')
- anchor_out: float32 [8, 16, 512, 128], P(None, 'fsdp', 'replica')
- momentum_out: float32 [8, 16, 512, 128], P(None, 'fsdp', 'replica')
Inputs may be any that keep to these rules, and one draw needn't show every extreme that they name: `excluded`: row indices within the replica's batch of 8192 rows; an index may repeat.
All inputs are finite; a program needn't handle non-finite values.
Results may differ from a plain program's by a relative error of at most 0.023.
Values may be sent and summed in bfloat16 or wider, within the bound.
No kernel may reach another device: no remote copies, remote signals or barrier semaphores. Data moves between devices by JAX's collectives and lax.ppermute only.
A program may use at most 192 MiB of HBM per device.

v0:
```python
import jax
import jax.numpy as jnp
from jax import lax
from jax.sharding import PartitionSpec as P

outer_momentum = 0.9
outer_rate = 0.7
mix_weight = 0.5


def body(hidden_in, value_cot, proj_weight, norm_gain, anchor, momentum, excluded, fragment):
    hidden_rows = hidden_in[0]
    row_count = hidden_rows.shape[0]
    inner_rate = 0.01 / row_count**0.5
    gain_rate = 0.1 / row_count**0.5
    weight = proj_weight[0]
    gain = norm_gain[0]
    frag = fragment[0]
    frag_cols = anchor.shape[3]
    replicas = lax.axis_size("replica")
    column_block = lax.dynamic_slice_in_dim(weight, frag * frag_cols, frag_cols, 1).astype(
        jnp.float32
    )
    anchor_local = lax.dynamic_index_in_dim(anchor, frag, 0, keepdims=False)[0]
    momentum_local = lax.dynamic_index_in_dim(momentum, frag, 0, keepdims=False)[0]
    summed_share = lax.psum_scatter(
        column_block.astype(jnp.bfloat16), "replica", scatter_dimension=0, tiled=True
    ).astype(jnp.float32)
    delta = anchor_local - summed_share / replicas
    momentum_new = outer_momentum * momentum_local + delta
    anchor_new = anchor_local - outer_rate * (delta + outer_momentum * momentum_new)
    anchor_full = lax.all_gather(
        anchor_new.astype(jnp.bfloat16), "replica", axis=0, tiled=True
    ).astype(anchor_new.dtype)
    first_row = lax.axis_index("fsdp") * row_count
    positions = first_row + jnp.arange(row_count, dtype=jnp.int32)
    hit = jnp.any(positions[:, None] == excluded[0][None, :], axis=1)
    kept_rows = jnp.where(hit, 0.0, 1.0).astype(jnp.float32)
    values = hidden_rows.astype(jnp.float32)
    inverse = lax.rsqrt(jnp.mean(values * values, axis=1, keepdims=True) + 1e-05)
    normed = values * inverse
    scaled = (normed * gain[None, :]).astype(jnp.bfloat16)
    masked = (value_cot[0].astype(jnp.float32) * kept_rows[:, None]).astype(jnp.bfloat16)
    full_weight = lax.all_gather(weight, "fsdp", axis=0, tiled=True)
    projected = jnp.dot(scaled, full_weight, preferred_element_type=jnp.float32)
    norm_grad = lax.dot_general(
        masked, full_weight, (((1,), (1,)), ((), ())), preferred_element_type=jnp.float32
    )
    weight_grad = lax.psum_scatter(
        lax.dot_general(
            scaled, masked, (((0,), (0,)), ((), ())), preferred_element_type=jnp.float32
        ).astype(jnp.bfloat16),
        "fsdp",
        scatter_dimension=0,
        tiled=True,
    ).astype(jnp.float32)
    gain_grad = lax.psum(jnp.sum(norm_grad * normed, axis=0).astype(jnp.bfloat16), "fsdp").astype(
        jnp.float32
    )
    weighted = norm_grad * gain[None, :]
    hidden_grad = (
        (weighted - normed * jnp.mean(weighted * normed, axis=1, keepdims=True)) * inverse
    ).astype(jnp.bfloat16)
    updated = weight.astype(jnp.float32) - inner_rate * weight_grad
    columns_now = lax.dynamic_slice_in_dim(updated, frag * frag_cols, frag_cols, 1)
    merged = mix_weight * anchor_full + (1.0 - mix_weight) * columns_now
    new_weight = lax.dynamic_update_slice_in_dim(updated, merged, frag * frag_cols, 1).astype(
        jnp.bfloat16
    )
    new_gain = gain - gain_rate * gain_grad
    anchor_out = lax.dynamic_update_index_in_dim(anchor, anchor_new[None], frag, 0)
    momentum_out = lax.dynamic_update_index_in_dim(momentum, momentum_new[None], frag, 0)
    return (
        projected.astype(jnp.bfloat16)[None],
        hidden_grad[None],
        new_weight[None],
        new_gain[None],
        anchor_out,
        momentum_out,
    )


def solution(mesh):
    placed = (
        P("replica", "fsdp", None),
        P("replica", "fsdp", None),
        P("replica", "fsdp", None),
        P("replica", None),
        P(None, "fsdp", "replica", None),
        P(None, "fsdp", "replica", None),
        P("replica", None),
        P(),
    )
    return jax.shard_map(
        body,
        mesh=mesh,
        in_specs=placed,
        out_specs=(
            P("replica", "fsdp", None),
            P("replica", "fsdp", None),
            P("replica", "fsdp", None),
            P("replica", None),
            P(None, "fsdp", "replica", None),
            P(None, "fsdp", "replica", None),
        ),
        check_vma=False,
    )
```

profile of v0, /device:TPU:1, one launch (start us, length us, event | category | flops | bytes accessed | tf_op | source)
XLA Modules:
  0.0 313.7 jit_solution(5242767039230448430)
XLA Ops:
  8.0 0.0 reduce-scatter.5.cloned.1.call-start
  8.0 1.0 copy.20
  9.0 0.9 copy.21
  10.6 1.6 dynamic-slice_bitcast_fusion
  12.2 0.0 reduce-scatter.5.cloned.1.call-update
  12.2 0.0 all-gather.3.cloned.1.call-start
  12.3 0.5 all-gather.3.cloned.1.call-update
  12.8 0.0 reduce-scatter.3.cloned.1.call-start
  12.8 1.1 compare_reduce_fusion
  13.9 5.1 %fusion.12 = f32[512]{0:T(512)S(1)} fusion(bf16[1,512,8192]{2,1,0:T(8,128)(2,1)} %param.8), kind=kLoop, calls=%fused_computation.14 | loop fusion | flops 12582400 | bytes 8390656 | tf_op jit(solution)/shard_map/reduce_sum | solution.py:40
  19.0 15.3 %convolution_convert_fusion = bf16[8192,1024]{1,0:T(8,128)(2,1)} fusion(bf16[1,512,8192]{2,1,0:T(8,128)(2,1)} %param.8, f32[8192]{0:T(1024)} %bitcast.96, f32[512]{0:T(512)S(1)} %add_rsqrt_fusion, bf16[1,512,1024]{2,1,0:T(8,128)(2,1)} %param.9, f32[512]{0:T(512)S(1)} %broadcast_select_fusion), kind=kOutput, calls=%fused_computation.21 | convolution fusion | flops 8616673280 | bytes 26251264 | tf_op jit(solution)/shard_map/dot_general | solution.py:50
  34.3 0.0 reduce-scatter.3.cloned.1.call-update
  34.3 82.2 %reduce-scatter.5.cloned.1.call-done = bf16[64,128]{1,0:T(8,128)(2,1)} async-done(((bf16[512,128]{1,0:T(8,128)(2,1)}), bf16[64,128]{1,0:T(8,128)(2,1)}) %reduce-scatter.5.cloned.1.call-update) | async-done | bytes 16400 | tf_op jit(solution)/shard_map/reduce_scatter | solution.py:26
  116.5 0.7 fusion.45
  117.3 28.3 %all_gather.7 = bf16[512,128]{1,0:T(8,128)(2,1)S(1)} all-gather(bf16[64,128]{1,0:T(8,128)(2,1)S(1)} %get-tuple-element.8), channel_id=1, replica_groups=mesh['replica'=8,'fsdp'=16] {'replica'}, dimensions={0}, use_global_device_ids=true | all-gather | bytes 147456 | tf_op jit(solution)/shard_map/all_gather | solution.py:32
  145.6 0.0 copy-start.1
  145.6 0.0 copy-start.2
  145.6 0.0 all-gather.3.cloned.1.call-done
  145.6 0.0 copy-done.3
  145.7 0.0 copy-done.4
  145.7 18.5 %fusion.11 = (bf16[8192]{0:T(1024)(128)(2,1)S(1)}, f32[512]{0:T(512)S(1)}, f32[512,8192]{1,0:T(8,128)}) fusion(bf16[1,512,8192]{2,1,0:T(8,128)(2,1)} %param.8, f32[512]{0:T(512)S(1)} %add_rsqrt_fusion, f32[8192]{0:T(1024)S(1)} %bitcast.97, bf16[1,8192,1024]{2,1,0:T(8,128)(2,1)} %all-gather.3.cloned.1.call-done, bf16[1,512,1024]{2,1,0:T(8,128)(2,1)S(1)} %copy-done.4, ...), kind=kOutput, calls=%fused_computation.13 | convolution fusion | flops 8620859392 | bytes 43046912 | tf_op jit(solution)/shard_map/dot_general | solution.py:46
  164.2 0.0 copy-done.1
  164.2 0.0 copy-done.2
  164.2 60.5 %psum.7 = bf16[8192]{0:T(1024)(128)(2,1)S(1)} all-reduce(bf16[8192]{0:T(1024)(128)(2,1)S(1)} %get-tuple-element.6), channel_id=1, replica_groups=mesh['replica'=8,'fsdp'=16] {'fsdp'}, use_global_device_ids=true, to_apply=%region_6.7 | all-reduce | flops 8192 | bytes 32768 | tf_op jit(solution)/shard_map/psum | solution.py:57
  224.7 0.6 multiply_subtract_fusion
  225.3 12.6 %fusion.21 = bf16[1,512,8192]{2,1,0:T(8,128)(2,1)} fusion(bf16[1,512,8192]{2,1,0:T(8,128)(2,1)} %param.8, f32[512,8192]{1,0:T(8,128)} %get-tuple-element.11, f32[512]{0:T(512)S(1)} %broadcast_multiply_fusion, f32[8192]{0:T(1024)S(1)} %bitcast.99, f32[512]{0:T(512)S(1)} %add_rsqrt_fusion), kind=kLoop, calls=%fused_computation.23 | loop fusion | flops 29360128 | bytes 33591296 | tf_op jit(solution)/shard_map/broadcast_in_dim | solution.py:75
  237.9 15.9 %fusion.35 = bf16[1,512,1024]{2,1,0:T(8,128)(2,1)} fusion(bf16[1,8192,1024]{2,1,0:T(8,128)(2,1)} %all-gather.3.cloned.1.call-done, bf16[1,512,8192]{2,1,0:T(8,128)(2,1)} %param.8, f32[8192]{0:T(1024)S(1)} %bitcast.100, f32[512]{0:T(512)S(1)} %add_rsqrt_fusion), kind=kOutput, calls=%fused_computation.36 | convolution fusion | flops 8607236096 | bytes 26249216 | tf_op jit(solution)/shard_map/dot_general | solution.py:45
  253.8 49.6 %reduce-scatter.3.cloned.1.call-done = bf16[512,1024]{1,0:T(8,128)(2,1)} async-done(((bf16[8192,1024]{1,0:T(8,128)(2,1)}), bf16[512,1024]{1,0:T(8,128)(2,1)}) %reduce-scatter.3.cloned.1.call-update) | async-done | bytes 1048592 | tf_op jit(solution)/shard_map/reduce_scatter | solution.py:49
  303.4 0.0 copy-done
  303.4 1.6 convert_subtract_fusion
  305.0 0.1 multiply_dynamic-update-slice_fusion
  305.1 1.1 convert_bitcast_fusion.2
  (8 shorter events, 0.0 us)
Async XLA Ops:
  8.0 108.5 %reduce-scatter.5.cloned.1.call-start = ((), (), s32[]{:S(2)}) async-start(), calls=%async_computation.3 | async-start | bytes 147456 | tf_op jit(solution)/shard_map/reduce_scatter | solution.py:26
  12.2 133.4 %all-gather.3.cloned.1.call-start = ((), (), s32[]{:S(2)}) async-start(), calls=%async_computation.4 | async-start | bytes 17825792 | tf_op jit(solution)/shard_map/all_gather | solution.py:44
  12.8 290.6 %reduce-scatter.3.cloned.1.call-start = ((), (), s32[]{:S(2)}) async-start(), calls=%async_computation.2 | async-start | bytes 17825792 | tf_op jit(solution)/shard_map/reduce_scatter | solution.py:49
  34.3 111.4 %copy-start.3 = (f32[1,8192]{1,0:T(1,128)S(1)}, f32[1,8192]{1,0:T(1,128)}, u32[]{:S(2)}) copy-start(f32[1,8192]{1,0:T(1,128)} %param.11) | copy-start | bytes 98308
  34.3 111.4 %copy-start.4 = (bf16[1,512,1024]{2,1,0:T(8,128)(2,1)S(1)}, bf16[1,512,1024]{2,1,0:T(8,128)(2,1)}, u32[]{:S(2)}) copy-start(bf16[1,512,1024]{2,1,0:T(8,128)(2,1)} %param.9) | copy-start | bytes 3145732
  145.6 18.6 %copy-start.1 = (f32[8,1,64,128]{3,2,1,0:T(8,128)}, f32[8,1,64,128]{3,2,1,0:T(8,128)S(1)}, u32[]{:S(2)}) copy-start(f32[8,1,64,128]{3,2,1,0:T(8,128)S(1)} %get-tuple-element.13) | copy-start | bytes 786436
  145.6 18.6 %copy-start.2 = (f32[8,1,64,128]{3,2,1,0:T(8,128)}, f32[8,1,64,128]{3,2,1,0:T(8,128)S(1)}, u32[]{:S(2)}) copy-start(f32[8,1,64,128]{3,2,1,0:T(8,128)S(1)} %get-tuple-element.12) | copy-start | bytes 786436
  237.9 65.5 %copy-start = (bf16[1,512,1024]{2,1,0:T(8,128)(2,1)S(1)}, bf16[1,512,1024]{2,1,0:T(8,128)(2,1)}, u32[]{:S(2)}) copy-start(bf16[1,512,1024]{2,1,0:T(8,128)(2,1)} %param.10) | copy-start | bytes 3145732
Sparse Core Ops, SparseCore 0:
  13.0 103.5 reduce-scatter.4
  118.9 184.3 reduce-scatter.2
Sparse Core Ops, SparseCore 1:
  14.4 95.7 all-gather.2
where the time goes:
time: 315 us; the launch traced here: 314 us
  waiting for transfers between devices  132 us (42%)
  blocking collectives  88.8 us (28%)
  matrix products  49.7 us (16%)
  other arithmetic  22.9 us (7%)
  between operations  16.2 us (5%)
  local copies, waits for them, and re-layouts  3.51 us (1%)
    reduce_scatter x1, waiting for transfers between devices, body(): lax.psum_scatter(column_block.astype(jnp.bfloat16), 'replica', scatter_di...  82.2 us
    psum x1, blocking collectives, body(): lax.psum(jnp.sum(norm_grad * normed, axis=0).astype(jnp.bfloat16), 'fsdp')  60.5 us
    reduce_scatter x1, waiting for transfers between devices, body(): lax.psum_scatter(lax.dot_general(scaled, masked, (((0,), (0,)), ((), ()))...  49.6 us
    all_gather x1, blocking collectives, body(): lax.all_gather(anchor_new.astype(jnp.bfloat16), 'replica', axis=0, tiled=...  28.3 us
    dot_general x1, matrix products, body(): lax.dot_general(masked, full_weight, (((1,), (1,)), ((), ())), preferred_...  18.5 us
    dot_general x1, matrix products, body(): projected = jnp.dot(scaled, full_weight, preferred_element_type=jnp.float32)  15.9 us
    dot_general x1, matrix products, body(): lax.dot_general(scaled, masked, (((0,), (0,)), ((), ())), preferred_eleme...  15.3 us
    broadcast_in_dim x1, other arithmetic, body(): hidden_grad[None]  12.6 us
  transfers between devices with their start and end apart: 3, of which 2 were waited for; matrix products, arithmetic and copies ran while one was open for 22% of the time, Pallas kernels for 0%

commit v1 on v0

v1 whole, which is shorter than its diff:
```python
import functools

import jax
import jax.numpy as jnp
from jax import lax
from jax.experimental import pallas as pl
from jax.experimental.pallas import tpu as pltpu
from jax.sharding import PartitionSpec as P

outer_momentum = 0.9
outer_rate = 0.7
mix_weight = 0.5

ROWS = 512
D = 8192
KV = 1024
HALF = D // 2
WIDE = HALF + KV
VMEM = 56 * 1024 * 1024
NZ, NY, NC = 4, 2, 2
bf16, f32 = jnp.bfloat16, jnp.float32


def params(n):
    return pltpu.CompilerParams(dimension_semantics=("arbitrary",) * n, vmem_limit_bytes=VMEM)


def cost(microseconds):
    return pl.CostEstimate(flops=0, bytes_accessed=int(microseconds * 3.3e6), transcendentals=0)


def shift(x, dz, dy, dc, name="x"):
    pairs = []
    for z in range(NZ):
        for y in range(NY):
            for c in range(NC):
                to = ((z + dz) % NZ, (y + dy) % NY, (c + dc) % NC)
                pairs.append(((z * NY + y) * NC + c, (to[0] * NY + to[1]) * NC + to[2]))
    with jax.named_scope(name):
        return lax.ppermute(x, "fsdp", pairs)


def flip_z(x, mask):
    pairs = [(i, i ^ (mask * NY * NC)) for i in range(NZ * NY * NC)]
    return lax.ppermute(x, "fsdp", pairs)


def flip_replica(x, mask):
    return lax.ppermute(x, "replica", [(i, i ^ mask) for i in range(8)])


Z, Y, CORE, FIRST, FRAG, REPLICA = range(6)
PAIR = 2 * ROWS


def pick(step, values):
    found = values[-1]
    for k, value in enumerate(values[:-1]):
        found = jnp.where(step == k, value, found)
    return found


def block_of(s, step, places):
    dz, dy = pick(step, [p[0] for p in places]), pick(step, [p[1] for p in places])
    return lax.rem(s[Z] + dz, NZ) * NY + lax.rem(s[Y] + dy, NY)


def pair_of(s, step, depths):
    return lax.rem(s[Z] + pick(step, depths), NZ)


def lanes(v, k):
    return v[:, k * 128 : (k + 1) * 128]


def norm_kernel(s_ref, x_ref, cot_ref, gain_ref, excl_ref, mine_ref, send_ref, inv_ref):
    core = s_ref[CORE]
    rows = x_ref.shape[0]
    position = s_ref[FIRST] + pl.program_id(0) * rows
    position = position + lax.broadcasted_iota(jnp.int32, (rows, 1), 0)
    hits = jnp.where(position == excl_ref[...], 1.0, 0.0)
    kept = 1.0 - jnp.max(hits, axis=1, keepdims=True)
    masked = (cot_ref[...].astype(f32) * kept).astype(bf16)
    mine_ref[:, HALF:] = masked
    send_ref[:, HALF:] = masked
    total = jnp.zeros((rows, 128), f32)
    for b in range(D // 128):
        v = x_ref[:, b * 128 : (b + 1) * 128].astype(f32)
        total = total + v * v
    total = jnp.sum(total, axis=1, keepdims=True)
    inverse = jnp.broadcast_to(lax.rsqrt(total / D + 1e-05), inv_ref.shape)
    inv_ref[...] = inverse
    for j in range(HALF // ROWS):
        for parity, out in ((core, mine_ref), (1 - core, send_ref)):
            at = pl.multiple_of((2 * j + parity) * ROWS, ROWS)
            x = x_ref[:, pl.ds(at, ROWS)].astype(f32)
            gain = gain_ref[:, pl.ds(at, ROWS)]
            for k in range(ROWS // 128):
                v = lanes(x, k) * inverse * lanes(gain, k)
                out[:, j * ROWS + k * 128 : j * ROWS + (k + 1) * 128] = v.astype(bf16)


def norm_call(scalars, hidden, cot, gain, excl):
    tile = 128
    return pl.pallas_call(
        norm_kernel,
        grid_spec=pltpu.PrefetchScalarGridSpec(
            num_scalar_prefetch=1,
            grid=(ROWS // tile,),
            in_specs=[
                pl.BlockSpec((tile, D), lambda t, s: (t, 0)),
                pl.BlockSpec((tile, KV), lambda t, s: (t, 0)),
                pl.BlockSpec((1, D), lambda t, s: (0, 0)),
                pl.BlockSpec((1, 1024), lambda t, s: (0, 0)),
            ],
            out_specs=[
                pl.BlockSpec((tile, WIDE), lambda t, s: (t, 0)),
                pl.BlockSpec((tile, WIDE), lambda t, s: (t, 0)),
                pl.BlockSpec((tile, 128), lambda t, s: (t, 0)),
            ],
        ),
        out_shape=[
            jax.ShapeDtypeStruct((ROWS, WIDE), bf16),
            jax.ShapeDtypeStruct((ROWS, WIDE), bf16),
            jax.ShapeDtypeStruct((ROWS, 128), f32),
        ],
        compiler_params=params(1),
        cost_estimate=cost(8),
        name="norm",
    )(scalars, hidden, cot, gain, excl)


def grad_kernel(count, s_ref, x0_ref, x1_ref, c0_ref, c1_ref, *rest):
    outs, (held, sems) = rest[:count], rest[count:]
    step = pl.program_id(0)
    dims = (((0,), (0,)), ((), ()))
    total = lax.dot_general(x0_ref[...], c0_ref[...], dims, preferred_element_type=f32)
    total = total + lax.dot_general(x1_ref[...], c1_ref[...], dims, preferred_element_type=f32)
    total = total.astype(bf16)
    copies = [pltpu.make_async_copy(held.at[k % 2], outs[k], sems.at[k % 2]) for k in range(count)]
    for k in range(count):

        @pl.when(step == k)
        def _(k=k):
            if k >= 2:
                copies[k - 2].wait()
            held[k % 2] = total
            copies[k].start()
            if k == count - 1:
                for copy in copies[max(k - 1, 0) :]:
                    copy.wait()


def grad_call(places, scalars, mine, recv, estimate):
    count = len(places)
    x = pl.BlockSpec((ROWS, ROWS), lambda t, s: (0, block_of(s, t, places)))
    c = pl.BlockSpec((ROWS, KV), lambda t, s: (0, HALF // KV))
    return pl.pallas_call(
        functools.partial(grad_kernel, count),
        grid_spec=pltpu.PrefetchScalarGridSpec(
            num_scalar_prefetch=1,
            grid=(count,),
            in_specs=[x, x, c, c],
            out_specs=[pl.BlockSpec(memory_space=pl.ANY)] * count,
            scratch_shapes=[pltpu.VMEM((2, ROWS, KV), bf16), pltpu.SemaphoreType.DMA((2,))],
        ),
        out_shape=[jax.ShapeDtypeStruct((ROWS, KV), bf16)] * count,
        compiler_params=params(1),
        cost_estimate=cost(estimate),
        name="weight_grad_blocks",
    )(scalars, mine, recv, mine, recv)


def weight_copies(depths, s_ref, weights, held, sems):
    copies = []
    for k in range(len(depths)):
        for dy in range(NY):
            at = pl.multiple_of(lax.rem(s_ref[Y] + dy, NY) * ROWS, ROWS)
            n = NY * k + dy
            copies.append(
                pltpu.make_async_copy(weights[n], held.at[k, pl.ds(at, ROWS)], sems.at[n])
            )
    return copies


def half_kernel(depths, s_ref, x_ref, c_ref, gain_ref, *rest):
    count = len(depths)
    weights, rest = rest[: NY * count], rest[NY * count :]
    outs, (held, sems, values, made, out_sems) = rest[: count + 1], rest[count + 1 :]
    step = pl.program_id(0)
    copies = weight_copies(depths, s_ref, weights, held, sems)
    back = [
        pltpu.make_async_copy(made.at[k % 2], outs[k], out_sems.at[k % 2]) for k in range(count + 1)
    ]

    @pl.when(step == 0)
    def _():
        for copy in copies:
            copy.start()

    for k in range(count):

        @pl.when(step == k)
        def _(k=k):
            copies[NY * k].wait()
            copies[NY * k + 1].wait()
            if k >= 2:
                back[k - 2].wait()

    w = held[step]
    part = jnp.dot(x_ref[...], w, preferred_element_type=f32)

    @pl.when(step == 0)
    def _():
        values[...] = part

    @pl.when(step > 0)
    def _():
        values[...] += part

    grad = lax.dot_general(c_ref[...], w, (((1,), (1,)), ((), ())), preferred_element_type=f32)
    first = lax.rem(s_ref[Z] + pick(step, depths), NZ) * NY
    slot = lax.rem(step, 2)
    for k in range(NY):
        at = pl.multiple_of((2 * (first + k) + s_ref[CORE]) * ROWS, ROWS)
        cols = slice(k * ROWS, (k + 1) * ROWS)
        made[slot, :, cols] = (grad[:, cols] * gain_ref[:, pl.ds(at, ROWS)]).astype(bf16)

    for k in range(count):

        @pl.when(step == k)
        def _(k=k):
            back[k].start()
            if k == count - 1:
                if count >= 2:
                    back[count - 2].wait()
                made[count % 2] = values[...].astype(bf16)
                back[count].start()
                back[count - 1].wait()
                back[count].wait()


def half_call(depths, scalars, x, gain, w, name, estimate):
    count = len(depths)
    weights = [w[dz, dy] for dz in depths for dy in range(NY)]
    return pl.pallas_call(
        functools.partial(half_kernel, depths),
        grid_spec=pltpu.PrefetchScalarGridSpec(
            num_scalar_prefetch=1,
            grid=(count,),
            in_specs=[
                pl.BlockSpec((ROWS, PAIR), lambda t, s: (0, pair_of(s, t, depths))),
                pl.BlockSpec((ROWS, KV), lambda t, s: (0, HALF // KV)),
                pl.BlockSpec((1, D), lambda t, s: (0, 0)),
            ]
            + [pl.BlockSpec(memory_space=pl.ANY)] * len(weights),
            out_specs=[pl.BlockSpec(memory_space=pl.ANY)] * (count + 1),
            scratch_shapes=[
                pltpu.VMEM((count, PAIR, KV), bf16),
                pltpu.SemaphoreType.DMA((NY * count,)),
                pltpu.VMEM((ROWS, KV), f32),
                pltpu.VMEM((2, ROWS, PAIR), bf16),
                pltpu.SemaphoreType.DMA((2,)),
            ],
        ),
        out_shape=[jax.ShapeDtypeStruct((ROWS, PAIR), bf16)] * (count + 1),
        compiler_params=params(1),
        cost_estimate=cost(estimate),
        name=name,
    )(scalars, x, x, gain, *weights)


def hidden_kernel(depths, s_ref, x_ref, c_ref, gain_ref, inv_ref, h_ref, *rest):
    step, count = pl.program_id(0), len(depths)
    gots, weights, rest = rest[: count + 2], rest[count + 2 : 3 * count + 2], rest[3 * count + 2 :]
    values_ref, out_ref, held, sems, values, mean, got, got_sems = rest
    received = [
        pltpu.make_async_copy(ref, got.at[k], got_sems.at[k]) for k, ref in enumerate(gots)
    ]
    copies = weight_copies(depths, s_ref, weights, held, sems)

    @pl.when(step == 0)
    def _():
        for copy in copies:
            copy.start()
        for copy in (*received[count:], *received[:count]):
            copy.start()

    for k in range(count):

        @pl.when(step == k)
        def _(k=k):
            copies[NY * k].wait()
            copies[NY * k + 1].wait()

        @pl.when(step == count + k)
        def _(k=k):
            received[k].wait()

    @pl.when(step < count)
    def _():
        part = jnp.dot(x_ref[...], held[step], preferred_element_type=f32)

        @pl.when(step == 0)
        def _():
            values[...] = part

        @pl.when(step > 0)
        def _():
            values[...] += part

    @pl.when(step == count)
    def _():
        for k in (count, count + 1):
            received[k].wait()
            values[...] += got[k].astype(f32)
        values_ref[...] = values[...].astype(bf16)
        dots = jnp.sum(values[...] * c_ref[...].astype(f32), axis=1, keepdims=True) / D
        mean[...] = jnp.broadcast_to(dots, mean.shape) * inv_ref[...]

    def finish(weighted, at):
        for n in range(ROWS // 128):
            cols = pl.ds(at + n * 128, 128)
            v = lanes(weighted, n) - h_ref[:, cols].astype(f32) * mean[...]
            out_ref[:, cols] = (v * inv_ref[...]).astype(bf16)

    @pl.when(step >= count)
    def _():
        core = s_ref[CORE]
        k = step - count
        first = 2 * PAIR * lax.rem(s_ref[Z] + pick(k, depths), NZ)
        for y in range(NY):
            cols = slice(y * ROWS, (y + 1) * ROWS)
            at = pl.multiple_of((2 * y + core) * ROWS, ROWS)
            gain = gain_ref[:, pl.ds(pl.multiple_of(first + at, ROWS), ROWS)]
            grad = lax.dot_general(
                c_ref[...], held[k, cols], (((1,), (1,)), ((), ())), preferred_element_type=f32
            )
            finish(grad * gain, at)
            at = pl.multiple_of((2 * y + 1 - core) * ROWS, ROWS)
            finish(got[k, :, cols].astype(f32), at)


def hidden_call(depths, scalars, hidden, mine, gain, inverse, gots, w):
    count = len(depths)
    weights = [w[dz, dy] for dz in depths for dy in range(NY)]

    def place(t, s):
        return pair_of(s, jnp.maximum(t - count, 0), depths)

    return pl.pallas_call(
        functools.partial(hidden_kernel, depths),
        grid_spec=pltpu.PrefetchScalarGridSpec(
            num_scalar_prefetch=1,
            grid=(2 * count,),
            in_specs=[
                pl.BlockSpec(
                    (ROWS, PAIR), lambda t, s: (0, pair_of(s, jnp.minimum(t, count - 1), depths))
                ),
                pl.BlockSpec((ROWS, KV), lambda t, s: (0, HALF // KV)),
                pl.BlockSpec((1, D), lambda t, s: (0, 0)),
                pl.BlockSpec((ROWS, 128), lambda t, s: (0, 0)),
                pl.BlockSpec((ROWS, 2 * PAIR), lambda t, s: (0, place(t, s))),
            ]
            + [pl.BlockSpec(memory_space=pl.ANY)] * len(gots)
            + [pl.BlockSpec(memory_space=pl.ANY)] * len(weights),
            out_specs=[
                pl.BlockSpec((ROWS, KV), lambda t, s: (0, 0)),
                pl.BlockSpec((ROWS, 2 * PAIR), lambda t, s: (0, place(t, s))),
            ],
            scratch_shapes=[
                pltpu.VMEM((count, PAIR, KV), bf16),
                pltpu.SemaphoreType.DMA((NY * count,)),
                pltpu.VMEM((ROWS, KV), f32),
                pltpu.VMEM((ROWS, 128), f32),
                pltpu.VMEM((count + 2, ROWS, PAIR), bf16),
                pltpu.SemaphoreType.DMA((count + 2,)),
            ],
        ),
        out_shape=[
            jax.ShapeDtypeStruct((ROWS, KV), bf16),
            jax.ShapeDtypeStruct((ROWS, D), bf16),
        ],
        compiler_params=params(1),
        cost_estimate=cost(100),
        name="hidden_grad",
    )(scalars, mine, mine, gain, inverse, hidden, *gots, *weights)


def update_kernel(rate, s_ref, w_ref, a_ref, b_ref, c_ref, d_ref, anchor_ref, out_ref):
    grad = a_ref[...].astype(f32) + b_ref[...].astype(f32)
    grad = grad + (c_ref[...].astype(f32) + d_ref[...].astype(f32))
    out_ref[...] = (w_ref[...].astype(f32) - rate * grad).astype(bf16)
    cols = anchor_ref.shape[1]
    at = pl.ds(pl.multiple_of(s_ref[FRAG] * cols, cols), cols)
    grad = a_ref[:, at].astype(f32) + b_ref[:, at].astype(f32)
    grad = grad + (c_ref[:, at].astype(f32) + d_ref[:, at].astype(f32))
    now = w_ref[:, at].astype(f32) - rate * grad
    out_ref[:, at] = (mix_weight * anchor_ref[...] + (1.0 - mix_weight) * now).astype(bf16)


def update_call(rate, scalars, weight, parts, anchor):
    tile = 256
    row = pl.BlockSpec((tile, KV), lambda t, s: (t, 0))
    return pl.pallas_call(
        functools.partial(update_kernel, rate),
        grid_spec=pltpu.PrefetchScalarGridSpec(
            num_scalar_prefetch=1,
            grid=(ROWS // tile,),
            in_specs=[row] * 5 + [pl.BlockSpec((tile, anchor.shape[1]), lambda t, s: (t, 0))],
            out_specs=row,
        ),
        out_shape=jax.ShapeDtypeStruct((ROWS, KV), bf16),
        compiler_params=params(1),
        cost_estimate=cost(3),
        name="update",
    )(scalars, weight, *parts, anchor)


by_delta = outer_rate * (1.0 + outer_momentum)
by_momentum = outer_rate * outer_momentum * outer_momentum


def term_kernel(replicas, s_ref, w_ref, a_ref, m_ref, out_ref):
    rows = a_ref.shape[2]
    out_ref[...] = w_ref[...].astype(f32) * (by_delta / replicas)
    at = pl.ds(pl.multiple_of(s_ref[REPLICA] * rows, rows), rows)
    out_ref[at, :] += (1.0 - by_delta) * a_ref[0, 0] - by_momentum * m_ref[0, 0]


def term_call(replicas, scalars, weight, anchor, momentum):
    _, _, rows, cols = anchor.shape
    state = pl.BlockSpec((1, 1, rows, cols), lambda t, s: (s[FRAG], 0, 0, 0))
    return pl.pallas_call(
        functools.partial(term_kernel, replicas),
        grid_spec=pltpu.PrefetchScalarGridSpec(
            num_scalar_prefetch=1,
            grid=(1,),
            in_specs=[pl.BlockSpec((ROWS, cols), lambda t, s: (0, s[FRAG])), state, state],
            out_specs=pl.BlockSpec((ROWS, cols), lambda t, s: (0, 0)),
        ),
        out_shape=jax.ShapeDtypeStruct((ROWS, cols), f32),
        compiler_params=params(1),
        cost_estimate=cost(1),
        name="outer_term",
    )(scalars, weight, anchor, momentum)


def outer_kernel(s_ref, total_ref, a_ref, m_ref, a_out, m_out):
    a_out[...] = a_ref[...]
    m_out[...] = m_ref[...]
    rows = a_ref.shape[2]
    frag = s_ref[FRAG]
    a, m = a_ref[frag, 0], m_ref[frag, 0]
    at = pl.ds(pl.multiple_of(s_ref[REPLICA] * rows, rows), rows)
    kept = (1.0 - by_delta) * a - by_momentum * m
    delta = a - (total_ref[at, :] - kept) / by_delta
    m_new = outer_momentum * m + delta
    m_out[frag, 0] = m_new
    a_out[frag, 0] = a - outer_rate * (delta + outer_momentum * m_new)


def outer_call(scalars, total, anchor, momentum):
    whole = pl.BlockSpec(anchor.shape, lambda t, s: (0, 0, 0, 0))
    return pl.pallas_call(
        outer_kernel,
        grid_spec=pltpu.PrefetchScalarGridSpec(
            num_scalar_prefetch=1,
            grid=(1,),
            in_specs=[pl.BlockSpec(total.shape, lambda t, s: (0, 0)), whole, whole],
            out_specs=[whole, whole],
        ),
        out_shape=[jax.ShapeDtypeStruct(anchor.shape, f32)] * 2,
        compiler_params=params(1),
        cost_estimate=cost(100),
        name="outer_step",
    )(scalars, total, anchor, momentum)


def gain_kernel(places, s_ref, *rest):
    grads, weights, out_ref = rest[:8], rest[8:16], rest[16]
    rows = grads[0].shape[0]
    ones = jnp.ones((8, KV), bf16)
    for k, (dz, dy) in enumerate(places):
        product = (grads[k][...].astype(f32) * weights[k][...].astype(f32)).astype(bf16)
        sums = lax.dot_general(ones, product, (((1,), (1,)), ((), ())), preferred_element_type=f32)
        block = lax.rem(s_ref[Z] + dz, NZ) * NY + lax.rem(s_ref[Y] + dy, NY)
        at = pl.multiple_of(block * ROWS + pl.program_id(0) * rows, rows)
        out_ref[:, pl.ds(at, rows)] = sums[:1]


def gain_call(places, scalars, g, w):
    tile = 256
    row = pl.BlockSpec((tile, KV), lambda t, s: (t, 0))
    return pl.pallas_call(
        functools.partial(gain_kernel, places),
        grid_spec=pltpu.PrefetchScalarGridSpec(
            num_scalar_prefetch=1,
            grid=(ROWS // tile,),
            in_specs=[row] * 16,
            out_specs=pl.BlockSpec((1, HALF), lambda t, s: (0, 0)),
        ),
        out_shape=jax.ShapeDtypeStruct((1, HALF), f32),
        compiler_params=params(1),
        cost_estimate=cost(0),
        name="gain_grad",
    )(scalars, *[g[p] for p in places], *[w[p] for p in places])


def after(x, *others):
    return lax.optimization_barrier((x, *others))[0]


def add(*terms):
    total = terms[0].astype(f32)
    for term in terms[1:]:
        total = total + term.astype(f32)
    return total.astype(bf16)


def body(hidden_in, value_cot, proj_weight, norm_gain, anchor, momentum, excluded, fragment):
    inner_rate = 0.01 / ROWS**0.5
    gain_rate = 0.1 / ROWS**0.5
    hidden, weight = hidden_in[0], proj_weight[0]
    here = lax.axis_index("fsdp")
    replica = lax.axis_index("replica")
    z, y, core = here // (NY * NC), (here // NC) % NY, here % NC
    scalars = jnp.stack([z, y, core, here * ROWS, fragment[0], replica]).astype(jnp.int32)

    w = {(0, 0): weight}
    w[1, 0] = shift(weight, -1, 0, 0, "ag_zm")
    w[0, 1] = shift(weight, 0, 1, 0, "ag_y")
    w[3, 0] = shift(weight, 1, 0, 0, "ag_zp")
    near = (w[0, 1], w[1, 0], w[3, 0])
    w[1, 1] = shift(after(w[0, 1], *near), -1, 0, 0, "ag_B")
    w[2, 0] = shift(after(w[3, 0], *near), 1, 0, 0, "ag_A")

    total = term_call(lax.axis_size("replica"), scalars, weight, anchor, momentum)
    first_term = total
    total = total + flip_replica(total, 2)
    first_sum = total
    total = total + flip_replica(total, 6)
    second_sum = total
    total = total + flip_replica(total, 1)

    mine, send, inverse = norm_call(
        after(scalars, first_term), hidden, value_cot[0], norm_gain, excluded
    )
    recv = shift(after(send, first_sum, *near), 0, 0, 1, "swap_x")

    g = {}

    def make(places, waits, estimate):
        g.update(zip(places, grad_call(places, after(scalars, *waits), mine, recv, estimate)))

    make([(2, 1)], [recv], 3)
    make([(3, 1), (1, 1), (2, 0)], [g[2, 1], second_sum], 8)
    make([(3, 0), (0, 1), (1, 0), (0, 0)], [g[2, 0], w[1, 1], w[2, 0]], 10)
    w[2, 1] = shift(after(w[1, 1], g[2, 1]), -1, 0, 0, "ag_D")
    w[3, 1] = shift(after(w[0, 1], w[2, 0], g[2, 1]), 1, 0, 0, "ag_C")
    far = shift(g[2, 1], 0, 1, 0, "rs_D")
    left = shift(g[3, 1], -1, 0, 0, "rs_C")
    side = shift(g[1, 1], 0, 1, 0, "rs_B")

    near_half, far_half = (0, 1), (3, 2)
    sent0 = half_call(near_half, after(scalars, g[0, 0]), recv, norm_gain, w, "half_near", 10)
    got0 = [shift(v, 0, 0, 1, "swap_w0") for v in sent0]
    over = shift(add(g[2, 0], after(far, sent0[0])), 1, 0, 0, "rs_A")
    sent1 = half_call(far_half, after(scalars, sent0[0], far), recv, norm_gain, w, "half_far", 0)
    got1 = [shift(v, 0, 0, 1, "swap_w1") for v in sent1]

    order = [(dz, dy) for dz in range(NZ) for dy in range(NY)]
    partial = gain_call(order, after(scalars, sent1[0], side), g, w)
    left, side, over = (after(v, partial) for v in (left, side, over))
    from_next = shift(after(g[3, 0], left), -1, 0, 0, "rs_zm")
    from_side = shift(add(g[0, 1], left), 0, 1, 0, "rs_y")
    from_last = shift(add(g[1, 0], side, over), 1, 0, 0, "rs_zp")

    anchor_out, momentum_out = outer_call(
        after(scalars, left, side, over), total, anchor, momentum
    )
    values_out, hidden_grad = hidden_call(
        (*near_half, *far_half),
        after(scalars, anchor_out), hidden, mine, norm_gain, inverse,
        [*got0[:-1], *got1[:-1], got0[-1], got1[-1]], w,
    )

    partial = partial + shift(partial, 0, 1, 0, "gain_y")
    partial = partial + flip_z(partial, 1)
    partial = partial + flip_z(partial, 3)
    other = shift(partial, 0, 0, 1, "gain_c")
    even = jnp.where(core == 0, partial, other).reshape(HALF // ROWS, ROWS)
    odd = jnp.where(core == 0, other, partial).reshape(HALF // ROWS, ROWS)
    gain_grad = jnp.stack([even, odd], axis=1).reshape(1, D) / norm_gain
    new_gain = norm_gain - gain_rate * gain_grad

    new_weight = update_call(
        inner_rate,
        scalars,
        weight,
        (after(g[0, 0], hidden_grad), from_next, from_side, from_last),
        total,
    )
    return (
        values_out[None],
        hidden_grad[None],
        new_weight[None],
        new_gain,
        anchor_out,
        momentum_out,
    )


def solution(mesh):
    placed = (
        P("replica", "fsdp", None),
        P("replica", "fsdp", None),
        P("replica", "fsdp", None),
        P("replica", None),
        P(None, "fsdp", "replica", None),
        P(None, "fsdp", "replica", None),
        P("replica", None),
        P(),
    )
    return jax.shard_map(
        body,
        mesh=mesh,
        in_specs=placed,
        out_specs=(
            P("replica", "fsdp", None),
            P("replica", "fsdp", None),
            P("replica", "fsdp", None),
            P("replica", None),
            P(None, "fsdp", "replica", None),
            P(None, "fsdp", "replica", None),
        ),
        check_vma=False,
    )
```

time: 315 us -> 180 us (0.57)
  waiting for transfers between devices: 132 us -> 31.1 us
  Pallas kernels: 0 us -> 97.5 us
  blocking collectives: 88.8 us -> 0 us
  matrix products: 49.7 us -> 0 us
  starting transfers between devices: 0.12 us -> 34.1 us
  other arithmetic: 22.9 us -> 7.48 us
  between operations: 16.2 us -> 1.63 us
  local copies, waits for them, and re-layouts: 3.51 us -> 7.39 us
    reduce_scatter x2 -> x0, waiting for transfers between devices: 132 us -> none  [the longest x1 82.2 us: body(): lax.psum_scatter(column_block.astype(jnp.bfloat16), 'replica', scatter_di...]
    pallas_call x0 -> x11, Pallas kernels: none -> 97.5 us  [the longest x1 25.7 us: hidden_call(): pl.pallas_call(functools.partial(hidden_kernel, depths), grid_spec=pltpu....]
    psum x1 -> x0, blocking collectives: 60.5 us -> none  [body(): lax.psum(jnp.sum(norm_grad * normed, axis=0).astype(jnp.bfloat16), 'fsdp')]
    dot_general x3 -> x0, matrix products: 49.7 us -> none  [the longest x1 18.5 us: body(): lax.dot_general(masked, full_weight, (((1,), (1,)), ((), ())), preferred_...]
    ppermute x0 -> x28, starting transfers between devices: none -> 34.1 us  [the longest x23 26 us: shift(): return lax.ppermute(x, 'fsdp', pairs)]
    ppermute x0 -> x28, waiting for transfers between devices: none -> 31.1 us  [the longest x23 26 us: shift(): return lax.ppermute(x, 'fsdp', pairs)]
    all_gather x1 -> x0, blocking collectives: 28.3 us -> none  [body(): lax.all_gather(anchor_new.astype(jnp.bfloat16), 'replica', axis=0, tiled=...]
    broadcast_in_dim x2 -> x0, other arithmetic: 13.7 us -> none  [the longest x1 12.6 us: body(): hidden_grad[None]]
  transfers between devices with their start and end apart: 3 -> 28, of which waited for: 2 -> 9; matrix products, arithmetic and copies ran while one was open for 22% -> 5% of each run, Pallas kernels for 0% -> 52%
where the time goes in v1:
time: 180 us; the launch traced here: 179 us
  Pallas kernels  97.5 us (54%)
  starting transfers between devices  34.1 us (19%)
  waiting for transfers between devices  31.1 us (17%)
  other arithmetic  7.48 us (4%)
  local copies, waits for them, and re-layouts  7.39 us (4%)
    ppermute x23, waiting for transfers between devices, shift(): return lax.ppermute(x, 'fsdp', pairs)  26 us
    ppermute x23, starting transfers between devices, shift(): return lax.ppermute(x, 'fsdp', pairs)  26 us
    pallas_call x1, Pallas kernels, hidden_call(): pl.pallas_call(functools.partial(hidden_kernel, depths), grid_spec=pltpu....  25.7 us
    pallas_call x3, Pallas kernels, grad_call(): pl.pallas_call(functools.partial(grad_kernel, count), grid_spec=pltpu.Pre...  22.1 us
    pallas_call x2, Pallas kernels, half_call(): pl.pallas_call(functools.partial(half_kernel, depths), grid_spec=pltpu.Pr...  21.5 us
    pallas_call x1, Pallas kernels, norm_call(): pl.pallas_call(norm_kernel, grid_spec=pltpu.PrefetchScalarGridSpec(num_sc...  10.5 us
    pallas_call x1, Pallas kernels, gain_call(): pl.pallas_call(functools.partial(gain_kernel, places), grid_spec=pltpu.Pr...  8.41 us
    unnamed x32, local copies, waits for them, and re-layouts  6.68 us
  transfers between devices with their start and end apart: 28, of which 9 were waited for; matrix products, arithmetic and copies ran while one was open for 5% of the time, Pallas kernels for 52%

profile of v1, /device:TPU:1, one launch (start us, length us, event | category | flops | bytes accessed | tf_op | source)
XLA Modules:
  0.0 179.2 jit_solution(6394965597765159812)
XLA Ops:
  0.6 2.2 %collective-permute-start.1 = (bf16[512,1024]{1,0:T(8,128)(2,1)}, bf16[512,1024]{1,0:T(8,128)(2,1)S(1)}, u32[]{:S(2)}, u32[]{:S(2)}) collective-permute-start(bf16[512,1024]{1,0:T(8,128)(2,1)} %bitcast.13), channel_id=1, source_target_pairs={{0,2},{1,3},{2,0},{3,1},{4,6},{5,7},{6,4},{7,5},{8,10},{9,11},{10,... | collective-permute-start | bytes 3145736 | tf_op jit(solution)/shard_map/ag_y/ppermute | solution.py:40
  2.8 3.8 %collective-permute-start.2 = (bf16[512,1024]{1,0:T(8,128)(2,1)}, bf16[512,1024]{1,0:T(8,128)(2,1)S(1)}, u32[]{:S(2)}, u32[]{:S(2)}) collective-permute-start(bf16[512,1024]{1,0:T(8,128)(2,1)} %bitcast.14), channel_id=1, source_target_pairs={{0,12},{1,13},{2,14},{3,15},{4,0},{5,1},{6,2},{7,3},{8,4},{9,5},{1... | collective-permute-start | bytes 3145736 | tf_op jit(solution)/shard_map/ag_zm/ppermute | solution.py:40
  7.9 2.3 %outer_term.1 = f32[512,128]{1,0:T(8,128)} custom-call(s32[6]{0:T(128)} %stack.26.s_ref, bf16[512,1024]{1,0:T(8,128)(2,1)} %bitcast.16, f32[8,1,64,128]{3,2,1,0:T(8,128)} %a_ref.3, f32[8,1,64,128]{3,2,1,0:T(8,128)} %m_ref.3), custom_call_target="tpu_custom_call" | custom-call | bytes 3300000 | tf_op jit(solution)/shard_map/outer_term/pallas_call | solution.py:434
  11.4 10.5 %norm.1 = (bf16[512,5120]{1,0:T(8,128)(2,1)}, bf16[512,5120]{1,0:T(8,128)(2,1)}, f32[512,128]{1,0:T(8,128)}) custom-call(s32[6]{0:T(128)} %stack.26.s_ref, bf16[512,8192]{1,0:T(8,128)(2,1)} %bitcast.11, bf16[512,1024]{1,0:T(8,128)(2,1)} %bitcast.21, f32[1,8192]{1,0:T(1,128)} %gain_ref.7, s32[1,1024]{1,0:T(1,128)} %excl_ref.1), custom_call_target="tpu_custom_call" | custom-call | bytes 26400000 | tf_op jit(solution)/shard_map/norm/pallas_call | solution.py:105
  21.9 3.7 %collective-permute-done.1.rest_1_.rest_9_.rest_7_ = bf16[512,1024]{1,0:T(8,128)(2,1)S(1)} collective-permute-done((bf16[512,1024]{1,0:T(8,128)(2,1)}, bf16[512,1024]{1,0:T(8,128)(2,1)S(1)}, u32[]{:S(2)}, u32[]{:S(2)}) %collective-permute-start.1) | collective-permute-done | bytes 1048608 | tf_op jit(solution)/shard_map/ag_y/ppermute | solution.py:40
  25.6 2.8 %collective-permute-done.2.rest_2_.rest_10_.rest_8_ = bf16[512,1024]{1,0:T(8,128)(2,1)S(1)} collective-permute-done((bf16[512,1024]{1,0:T(8,128)(2,1)}, bf16[512,1024]{1,0:T(8,128)(2,1)S(1)}, u32[]{:S(2)}, u32[]{:S(2)}) %collective-permute-start.2) | collective-permute-done | bytes 1048608 | tf_op jit(solution)/shard_map/ag_zm/ppermute | solution.py:40
  28.4 3.1 %collective-permute-done.3.rest_0_.rest_14_.rest_10_ = bf16[512,1024]{1,0:T(8,128)(2,1)} collective-permute-done((bf16[512,1024]{1,0:T(8,128)(2,1)}, bf16[512,1024]{1,0:T(8,128)(2,1)}, u32[]{:S(2)}, u32[]{:S(2)}) %collective-permute-start.3) | collective-permute-done | bytes 1048608 | tf_op jit(solution)/shard_map/ag_zp/ppermute | solution.py:40
  31.5 2.2 %collective-permute-start.4 = (bf16[512,5120]{1,0:T(8,128)(2,1)}, bf16[512,5120]{1,0:T(8,128)(2,1)S(1)}, u32[]{:S(2)}, u32[]{:S(2)}) collective-permute-start(bf16[512,5120]{1,0:T(8,128)(2,1)} %get-tuple-element.48), channel_id=1, source_target_pairs={{0,1},{1,0},{2,3},{3,2},{4,5},{5,4},{6,7},{7,6},{8,9},{9,8},{10,11... | collective-permute-start | bytes 15728648 | tf_op jit(solution)/shard_map/swap_x/ppermute | solution.py:40
  33.7 2.7 %collective-permute-start.7 = (bf16[512,1024]{1,0:T(8,128)(2,1)S(1)}, bf16[512,1024]{1,0:T(8,128)(2,1)}, u32[]{:S(2)}, u32[]{:S(2)}) collective-permute-start(bf16[512,1024]{1,0:T(8,128)(2,1)S(1)} %collective-permute-done.1.rest_1_.rest_9_.rest_7_), channel_id=1, source_target_pairs={{0,12},{1,13},{2,14},{3,15},{4,0},{5,1},{6,2},{7,3},{8,4},{9,5},{1... | collective-permute-start | bytes 3145736 | tf_op jit(solution)/shard_map/ag_B/ppermute | solution.py:40
  36.4 5.8 %collective-permute-done.4.x1_ref.c1_ref.x_ref.c_ref = bf16[512,5120]{1,0:T(8,128)(2,1)S(1)} collective-permute-done((bf16[512,5120]{1,0:T(8,128)(2,1)}, bf16[512,5120]{1,0:T(8,128)(2,1)S(1)}, u32[]{:S(2)}, u32[]{:S(2)}) %collective-permute-start.4) | collective-permute-done | bytes 5242912 | tf_op jit(solution)/shard_map/swap_x/ppermute | solution.py:40
  42.2 2.4 %copy-done = bf16[512,5120]{1,0:T(8,128)(2,1)} copy-done((bf16[512,5120]{1,0:T(8,128)(2,1)}, bf16[512,5120]{1,0:T(8,128)(2,1)S(1)}, u32[]{:S(2)}) %copy-start) | copy-done | bytes 5242904
  44.6 4.8 %weight_grad_blocks.3.rest_5_ = bf16[512,1024]{1,0:T(8,128)(2,1)} custom-call(s32[6]{0:T(128)} %stack.26.s_ref, bf16[512,5120]{1,0:T(8,128)(2,1)} %get-tuple-element.50.x0_ref.c0_ref.x_ref.c_ref, bf16[512,5120]{1,0:T(8,128)(2,1)} %copy-done, bf16[512,5120]{1,0:T(8,128)(2,1)} %get-tuple-element.50.x0_ref.c0_ref.x_ref.c_ref, bf16[512,5120]{1,0:T(8,128)(2,1)} %copy-done), custom_call_target="tpu_custom_call" | custom-call | bytes 9900000 | tf_op jit(solution)/shard_map/weight_grad_blocks/pallas_call | solution.py:158
  49.6 2.5 %collective-permute-start.5 = (f32[512,128]{1,0:T(8,128)S(1)}, f32[512,128]{1,0:T(8,128)S(1)}, u32[]{:S(2)}, u32[]{:S(2)}) collective-permute-start(f32[512,128]{1,0:T(8,128)S(1)} %add.41), channel_id=1, source_target_pairs={{0,96},{16,112},{32,64},{48,80},{64,32},{80,48},{96,0},{112,16},{1... | collective-permute-start | bytes 786440 | tf_op jit(solution)/shard_map/ppermute | solution.py:49
  52.1 7.9 %collective-permute-done.8.rest_2_.rest_12_ = bf16[512,1024]{1,0:T(8,128)(2,1)} collective-permute-done((bf16[512,1024]{1,0:T(8,128)(2,1)}, bf16[512,1024]{1,0:T(8,128)(2,1)}, u32[]{:S(2)}, u32[]{:S(2)}) %collective-permute-start.8) | collective-permute-done | bytes 1048608 | tf_op jit(solution)/shard_map/ag_A/ppermute | solution.py:40
  60.1 2.7 %collective-permute-start.11 = (bf16[512,1024]{1,0:T(8,128)(2,1)}, bf16[512,1024]{1,0:T(8,128)(2,1)S(1)}, u32[]{:S(2)}, u32[]{:S(2)}) collective-permute-start(bf16[512,1024]{1,0:T(8,128)(2,1)} %collective-permute-done.7.rest_3_.rest_11_.rest_9_), channel_id=1, source_target_pairs={{0,12},{1,13},{2,14},{3,15},{4,0},{5,1},{6,2},{7,3},{8,4},{9,5},{1... | collective-permute-start | bytes 3145736 | tf_op jit(solution)/shard_map/ag_D/ppermute | solution.py:40
  62.8 7.9 %weight_grad_blocks.4 = (bf16[512,1024]{1,0:T(8,128)(2,1)}, bf16[512,1024]{1,0:T(8,128)(2,1)}, bf16[512,1024]{1,0:T(8,128)(2,1)}) custom-call(s32[6]{0:T(128)} %stack.26.s_ref, bf16[512,5120]{1,0:T(8,128)(2,1)} %get-tuple-element.50.x0_ref.c0_ref.x_ref.c_ref, bf16[512,5120]{1,0:T(8,128)(2,1)} %copy-done, ...), custom_call_target="tpu_custom_call" | custom-call | bytes 26400000 | tf_op jit(solution)/shard_map/weight_grad_blocks/pallas_call | solution.py:158
  71.0 9.4 %weight_grad_blocks.5 = (bf16[512,1024]{1,0:T(8,128)(2,1)}, bf16[512,1024]{1,0:T(8,128)(2,1)}, bf16[512,1024]{1,0:T(8,128)(2,1)}, bf16[512,1024]{1,0:T(8,128)(2,1)}) custom-call(s32[6]{0:T(128)} %stack.26.s_ref, bf16[512,5120]{1,0:T(8,128)(2,1)} %get-tuple-element.50.x0_ref.c0_ref.x_ref.c_ref, bf16[512,5120]{1,0:T(8,128)(2,1)} %copy-done, ...), custom_call_target="tpu_custom_call" | custom-call | bytes 33000000 | tf_op jit(solution)/shard_map/weight_grad_blocks/pallas_call | solution.py:158
  80.4 10.8 %half_near.1 = (bf16[512,1024]{1,0:T(8,128)(2,1)}, bf16[512,1024]{1,0:T(8,128)(2,1)}, bf16[512,1024]{1,0:T(8,128)(2,1)}) custom-call(s32[6]{0:T(128)} %stack.26.s_ref, bf16[512,5120]{1,0:T(8,128)(2,1)} %copy-done, bf16[512,5120]{1,0:T(8,128)(2,1)} %copy-done, f32[1,8192]{1,0:T(1,128)} %gain_ref.7, bf16[512,1024]{1,0:T(8,128)(2,1)} %bitcast.17, ...), custom_call_target="tpu_custom_call" | custom-call | bytes 33000000 | tf_op jit(solution)/shard_map/half_near/pallas_call | solution.py:246
  91.2 1.4 add_convert_fusion.2
  92.6 1.4 collective-permute-start.13
  94.1 2.9 %collective-permute-start.14 = (f32[512,128]{1,0:T(8,128)S(1)}, f32[512,128]{1,0:T(8,128)S(1)}, u32[]{:S(2)}, u32[]{:S(2)}) collective-permute-start(f32[512,128]{1,0:T(8,128)S(1)} %add.42), channel_id=1, source_target_pairs={{0,16},{16,0},{32,48},{48,32},{64,80},{80,64},{96,112},{112,96},{1... | collective-permute-start | bytes 786440 | tf_op jit(solution)/shard_map/ppermute | solution.py:49
  98.0 10.7 %half_far.1 = (bf16[512,1024]{1,0:T(8,128)(2,1)}, bf16[512,1024]{1,0:T(8,128)(2,1)}, bf16[512,1024]{1,0:T(8,128)(2,1)}) custom-call(s32[6]{0:T(128)} %stack.26.s_ref, bf16[512,5120]{1,0:T(8,128)(2,1)} %copy-done, bf16[512,5120]{1,0:T(8,128)(2,1)} %copy-done, f32[1,8192]{1,0:T(1,128)} %gain_ref.7, ...), custom_call_target="tpu_custom_call" | custom-call | tf_op jit(solution)/shard_map/half_far/pallas_call | solution.py:246
  108.7 8.4 %gain_grad.1 = f32[1,4096]{1,0:T(1,128)} custom-call(s32[6]{0:T(128)} %stack.26.s_ref, bf16[512,1024]{1,0:T(8,128)(2,1)} %get-tuple-element.83.rest_0_.a_ref, bf16[512,1024]{1,0:T(8,128)(2,1)} %get-tuple-element.66.rest_1_, bf16[512,1024]{1,0:T(8,128)(2,1)} %get-tuple-element.67.rest_2_, bf16[512,1024]{1,0:T(8,128)(2,1)} %get-tuple-element.64.rest_3_, ...), custom_call_target="tpu_custom_call" | custom-call | tf_op jit(solution)/shard_map/gain_grad/pallas_call | solution.py:495
  117.6 2.4 %collective-permute-done.24 = f32[1,4096]{1,0:T(1,128)S(1)} collective-permute-done((f32[1,4096]{1,0:T(1,128)}, f32[1,4096]{1,0:T(1,128)S(1)}, u32[]{:S(2)}, u32[]{:S(2)}) %collective-permute-start.24) | collective-permute-done | bytes 16416 | tf_op jit(solution)/shard_map/gain_y/ppermute | solution.py:40
  120.9 2.5 %collective-permute-done.25 = f32[1,4096]{1,0:T(1,128)S(1)} collective-permute-done((f32[1,4096]{1,0:T(1,128)S(1)}, f32[1,4096]{1,0:T(1,128)S(1)}, u32[]{:S(2)}, u32[]{:S(2)}) %collective-permute-start.25) | collective-permute-done | bytes 16416 | tf_op jit(solution)/shard_map/ppermute | solution.py:45
  124.8 2.6 %collective-permute-done.26 = f32[1,4096]{1,0:T(1,128)S(1)} collective-permute-done((f32[1,4096]{1,0:T(1,128)S(1)}, f32[1,4096]{1,0:T(1,128)S(1)}, u32[]{:S(2)}, u32[]{:S(2)}) %collective-permute-start.26) | collective-permute-done | bytes 16416 | tf_op jit(solution)/shard_map/ppermute | solution.py:45
  127.3 6.0 %collective-permute-start.27 = (f32[1,4096]{1,0:T(1,128)S(1)}, f32[1,4096]{1,0:T(1,128)S(1)}, u32[]{:S(2)}, u32[]{:S(2)}) collective-permute-start(f32[1,4096]{1,0:T(1,128)S(1)} %add.50), channel_id=1, source_target_pairs={{0,1},{1,0},{2,3},{3,2},{4,5},{5,4},{6,7},{7,6},{8,9},{9,8},{10,11... | collective-permute-start | bytes 49160 | tf_op jit(solution)/shard_map/gain_c/ppermute | solution.py:40
  135.3 1.6 add_convert_fusion.1
  137.6 2.2 %add_convert_fusion = bf16[512,1024]{1,0:T(8,128)(2,1)S(1)} fusion(bf16[512,1024]{1,0:T(8,128)(2,1)} %collective-permute-done.13, bf16[512,1024]{1,0:T(8,128)(2,1)} %copy-done.10, bf16[512,1024]{1,0:T(8,128)(2,1)S(1)} %copy-done.7), kind=kLoop, calls=%fused_computation | loop fusion | flops 3145728 | bytes 4194304 | tf_op jit(solution)/shard_map/convert_element_type | solution.py:518
  143.1 2.6 %outer_step.1 = (f32[8,1,64,128]{3,2,1,0:T(8,128)}, f32[8,1,64,128]{3,2,1,0:T(8,128)}) custom-call(s32[6]{0:T(128)} %stack.26.s_ref, f32[512,128]{1,0:T(8,128)} %add.44.total_ref.anchor_ref, f32[8,1,64,128]{3,2,1,0:T(8,128)} %a_ref.3, f32[8,1,64,128]{3,2,1,0:T(8,128)} %m_ref.3), custom_call_target="tpu_custom_call" | custom-call | bytes 330000000 | tf_op jit(solution)/shard_map/outer_step/pallas_call | solution.py:465
  146.7 25.7 %hidden_grad.1 = (bf16[512,1024]{1,0:T(8,128)(2,1)}, bf16[512,8192]{1,0:T(8,128)(2,1)}) custom-call(s32[6]{0:T(128)} %stack.26.s_ref, bf16[512,5120]{1,0:T(8,128)(2,1)} %get-tuple-element.50.x0_ref.c0_ref.x_ref.c_ref, bf16[512,5120]{1,0:T(8,128)(2,1)} %get-tuple-element.50.x0_ref.c0_ref.x_ref.c_ref, f32[1,8192]{1,0:T(1,128)} %gain_ref.7, ...), custom_call_target="tpu_custom_call" | custom-call | bytes 330000000 | tf_op jit(solution)/shard_map/hidden_grad/pallas_call | solution.py:351
  174.7 4.4 %update.1 = bf16[512,1024]{1,0:T(8,128)(2,1)} custom-call(s32[6]{0:T(128)} %stack.26.s_ref, bf16[512,1024]{1,0:T(8,128)(2,1)} %bitcast.20, bf16[512,1024]{1,0:T(8,128)(2,1)} %get-tuple-element.83.rest_0_.a_ref, bf16[512,1024]{1,0:T(8,128)(2,1)} %copy-done.12, bf16[512,1024]{1,0:T(8,128)(2,1)} %copy-done.11, bf16[512,1024]{1,0:T(8,128)(2,1)} %copy-done.13, ...), custom_call_target="tpu_custom_call" | custom-call | bytes 9900000 | tf_op jit(solution)/shard_map/update/pallas_call | solution.py:405
  (84 shorter events, 15.3 us)
Async XLA Ops:
  0.6 25.0 %collective-permute-start.1 = (bf16[512,1024]{1,0:T(8,128)(2,1)}, bf16[512,1024]{1,0:T(8,128)(2,1)S(1)}, u32[]{:S(2)}, u32[]{:S(2)}) collective-permute-start(bf16[512,1024]{1,0:T(8,128)(2,1)} %bitcast.13), channel_id=1, source_target_pairs={{0,2},{1,3},{2,0},{3,1},{4,6},{5,7},{6,4},{7,5},{8,10},{9,11},{10,... | collective-permute-start | bytes 3145736 | tf_op jit(solution)/shard_map/ag_y/ppermute | solution.py:40
  2.8 25.6 %collective-permute-start.2 = (bf16[512,1024]{1,0:T(8,128)(2,1)}, bf16[512,1024]{1,0:T(8,128)(2,1)S(1)}, u32[]{:S(2)}, u32[]{:S(2)}) collective-permute-start(bf16[512,1024]{1,0:T(8,128)(2,1)} %bitcast.14), channel_id=1, source_target_pairs={{0,12},{1,13},{2,14},{3,15},{4,0},{5,1},{6,2},{7,3},{8,4},{9,5},{1... | collective-permute-start | bytes 3145736 | tf_op jit(solution)/shard_map/ag_zm/ppermute | solution.py:40
  6.6 24.9 %collective-permute-start.3 = (bf16[512,1024]{1,0:T(8,128)(2,1)}, bf16[512,1024]{1,0:T(8,128)(2,1)}, u32[]{:S(2)}, u32[]{:S(2)}) collective-permute-start(bf16[512,1024]{1,0:T(8,128)(2,1)} %bitcast.15), channel_id=1, source_target_pairs={{0,4},{1,5},{2,6},{3,7},{4,8},{5,9},{6,10},{7,11},{8,12},{9,13},{1... | collective-permute-start | bytes 3145736 | tf_op jit(solution)/shard_map/ag_zp/ppermute | solution.py:40
  10.2 11.7 %collective-permute-start = (f32[512,128]{1,0:T(8,128)}, f32[512,128]{1,0:T(8,128)S(1)}, u32[]{:S(2)}, u32[]{:S(2)}) collective-permute-start(f32[512,128]{1,0:T(8,128)} %outer_term.1), channel_id=1, source_target_pairs={{0,32},{16,48},{32,0},{48,16},{64,96},{80,112},{96,64},{112,80},{1... | collective-permute-start | bytes 786440 | tf_op jit(solution)/shard_map/ppermute | solution.py:49
  25.6 34.4 %copy-start.1 = (bf16[512,1024]{1,0:T(8,128)(2,1)}, bf16[512,1024]{1,0:T(8,128)(2,1)S(1)}, u32[]{:S(2)}) copy-start(bf16[512,1024]{1,0:T(8,128)(2,1)S(1)} %collective-permute-done.1.rest_1_.rest_9_.rest_7_) | copy-start | bytes 3145732
  28.4 20.9 %copy-start.2 = (bf16[512,1024]{1,0:T(8,128)(2,1)}, bf16[512,1024]{1,0:T(8,128)(2,1)S(1)}, u32[]{:S(2)}) copy-start(bf16[512,1024]{1,0:T(8,128)(2,1)S(1)} %collective-permute-done.2.rest_2_.rest_10_.rest_8_) | copy-start | bytes 3145732
  31.5 10.7 %collective-permute-start.4 = (bf16[512,5120]{1,0:T(8,128)(2,1)}, bf16[512,5120]{1,0:T(8,128)(2,1)S(1)}, u32[]{:S(2)}, u32[]{:S(2)}) collective-permute-start(bf16[512,5120]{1,0:T(8,128)(2,1)} %get-tuple-element.48), channel_id=1, source_target_pairs={{0,1},{1,0},{2,3},{3,2},{4,5},{5,4},{6,7},{7,6},{8,9},{9,8},{10,11... | collective-permute-start | bytes 15728648 | tf_op jit(solution)/shard_map/swap_x/ppermute | solution.py:40
  33.7 26.3 %collective-permute-start.8 = (bf16[512,1024]{1,0:T(8,128)(2,1)}, bf16[512,1024]{1,0:T(8,128)(2,1)}, u32[]{:S(2)}, u32[]{:S(2)}) collective-permute-start(bf16[512,1024]{1,0:T(8,128)(2,1)} %collective-permute-done.3.rest_0_.rest_14_.rest_10_), channel_id=1, source_target_pairs={{0,4},{1,5},{2,6},{3,7},{4,8},{5,9},{6,10},{7,11},{8,12},{9,13},{1... | collective-permute-start | bytes 3145736 | tf_op jit(solution)/shard_map/ag_A/ppermute | solution.py:40
  33.7 26.4 %collective-permute-start.7 = (bf16[512,1024]{1,0:T(8,128)(2,1)S(1)}, bf16[512,1024]{1,0:T(8,128)(2,1)}, u32[]{:S(2)}, u32[]{:S(2)}) collective-permute-start(bf16[512,1024]{1,0:T(8,128)(2,1)S(1)} %collective-permute-done.1.rest_1_.rest_9_.rest_7_), channel_id=1, source_target_pairs={{0,12},{1,13},{2,14},{3,15},{4,0},{5,1},{6,2},{7,3},{8,4},{9,5},{1... | collective-permute-start | bytes 3145736 | tf_op jit(solution)/shard_map/ag_B/ppermute | solution.py:40
  49.4 41.9 %collective-permute-start.9 = (bf16[512,1024]{1,0:T(8,128)(2,1)}, bf16[512,1024]{1,0:T(8,128)(2,1)S(1)}, u32[]{:S(2)}, u32[]{:S(2)}) collective-permute-start(bf16[512,1024]{1,0:T(8,128)(2,1)} %weight_grad_blocks.3.rest_5_), channel_id=1, source_target_pairs={{0,2},{1,3},{2,0},{3,1},{4,6},{5,7},{6,4},{7,5},{8,10},{9,11},{10,... | collective-permute-start | bytes 3145736 | tf_op jit(solution)/shard_map/rs_D/ppermute | solution.py:40
  49.6 10.4 %collective-permute-start.5 = (f32[512,128]{1,0:T(8,128)S(1)}, f32[512,128]{1,0:T(8,128)S(1)}, u32[]{:S(2)}, u32[]{:S(2)}) collective-permute-start(f32[512,128]{1,0:T(8,128)S(1)} %add.41), channel_id=1, source_target_pairs={{0,96},{16,112},{32,64},{48,80},{64,32},{80,48},{96,0},{112,16},{1... | collective-permute-start | bytes 786440 | tf_op jit(solution)/shard_map/ppermute | solution.py:49
  60.0 34.0 %collective-permute-start.10 = (bf16[512,1024]{1,0:T(8,128)(2,1)S(1)}, bf16[512,1024]{1,0:T(8,128)(2,1)S(1)}, u32[]{:S(2)}, u32[]{:S(2)}) collective-permute-start(bf16[512,1024]{1,0:T(8,128)(2,1)S(1)} %collective-permute-done.1.rest_1_.rest_9_.rest_7_), channel_id=1, source_target_pairs={{0,4},{1,5},{2,6},{3,7},{4,8},{5,9},{6,10},{7,11},{8,12},{9,13},{1... | collective-permute-start | bytes 3145736 | tf_op jit(solution)/shard_map/ag_C/ppermute | solution.py:40
  60.1 36.9 %collective-permute-start.11 = (bf16[512,1024]{1,0:T(8,128)(2,1)}, bf16[512,1024]{1,0:T(8,128)(2,1)S(1)}, u32[]{:S(2)}, u32[]{:S(2)}) collective-permute-start(bf16[512,1024]{1,0:T(8,128)(2,1)} %collective-permute-done.7.rest_3_.rest_11_.rest_9_), channel_id=1, source_target_pairs={{0,12},{1,13},{2,14},{3,15},{4,0},{5,1},{6,2},{7,3},{8,4},{9,5},{1... | collective-permute-start | bytes 3145736 | tf_op jit(solution)/shard_map/ag_D/ppermute | solution.py:40
  70.7 38.0 %collective-permute-start.12 = (bf16[512,1024]{1,0:T(8,128)(2,1)}, bf16[512,1024]{1,0:T(8,128)(2,1)S(1)}, u32[]{:S(2)}, u32[]{:S(2)}) collective-permute-start(bf16[512,1024]{1,0:T(8,128)(2,1)} %get-tuple-element.64.rest_3_), channel_id=1, source_target_pairs={{0,2},{1,3},{2,0},{3,1},{4,6},{5,7},{6,4},{7,5},{8,10},{9,11},{10,... | collective-permute-start | bytes 3145736 | tf_op jit(solution)/shard_map/rs_B/ppermute | solution.py:40
  71.0 62.9 %collective-permute-start.6 = (bf16[512,1024]{1,0:T(8,128)(2,1)}, bf16[512,1024]{1,0:T(8,128)(2,1)}, u32[]{:S(2)}, u32[]{:S(2)}) collective-permute-start(bf16[512,1024]{1,0:T(8,128)(2,1)} %get-tuple-element.52.rest_7_), channel_id=1, source_target_pairs={{0,12},{1,13},{2,14},{3,15},{4,0},{5,1},{6,2},{7,3},{8,4},{9,5},{1... | collective-permute-start | bytes 3145736 | tf_op jit(solution)/shard_map/rs_C/ppermute | solution.py:40
  80.4 10.8 %copy-start.6 = (bf16[512,1024]{1,0:T(8,128)(2,1)S(1)}, bf16[512,1024]{1,0:T(8,128)(2,1)}, u32[]{:S(2)}) copy-start(bf16[512,1024]{1,0:T(8,128)(2,1)} %get-tuple-element.53.rest_4_) | copy-start | bytes 3145732
  92.6 44.5 %collective-permute-start.13 = (bf16[512,1024]{1,0:T(8,128)(2,1)}, bf16[512,1024]{1,0:T(8,128)(2,1)}, u32[]{:S(2)}, u32[]{:S(2)}) collective-permute-start(bf16[512,1024]{1,0:T(8,128)(2,1)} %add_convert_fusion.2), channel_id=1, source_target_pairs={{0,4},{1,5},{2,6},{3,7},{4,8},{5,9},{6,10},{7,11},{8,12},{9,13},{1... | collective-permute-start | bytes 3145736 | tf_op jit(solution)/shard_map/rs_A/ppermute | solution.py:40
  94.1 39.4 %collective-permute-start.14 = (f32[512,128]{1,0:T(8,128)S(1)}, f32[512,128]{1,0:T(8,128)S(1)}, u32[]{:S(2)}, u32[]{:S(2)}) collective-permute-start(f32[512,128]{1,0:T(8,128)S(1)} %add.42), channel_id=1, source_target_pairs={{0,16},{16,0},{32,48},{48,32},{64,80},{80,64},{96,112},{112,96},{1... | collective-permute-start | bytes 786440 | tf_op jit(solution)/shard_map/ppermute | solution.py:49
  108.7 26.6 %copy-start.5 = (bf16[512,1024]{1,0:T(8,128)(2,1)S(1)}, bf16[512,1024]{1,0:T(8,128)(2,1)}, u32[]{:S(2)}) copy-start(bf16[512,1024]{1,0:T(8,128)(2,1)} %get-tuple-element.66.rest_1_) | copy-start | bytes 3145732
  117.1 2.9 %collective-permute-start.24 = (f32[1,4096]{1,0:T(1,128)}, f32[1,4096]{1,0:T(1,128)S(1)}, u32[]{:S(2)}, u32[]{:S(2)}) collective-permute-start(f32[1,4096]{1,0:T(1,128)} %gain_grad.1), channel_id=1, source_target_pairs={{0,2},{1,3},{2,0},{3,1},{4,6},{5,7},{6,4},{7,5},{8,10},{9,11},{10,... | collective-permute-start | bytes 49160 | tf_op jit(solution)/shard_map/gain_y/ppermute | solution.py:40
  120.8 2.7 %collective-permute-start.25 = (f32[1,4096]{1,0:T(1,128)S(1)}, f32[1,4096]{1,0:T(1,128)S(1)}, u32[]{:S(2)}, u32[]{:S(2)}) collective-permute-start(f32[1,4096]{1,0:T(1,128)S(1)} %add.48), channel_id=1, source_target_pairs={{0,4},{1,5},{2,6},{3,7},{4,0},{5,1},{6,2},{7,3},{8,12},{9,13},{10,... | collective-permute-start | bytes 49160 | tf_op jit(solution)/shard_map/ppermute | solution.py:45
  123.4 3.9 %collective-permute-start.26 = (f32[1,4096]{1,0:T(1,128)S(1)}, f32[1,4096]{1,0:T(1,128)S(1)}, u32[]{:S(2)}, u32[]{:S(2)}) collective-permute-start(f32[1,4096]{1,0:T(1,128)S(1)} %add.49), channel_id=1, source_target_pairs={{0,12},{1,13},{2,14},{3,15},{4,8},{5,9},{6,10},{7,11},{8,4},{9,5},... | collective-permute-start | bytes 49160 | tf_op jit(solution)/shard_map/ppermute | solution.py:45
  127.3 6.8 %collective-permute-start.27 = (f32[1,4096]{1,0:T(1,128)S(1)}, f32[1,4096]{1,0:T(1,128)S(1)}, u32[]{:S(2)}, u32[]{:S(2)}) collective-permute-start(f32[1,4096]{1,0:T(1,128)S(1)} %add.50), channel_id=1, source_target_pairs={{0,1},{1,0},{2,3},{3,2},{4,5},{5,4},{6,7},{7,6},{8,9},{9,8},{10,11... | collective-permute-start | bytes 49160 | tf_op jit(solution)/shard_map/gain_c/ppermute | solution.py:40
  133.3 6.5 %collective-permute-start.15 = (bf16[512,1024]{1,0:T(8,128)(2,1)}, bf16[512,1024]{1,0:T(8,128)(2,1)}, u32[]{:S(2)}, u32[]{:S(2)}) collective-permute-start(bf16[512,1024]{1,0:T(8,128)(2,1)} %get-tuple-element.59), channel_id=1, source_target_pairs={{0,1},{1,0},{2,3},{3,2},{4,5},{5,4},{6,7},{7,6},{8,9},{9,8},{10,11... | collective-permute-start | bytes 3145736 | tf_op jit(solution)/shard_map/swap_w0/ppermute | solution.py:40
  133.4 7.4 %collective-permute-start.16 = (bf16[512,1024]{1,0:T(8,128)(2,1)}, bf16[512,1024]{1,0:T(8,128)(2,1)}, u32[]{:S(2)}, u32[]{:S(2)}) collective-permute-start(bf16[512,1024]{1,0:T(8,128)(2,1)} %get-tuple-element.77), channel_id=1, source_target_pairs={{0,1},{1,0},{2,3},{3,2},{4,5},{5,4},{6,7},{7,6},{8,9},{9,8},{10,11... | collective-permute-start | bytes 3145736 | tf_op jit(solution)/shard_map/swap_w0/ppermute | solution.py:40
  133.9 7.7 %collective-permute-start.19 = (bf16[512,1024]{1,0:T(8,128)(2,1)}, bf16[512,1024]{1,0:T(8,128)(2,1)}, u32[]{:S(2)}, u32[]{:S(2)}) collective-permute-start(bf16[512,1024]{1,0:T(8,128)(2,1)} %get-tuple-element.79), channel_id=1, source_target_pairs={{0,1},{1,0},{2,3},{3,2},{4,5},{5,4},{6,7},{7,6},{8,9},{9,8},{10,11... | collective-permute-start | bytes 3145736 | tf_op jit(solution)/shard_map/swap_w0/ppermute | solution.py:40
  134.2 7.5 %collective-permute-start.17 = (bf16[512,1024]{1,0:T(8,128)(2,1)}, bf16[512,1024]{1,0:T(8,128)(2,1)}, u32[]{:S(2)}, u32[]{:S(2)}) collective-permute-start(bf16[512,1024]{1,0:T(8,128)(2,1)} %get-tuple-element.63), channel_id=1, source_target_pairs={{0,1},{1,0},{2,3},{3,2},{4,5},{5,4},{6,7},{7,6},{8,9},{9,8},{10,11... | collective-permute-start | bytes 3145736 | tf_op jit(solution)/shard_map/swap_w1/ppermute | solution.py:40
  137.1 35.3 %collective-permute-start.22 = (bf16[512,1024]{1,0:T(8,128)(2,1)S(1)}, bf16[512,1024]{1,0:T(8,128)(2,1)S(1)}, u32[]{:S(2)}, u32[]{:S(2)}) collective-permute-start(bf16[512,1024]{1,0:T(8,128)(2,1)S(1)} %add_convert_fusion.1), channel_id=1, source_target_pairs={{0,2},{1,3},{2,0},{3,1},{4,6},{5,7},{6,4},{7,5},{8,10},{9,11},{10,... | collective-permute-start | bytes 3145736 | tf_op jit(solution)/shard_map/rs_y/ppermute | solution.py:40
  139.8 32.6 %collective-permute-start.21 = (bf16[512,1024]{1,0:T(8,128)(2,1)S(1)}, bf16[512,1024]{1,0:T(8,128)(2,1)S(1)}, u32[]{:S(2)}, u32[]{:S(2)}) collective-permute-start(bf16[512,1024]{1,0:T(8,128)(2,1)S(1)} %copy-done.8), channel_id=1, source_target_pairs={{0,12},{1,13},{2,14},{3,15},{4,0},{5,1},{6,2},{7,3},{8,4},{9,5},{1... | collective-permute-start | bytes 3145736 | tf_op jit(solution)/shard_map/rs_zm/ppermute | solution.py:40
  140.8 4.8 %collective-permute-start.18 = (bf16[512,1024]{1,0:T(8,128)(2,1)}, bf16[512,1024]{1,0:T(8,128)(2,1)S(1)}, u32[]{:S(2)}, u32[]{:S(2)}) collective-permute-start(bf16[512,1024]{1,0:T(8,128)(2,1)} %get-tuple-element.78), channel_id=1, source_target_pairs={{0,1},{1,0},{2,3},{3,2},{4,5},{5,4},{6,7},{7,6},{8,9},{9,8},{10,11... | collective-permute-start | bytes 3145736 | tf_op jit(solution)/shard_map/swap_w1/ppermute | solution.py:40
  141.6 4.1 %collective-permute-start.20 = (bf16[512,1024]{1,0:T(8,128)(2,1)}, bf16[512,1024]{1,0:T(8,128)(2,1)}, u32[]{:S(2)}, u32[]{:S(2)}) collective-permute-start(bf16[512,1024]{1,0:T(8,128)(2,1)} %get-tuple-element.80), channel_id=1, source_target_pairs={{0,1},{1,0},{2,3},{3,2},{4,5},{5,4},{6,7},{7,6},{8,9},{9,8},{10,11... | collective-permute-start | bytes 3145736 | tf_op jit(solution)/shard_map/swap_w1/ppermute | solution.py:40
  141.7 30.8 %collective-permute-start.23 = (bf16[512,1024]{1,0:T(8,128)(2,1)S(1)}, bf16[512,1024]{1,0:T(8,128)(2,1)S(1)}, u32[]{:S(2)}, u32[]{:S(2)}) collective-permute-start(bf16[512,1024]{1,0:T(8,128)(2,1)S(1)} %add_convert_fusion), channel_id=1, source_target_pairs={{0,4},{1,5},{2,6},{3,7},{4,8},{5,9},{6,10},{7,11},{8,12},{9,13},{1... | collective-permute-start | bytes 3145736 | tf_op jit(solution)/shard_map/rs_zp/ppermute | solution.py:40
  (12 other events, 40.6 us)

commit v2 on v1

--- a/solution.py
+++ b/solution.py
@@ -16,7 +16,7 @@
 KV = 1024
 HALF = D // 2
 WIDE = HALF + KV
-VMEM = 56 * 1024 * 1024
+VMEM = 62 * 1024 * 1024
 NZ, NY, NC = 4, 2, 2
 bf16, f32 = jnp.bfloat16, jnp.float32
 
@@ -73,7 +73,8 @@
     return v[:, k * 128 : (k + 1) * 128]
 
 
-def norm_kernel(s_ref, x_ref, cot_ref, gain_ref, excl_ref, mine_ref, send_ref, inv_ref):
+def norm_kernel(s_ref, x_ref, cot_ref, gain_ref, excl_ref, mine_ref, *rest):
+    sends, (masked_ref, inv_ref) = rest[:NZ], rest[NZ:]
     core = s_ref[CORE]
     rows = x_ref.shape[0]
     position = s_ref[FIRST] + pl.program_id(0) * rows
@@ -82,7 +83,7 @@
     kept = 1.0 - jnp.max(hits, axis=1, keepdims=True)
     masked = (cot_ref[...].astype(f32) * kept).astype(bf16)
     mine_ref[:, HALF:] = masked
-    send_ref[:, HALF:] = masked
+    masked_ref[...] = masked
     total = jnp.zeros((rows, 128), f32)
     for b in range(D // 128):
         v = x_ref[:, b * 128 : (b + 1) * 128].astype(f32)
@@ -90,14 +91,21 @@
     total = jnp.sum(total, axis=1, keepdims=True)
     inverse = jnp.broadcast_to(lax.rsqrt(total / D + 1e-05), inv_ref.shape)
     inv_ref[...] = inverse
+
+    def scaled(at, out, to):
+        x = x_ref[:, pl.ds(at, ROWS)].astype(f32)
+        gain = gain_ref[:, pl.ds(at, ROWS)]
+        for k in range(ROWS // 128):
+            v = lanes(x, k) * inverse * lanes(gain, k)
+            out[:, to + k * 128 : to + (k + 1) * 128] = v.astype(bf16)
+
     for j in range(HALF // ROWS):
-        for parity, out in ((core, mine_ref), (1 - core, send_ref)):
-            at = pl.multiple_of((2 * j + parity) * ROWS, ROWS)
-            x = x_ref[:, pl.ds(at, ROWS)].astype(f32)
-            gain = gain_ref[:, pl.ds(at, ROWS)]
-            for k in range(ROWS // 128):
-                v = lanes(x, k) * inverse * lanes(gain, k)
-                out[:, j * ROWS + k * 128 : j * ROWS + (k + 1) * 128] = v.astype(bf16)
+        scaled(pl.multiple_of((2 * j + core) * ROWS, ROWS), mine_ref, j * ROWS)
+    for dz, send_ref in enumerate(sends):
+        first = lax.rem(s_ref[Z] + dz, NZ) * NY
+        for y in range(NY):
+            at = pl.multiple_of((2 * (first + y) + 1 - core) * ROWS, ROWS)
+            scaled(at, send_ref, y * ROWS)
 
 
 def norm_call(scalars, hidden, cot, gain, excl):
@@ -115,13 +123,15 @@
             ],
             out_specs=[
                 pl.BlockSpec((tile, WIDE), lambda t, s: (t, 0)),
-                pl.BlockSpec((tile, WIDE), lambda t, s: (t, 0)),
+                *[pl.BlockSpec((tile, PAIR), lambda t, s: (t, 0))] * NZ,
+                pl.BlockSpec((tile, KV), lambda t, s: (t, 0)),
                 pl.BlockSpec((tile, 128), lambda t, s: (t, 0)),
             ],
         ),
         out_shape=[
             jax.ShapeDtypeStruct((ROWS, WIDE), bf16),
-            jax.ShapeDtypeStruct((ROWS, WIDE), bf16),
+            *[jax.ShapeDtypeStruct((ROWS, PAIR), bf16)] * NZ,
+            jax.ShapeDtypeStruct((ROWS, KV), bf16),
             jax.ShapeDtypeStruct((ROWS, 128), f32),
         ],
         compiler_params=params(1),
@@ -130,14 +140,33 @@
     )(scalars, hidden, cot, gain, excl)
 
 
-def grad_kernel(count, s_ref, x0_ref, x1_ref, c0_ref, c1_ref, *rest):
-    outs, (held, sems) = rest[:count], rest[count:]
+def grad_kernel(places, s_ref, x0_ref, c0_ref, c1_ref, *rest):
+    count = len(places)
+    x1_refs, outs, (x1, x1_sems, held, sems) = rest[:count], rest[count : 2 * count], rest[2 * count :]
     step = pl.program_id(0)
     dims = (((0,), (0,)), ((), ()))
+    loads = []
+    for k, (_, dy) in enumerate(places):
+        at = pl.multiple_of(lax.rem(s_ref[Y] + dy, NY) * ROWS, ROWS)
+        loads.append(
+            pltpu.make_async_copy(x1_refs[k].at[:, pl.ds(at, ROWS)], x1.at[k], x1_sems.at[k])
+        )
+    copies = [pltpu.make_async_copy(held.at[k % 2], outs[k], sems.at[k % 2]) for k in range(count)]
+
+    @pl.when(step == 0)
+    def _():
+        for load in loads:
+            load.start()
+
     total = lax.dot_general(x0_ref[...], c0_ref[...], dims, preferred_element_type=f32)
-    total = total + lax.dot_general(x1_ref[...], c1_ref[...], dims, preferred_element_type=f32)
+    for k in range(count):
+
+        @pl.when(step == k)
+        def _(k=k):
+            loads[k].wait()
+
+    total = total + lax.dot_general(x1[step], c1_ref[...], dims, preferred_element_type=f32)
     total = total.astype(bf16)
-    copies = [pltpu.make_async_copy(held.at[k % 2], outs[k], sems.at[k % 2]) for k in range(count)]
     for k in range(count):
 
         @pl.when(step == k)
@@ -151,24 +180,33 @@
                     copy.wait()
 
 
-def grad_call(places, scalars, mine, recv, estimate):
+def grad_call(places, scalars, mine, recv, recv_cot, estimate):
     count = len(places)
-    x = pl.BlockSpec((ROWS, ROWS), lambda t, s: (0, block_of(s, t, places)))
-    c = pl.BlockSpec((ROWS, KV), lambda t, s: (0, HALF // KV))
+    c = pl.BlockSpec((ROWS, KV), lambda t, s: (0, 0))
     return pl.pallas_call(
-        functools.partial(grad_kernel, count),
+        functools.partial(grad_kernel, places),
         grid_spec=pltpu.PrefetchScalarGridSpec(
             num_scalar_prefetch=1,
             grid=(count,),
-            in_specs=[x, x, c, c],
-            out_specs=[pl.BlockSpec(memory_space=pl.ANY)] * count,
-            scratch_shapes=[pltpu.VMEM((2, ROWS, KV), bf16), pltpu.SemaphoreType.DMA((2,))],
+            in_specs=[
+                pl.BlockSpec((ROWS, ROWS), lambda t, s: (0, block_of(s, t, places))),
+                pl.BlockSpec((ROWS, KV), lambda t, s: (0, HALF // KV)),
+                c,
+            ]
+            + [pl.BlockSpec(memory_space=pltpu.HBM)] * count,
+            out_specs=[pl.BlockSpec(memory_space=pltpu.HBM)] * count,
+            scratch_shapes=[
+                pltpu.VMEM((count, ROWS, ROWS), bf16),
+                pltpu.SemaphoreType.DMA((count,)),
+                pltpu.VMEM((2, ROWS, KV), bf16),
+                pltpu.SemaphoreType.DMA((2,)),
+            ],
         ),
         out_shape=[jax.ShapeDtypeStruct((ROWS, KV), bf16)] * count,
         compiler_params=params(1),
         cost_estimate=cost(estimate),
         name="weight_grad_blocks",
-    )(scalars, mine, recv, mine, recv)
+    )(scalars, mine, mine, recv_cot, *[recv[dz] for dz, _ in places])
 
 
 def weight_copies(depths, s_ref, weights, held, sems):
@@ -183,11 +221,12 @@
     return copies
 
 
-def half_kernel(depths, s_ref, x_ref, c_ref, gain_ref, *rest):
+def half_kernel(depths, s_ref, c_ref, gain_ref, *rest):
     count = len(depths)
-    weights, rest = rest[: NY * count], rest[NY * count :]
-    outs, (held, sems, values, made, out_sems) = rest[: count + 1], rest[count + 1 :]
+    xs, weights, rest = rest[:count], rest[count : 3 * count], rest[3 * count :]
+    outs, (x, x_sems, held, sems, values, made, out_sems) = rest[: count + 1], rest[count + 1 :]
     step = pl.program_id(0)
+    loads = [pltpu.make_async_copy(ref, x.at[k], x_sems.at[k]) for k, ref in enumerate(xs)]
     copies = weight_copies(depths, s_ref, weights, held, sems)
     back = [
         pltpu.make_async_copy(made.at[k % 2], outs[k], out_sems.at[k % 2]) for k in range(count + 1)
@@ -195,20 +234,23 @@
 
     @pl.when(step == 0)
     def _():
-        for copy in copies:
-            copy.start()
+        for k in range(count):
+            loads[k].start()
+            copies[NY * k].start()
+            copies[NY * k + 1].start()
 
     for k in range(count):
 
         @pl.when(step == k)
         def _(k=k):
+            loads[k].wait()
             copies[NY * k].wait()
             copies[NY * k + 1].wait()
             if k >= 2:
                 back[k - 2].wait()
 
     w = held[step]
-    part = jnp.dot(x_ref[...], w, preferred_element_type=f32)
+    part = jnp.dot(x[step], w, preferred_element_type=f32)
 
     @pl.when(step == 0)
     def _():
@@ -240,7 +282,7 @@
                 back[count].wait()
 
 
-def half_call(depths, scalars, x, gain, w, name, estimate):
+def half_call(depths, scalars, x, cot, gain, w, name, estimate):
     count = len(depths)
     weights = [w[dz, dy] for dz in depths for dy in range(NY)]
     return pl.pallas_call(
@@ -249,13 +291,14 @@
             num_scalar_prefetch=1,
             grid=(count,),
             in_specs=[
-                pl.BlockSpec((ROWS, PAIR), lambda t, s: (0, pair_of(s, t, depths))),
-                pl.BlockSpec((ROWS, KV), lambda t, s: (0, HALF // KV)),
+                pl.BlockSpec((ROWS, KV), lambda t, s: (0, 0)),
                 pl.BlockSpec((1, D), lambda t, s: (0, 0)),
             ]
-            + [pl.BlockSpec(memory_space=pl.ANY)] * len(weights),
-            out_specs=[pl.BlockSpec(memory_space=pl.ANY)] * (count + 1),
+            + [pl.BlockSpec(memory_space=pltpu.HBM)] * (count + len(weights)),
+            out_specs=[pl.BlockSpec(memory_space=pltpu.HBM)] * (count + 1),
             scratch_shapes=[
+                pltpu.VMEM((count, ROWS, PAIR), bf16),
+                pltpu.SemaphoreType.DMA((count,)),
                 pltpu.VMEM((count, PAIR, KV), bf16),
                 pltpu.SemaphoreType.DMA((NY * count,)),
                 pltpu.VMEM((ROWS, KV), f32),
@@ -267,7 +310,7 @@
         compiler_params=params(1),
         cost_estimate=cost(estimate),
         name=name,
-    )(scalars, x, x, gain, *weights)
+    )(scalars, cot, gain, *[x[dz] for dz in depths], *weights)
 
 
 def hidden_kernel(depths, s_ref, x_ref, c_ref, gain_ref, inv_ref, h_ref, *rest):
@@ -362,8 +405,8 @@
                 pl.BlockSpec((ROWS, 128), lambda t, s: (0, 0)),
                 pl.BlockSpec((ROWS, 2 * PAIR), lambda t, s: (0, place(t, s))),
             ]
-            + [pl.BlockSpec(memory_space=pl.ANY)] * len(gots)
-            + [pl.BlockSpec(memory_space=pl.ANY)] * len(weights),
+            + [pl.BlockSpec(memory_space=pltpu.HBM)] * len(gots)
+            + [pl.BlockSpec(memory_space=pltpu.HBM)] * len(weights),
             out_specs=[
                 pl.BlockSpec((ROWS, KV), lambda t, s: (0, 0)),
                 pl.BlockSpec((ROWS, 2 * PAIR), lambda t, s: (0, place(t, s))),
@@ -387,34 +430,60 @@
     )(scalars, mine, mine, gain, inverse, hidden, *gots, *weights)
 
 
-def update_kernel(rate, s_ref, w_ref, a_ref, b_ref, c_ref, d_ref, anchor_ref, out_ref):
+def update_kernel(rate, s_ref, w_ref, a_ref, b_ref, c_ref, d_ref, total_ref, *rest):
+    anchor_ref, momentum_ref, all_ref, out_ref, anchor_out, momentum_out = rest
     grad = a_ref[...].astype(f32) + b_ref[...].astype(f32)
     grad = grad + (c_ref[...].astype(f32) + d_ref[...].astype(f32))
     out_ref[...] = (w_ref[...].astype(f32) - rate * grad).astype(bf16)
-    cols = anchor_ref.shape[1]
+    cols = total_ref.shape[1]
     at = pl.ds(pl.multiple_of(s_ref[FRAG] * cols, cols), cols)
     grad = a_ref[:, at].astype(f32) + b_ref[:, at].astype(f32)
     grad = grad + (c_ref[:, at].astype(f32) + d_ref[:, at].astype(f32))
     now = w_ref[:, at].astype(f32) - rate * grad
-    out_ref[:, at] = (mix_weight * anchor_ref[...] + (1.0 - mix_weight) * now).astype(bf16)
-
-
-def update_call(rate, scalars, weight, parts, anchor):
+    out_ref[:, at] = (mix_weight * total_ref[...] + (1.0 - mix_weight) * now).astype(bf16)
+
+    @pl.when(pl.program_id(0) == 0)
+    def _():
+        anchor_out[...] = anchor_ref[...]
+        momentum_out[...] = momentum_ref[...]
+        rows = anchor_ref.shape[2]
+        frag = s_ref[FRAG]
+        a, m = anchor_ref[frag, 0], momentum_ref[frag, 0]
+        at = pl.ds(pl.multiple_of(s_ref[REPLICA] * rows, rows), rows)
+        kept = (1.0 - by_delta) * a - by_momentum * m
+        delta = a - (all_ref[at, :] - kept) / by_delta
+        m_new = outer_momentum * m + delta
+        momentum_out[frag, 0] = m_new
+        anchor_out[frag, 0] = a - outer_rate * (delta + outer_momentum * m_new)
+
+
+def update_call(rate, scalars, weight, parts, total, anchor, momentum):
     tile = 256
     row = pl.BlockSpec((tile, KV), lambda t, s: (t, 0))
+    whole = pl.BlockSpec(anchor.shape, lambda t, s: (0, 0, 0, 0))
     return pl.pallas_call(
         functools.partial(update_kernel, rate),
         grid_spec=pltpu.PrefetchScalarGridSpec(
             num_scalar_prefetch=1,
             grid=(ROWS // tile,),
-            in_specs=[row] * 5 + [pl.BlockSpec((tile, anchor.shape[1]), lambda t, s: (t, 0))],
-            out_specs=row,
+            in_specs=[
+                *[row] * 5,
+                pl.BlockSpec((tile, total.shape[1]), lambda t, s: (t, 0)),
+                whole,
+                whole,
+                pl.BlockSpec(total.shape, lambda t, s: (0, 0)),
+            ],
+            out_specs=[row, whole, whole],
         ),
-        out_shape=jax.ShapeDtypeStruct((ROWS, KV), bf16),
+        out_shape=[
+            jax.ShapeDtypeStruct((ROWS, KV), bf16),
+            jax.ShapeDtypeStruct(anchor.shape, f32),
+            jax.ShapeDtypeStruct(anchor.shape, f32),
+        ],
         compiler_params=params(1),
         cost_estimate=cost(3),
         name="update",
-    )(scalars, weight, *parts, anchor)
+    )(scalars, weight, *parts, total, anchor, momentum, total)
 
 
 by_delta = outer_rate * (1.0 + outer_momentum)
@@ -446,41 +515,17 @@
     )(scalars, weight, anchor, momentum)
 
 
-def outer_kernel(s_ref, total_ref, a_ref, m_ref, a_out, m_out):
-    a_out[...] = a_ref[...]
-    m_out[...] = m_ref[...]
-    rows = a_ref.shape[2]
-    frag = s_ref[FRAG]
-    a, m = a_ref[frag, 0], m_ref[frag, 0]
-    at = pl.ds(pl.multiple_of(s_ref[REPLICA] * rows, rows), rows)
-    kept = (1.0 - by_delta) * a - by_momentum * m
-    delta = a - (total_ref[at, :] - kept) / by_delta
-    m_new = outer_momentum * m + delta
-    m_out[frag, 0] = m_new
-    a_out[frag, 0] = a - outer_rate * (delta + outer_momentum * m_new)
-
-
-def outer_call(scalars, total, anchor, momentum):
-    whole = pl.BlockSpec(anchor.shape, lambda t, s: (0, 0, 0, 0))
-    return pl.pallas_call(
-        outer_kernel,
-        grid_spec=pltpu.PrefetchScalarGridSpec(
-            num_scalar_prefetch=1,
-            grid=(1,),
-            in_specs=[pl.BlockSpec(total.shape, lambda t, s: (0, 0)), whole, whole],
-            out_specs=[whole, whole],
-        ),
-        out_shape=[jax.ShapeDtypeStruct(anchor.shape, f32)] * 2,
-        compiler_params=params(1),
-        cost_estimate=cost(100),
-        name="outer_step",
-    )(scalars, total, anchor, momentum)
-
-
-def gain_kernel(places, s_ref, *rest):
-    grads, weights, out_ref = rest[:8], rest[8:16], rest[16]
+def gain_kernel(places, add, s_ref, *rest):
+    count = len(places)
+    grads, weights, rest = rest[:count], rest[count : 2 * count], rest[2 * count :]
+    out_ref = rest[-1]
     rows = grads[0].shape[0]
     ones = jnp.ones((8, KV), bf16)
+
+    @pl.when(pl.program_id(0) == 0)
+    def _():
+        out_ref[...] = rest[0][...] if add else jnp.zeros(out_ref.shape, f32)
+
     for k, (dz, dy) in enumerate(places):
         product = (grads[k][...].astype(f32) * weights[k][...].astype(f32)).astype(bf16)
         sums = lax.dot_general(ones, product, (((1,), (1,)), ((), ())), preferred_element_type=f32)
@@ -489,22 +534,44 @@
         out_ref[:, pl.ds(at, rows)] = sums[:1]
 
 
-def gain_call(places, scalars, g, w):
+def gain_call(places, scalars, g, w, before=None):
     tile = 256
     row = pl.BlockSpec((tile, KV), lambda t, s: (t, 0))
+    whole = pl.BlockSpec((1, HALF), lambda t, s: (0, 0))
+    extra = [] if before is None else [before]
     return pl.pallas_call(
-        functools.partial(gain_kernel, places),
+        functools.partial(gain_kernel, places, before is not None),
         grid_spec=pltpu.PrefetchScalarGridSpec(
             num_scalar_prefetch=1,
             grid=(ROWS // tile,),
-            in_specs=[row] * 16,
-            out_specs=pl.BlockSpec((1, HALF), lambda t, s: (0, 0)),
+            in_specs=[row] * (2 * len(places)) + [whole] * len(extra),
+            out_specs=whole,
         ),
         out_shape=jax.ShapeDtypeStruct((1, HALF), f32),
         compiler_params=params(1),
         cost_estimate=cost(0),
         name="gain_grad",
-    )(scalars, *[g[p] for p in places], *[w[p] for p in places])
+    )(scalars, *[g[p] for p in places], *[w[p] for p in places], *extra)
+
+
+def relay_kernel(a_ref, b_ref, c_ref, d_ref, e_ref, two_ref, three_ref):
+    two_ref[...] = (a_ref[...].astype(f32) + b_ref[...].astype(f32)).astype(bf16)
+    three = c_ref[...].astype(f32) + d_ref[...].astype(f32) + e_ref[...].astype(f32)
+    three_ref[...] = three.astype(bf16)
+
+
+def relay_call(*terms):
+    row = pl.BlockSpec((ROWS // 4, KV), lambda t: (t, 0))
+    return pl.pallas_call(
+        relay_kernel,
+        grid=(4,),
+        in_specs=[row] * 5,
+        out_specs=[row] * 2,
+        out_shape=[jax.ShapeDtypeStruct((ROWS, KV), bf16)] * 2,
+        compiler_params=params(1),
+        cost_estimate=cost(3),
+        name="relay_sums",
+    )(*terms)
 
 
 def after(x, *others):
@@ -537,70 +604,77 @@
 
     total = term_call(lax.axis_size("replica"), scalars, weight, anchor, momentum)
     first_term = total
+    total = total + flip_replica(after(total, w[0, 1]), 1)
+    first_sum = total
     total = total + flip_replica(total, 2)
-    first_sum = total
+    second_sum = total
     total = total + flip_replica(total, 6)
-    second_sum = total
-    total = total + flip_replica(total, 1)
-
-    mine, send, inverse = norm_call(
+
+    mine, *send, inverse = norm_call(
         after(scalars, first_term), hidden, value_cot[0], norm_gain, excluded
     )
-    recv = shift(after(send, first_sum, *near), 0, 0, 1, "swap_x")
+    recv = [shift(v, 0, 0, 1, "swap_x") for v in send]
+    recv_cot = recv.pop()
 
     g = {}
 
     def make(places, waits, estimate):
-        g.update(zip(places, grad_call(places, after(scalars, *waits), mine, recv, estimate)))
-
-    make([(2, 1)], [recv], 3)
-    make([(3, 1), (1, 1), (2, 0)], [g[2, 1], second_sum], 8)
-    make([(3, 0), (0, 1), (1, 0), (0, 0)], [g[2, 0], w[1, 1], w[2, 0]], 10)
-    w[2, 1] = shift(after(w[1, 1], g[2, 1]), -1, 0, 0, "ag_D")
-    w[3, 1] = shift(after(w[0, 1], w[2, 0], g[2, 1]), 1, 0, 0, "ag_C")
-    far = shift(g[2, 1], 0, 1, 0, "rs_D")
-    left = shift(g[3, 1], -1, 0, 0, "rs_C")
+        g.update(zip(places, grad_call(places, after(scalars, *waits), mine, recv, recv_cot, estimate)))
+
+    make([(2, 1), (1, 1), (3, 1), (2, 0), (3, 0), (0, 1), (1, 0), (0, 0)], near, 16)
+    far = shift(after(g[2, 1], first_sum), 0, 1, 0, "rs_D")
     side = shift(g[1, 1], 0, 1, 0, "rs_B")
+    w[2, 1] = shift(after(w[1, 1], g[2, 0]), -1, 0, 0, "ag_D")
+    w[3, 1] = shift(after(w[0, 1], w[2, 0], g[2, 0]), 1, 0, 0, "ag_C")
 
     near_half, far_half = (0, 1), (3, 2)
-    sent0 = half_call(near_half, after(scalars, g[0, 0]), recv, norm_gain, w, "half_near", 10)
+    sent0 = half_call(
+        near_half, after(scalars, g[0, 0]), recv, recv_cot, norm_gain, w, "half_near", 10
+    )
     got0 = [shift(v, 0, 0, 1, "swap_w0") for v in sent0]
-    over = shift(add(g[2, 0], after(far, sent0[0])), 1, 0, 0, "rs_A")
-    sent1 = half_call(far_half, after(scalars, sent0[0], far), recv, norm_gain, w, "half_far", 0)
+    near_order = [(dz, dy) for dz in near_half for dy in range(NY)]
+    far_order = [(dz, dy) for dz in far_half for dy in range(NY)]
+    near_sums = gain_call(near_order, after(scalars, sent0[0]), g, w)
+    left = shift(after(g[3, 1], near_sums), -1, 0, 0, "rs_C")
+    over = shift(add(g[2, 0], after(far, near_sums)), 1, 0, 0, "rs_A")
+    sent1 = half_call(
+        far_half, after(scalars, sent0[0], far), recv, recv_cot, norm_gain, w,
+        "half_far", 0,
+    )
     got1 = [shift(v, 0, 0, 1, "swap_w1") for v in sent1]
 
-    order = [(dz, dy) for dz in range(NZ) for dy in range(NY)]
-    partial = gain_call(order, after(scalars, sent1[0], side), g, w)
+    partial = gain_call(far_order, after(scalars, sent1[0], second_sum), g, w, near_sums)
     left, side, over = (after(v, partial) for v in (left, side, over))
     from_next = shift(after(g[3, 0], left), -1, 0, 0, "rs_zm")
-    from_side = shift(add(g[0, 1], left), 0, 1, 0, "rs_y")
-    from_last = shift(add(g[1, 0], side, over), 1, 0, 0, "rs_zp")
-
-    anchor_out, momentum_out = outer_call(
-        after(scalars, left, side, over), total, anchor, momentum
-    )
+    to_side, to_last = relay_call(g[0, 1], left, g[1, 0], side, over)
+    from_side = shift(to_side, 0, 1, 0, "rs_y")
+    from_last = shift(to_last, 1, 0, 0, "rs_zp")
+
     values_out, hidden_grad = hidden_call(
         (*near_half, *far_half),
-        after(scalars, anchor_out), hidden, mine, norm_gain, inverse,
+        after(scalars, left, side, over), hidden, mine, norm_gain, inverse,
         [*got0[:-1], *got1[:-1], got0[-1], got1[-1]], w,
     )
 
     partial = partial + shift(partial, 0, 1, 0, "gain_y")
     partial = partial + flip_z(partial, 1)
     partial = partial + flip_z(partial, 3)
-    other = shift(partial, 0, 0, 1, "gain_c")
-    even = jnp.where(core == 0, partial, other).reshape(HALF // ROWS, ROWS)
-    odd = jnp.where(core == 0, other, partial).reshape(HALF // ROWS, ROWS)
-    gain_grad = jnp.stack([even, odd], axis=1).reshape(1, D) / norm_gain
-    new_gain = norm_gain - gain_rate * gain_grad
-
-    new_weight = update_call(
+    other = shift(after(partial, hidden_grad), 0, 0, 1, "gain_c")
+    new_weight, anchor_out, momentum_out = update_call(
         inner_rate,
         scalars,
         weight,
         (after(g[0, 0], hidden_grad), from_next, from_side, from_last),
         total,
+        anchor,
+        momentum,
     )
+    other = after(other, new_weight)
+    even = jnp.where(core == 0, partial, other).reshape(HALF // ROWS, ROWS)
+    odd = jnp.where(core == 0, other, partial).reshape(HALF // ROWS, ROWS)
+    gain_grad = jnp.stack([even, odd], axis=1).reshape(1, D) / norm_gain
+    new_gain = norm_gain - gain_rate * gain_grad
+
     return (
         values_out[None],
         hidden_grad[None],

time: 180 us -> 160 us (0.89)
  waiting for transfers between devices: 31.1 us -> 12.2 us
  starting transfers between devices: 34.1 us -> 39.9 us
  local copies, waits for them, and re-layouts: 7.39 us -> 2.34 us
  other arithmetic: 7.48 us -> 5.3 us
    ppermute x23 -> x27, waiting for transfers between devices: 26 us -> 10.4 us  [shift(): return lax.ppermute(x, 'fsdp', pairs)]
    unnamed x32 -> x12, local copies, waits for them, and re-layouts: 6.68 us -> 1.65 us
    ppermute x2, starting transfers between devices: 1.48 us -> 4.77 us  [flip_z(): return lax.ppermute(x, 'fsdp', pairs)]
    ppermute x2, waiting for transfers between devices: 5.07 us -> 1.79 us  [flip_z(): return lax.ppermute(x, 'fsdp', pairs)]
    ppermute x23 -> x27, starting transfers between devices: 26 us -> 28.5 us  [shift(): return lax.ppermute(x, 'fsdp', pairs)]
    convert_element_type x3 -> x1, other arithmetic: 5.16 us -> 2.94 us  [add(): return total.astype(bf16)]
    pallas_call x5 -> x4, Pallas kernels: 33.1 us -> 32 us  [the longest x1 16.9 us: grad_call(): pl.pallas_call(functools.partial(grad_kernel, places), grid_spec=pltpu.Pr...]
  transfers between devices with their start and end apart: 28 -> 32, of which waited for: 9 -> 5; matrix products, arithmetic and copies ran while one was open for 5% -> 3% of each run, Pallas kernels for 52% -> 62%
where the time goes in v2:
time: 160 us; the launch traced here: 159 us
  Pallas kernels  97.9 us (61%)
  starting transfers between devices  39.9 us (25%)
  waiting for transfers between devices  12.2 us (8%)
  other arithmetic  5.3 us (3%)
  local copies, waits for them, and re-layouts  2.34 us (1%)
    ppermute x27, starting transfers between devices, shift(): return lax.ppermute(x, 'fsdp', pairs)  28.5 us
    pallas_call x1, Pallas kernels, hidden_call(): pl.pallas_call(functools.partial(hidden_kernel, depths), grid_spec=pltpu....  25.7 us
    pallas_call x2, Pallas kernels, half_call(): pl.pallas_call(functools.partial(half_kernel, depths), grid_spec=pltpu.Pr...  21.8 us
    pallas_call x1, Pallas kernels, grad_call(): pl.pallas_call(functools.partial(grad_kernel, places), grid_spec=pltpu.Pr...  16.9 us
    pallas_call x2, Pallas kernels, gain_call(): pl.pallas_call(functools.partial(gain_kernel, places, before is not None)...  10.8 us
    pallas_call x1, Pallas kernels, norm_call(): pl.pallas_call(norm_kernel, grid_spec=pltpu.PrefetchScalarGridSpec(num_sc...  10.7 us
    ppermute x27, waiting for transfers between devices, shift(): return lax.ppermute(x, 'fsdp', pairs)  10.4 us
    ppermute x3, starting transfers between devices, flip_replica(): return lax.ppermute(x, 'replica', [(i, i ^ mask) for i in range(8)])  6.61 us
  transfers between devices with their start and end apart: 32, of which 5 were waited for; matrix products, arithmetic and copies ran while one was open for 3% of the time, Pallas kernels for 62%

profile of v2, /device:TPU:1, one launch (start us, length us, event | category | flops | bytes accessed | tf_op | source)
XLA Modules:
  0.0 159.2 jit_solution(16541042622616963162)
XLA Ops:
  0.6 2.5 %collective-permute-start.2 = (bf16[512,1024]{1,0:T(8,128)(2,1)}, bf16[512,1024]{1,0:T(8,128)(2,1)}, u32[]{:S(2)}, u32[]{:S(2)}) collective-permute-start(bf16[512,1024]{1,0:T(8,128)(2,1)} %bitcast.13), channel_id=1, source_target_pairs={{0,4},{1,5},{2,6},{3,7},{4,8},{5,9},{6,10},{7,11},{8,12},{9,13},{1... | collective-permute-start | bytes 3145736 | tf_op jit(solution)/shard_map/ag_zp/ppermute | solution.py:40
  3.2 2.2 %collective-permute-start.1 = (bf16[512,1024]{1,0:T(8,128)(2,1)}, bf16[512,1024]{1,0:T(8,128)(2,1)}, u32[]{:S(2)}, u32[]{:S(2)}) collective-permute-start(bf16[512,1024]{1,0:T(8,128)(2,1)} %bitcast.14), channel_id=1, source_target_pairs={{0,12},{1,13},{2,14},{3,15},{4,0},{5,1},{6,2},{7,3},{8,4},{9,5},{1... | collective-permute-start | bytes 3145736 | tf_op jit(solution)/shard_map/ag_zm/ppermute | solution.py:40
  5.4 1.3 collective-permute-start
  7.9 2.3 %outer_term.1 = f32[512,128]{1,0:T(8,128)} custom-call(s32[6]{0:T(128)} %stack.26.s_ref, bf16[512,1024]{1,0:T(8,128)(2,1)} %bitcast.16, f32[8,1,64,128]{3,2,1,0:T(8,128)} %rest_0_.1, f32[8,1,64,128]{3,2,1,0:T(8,128)} %rest_1_.1), custom_call_target="tpu_custom_call" | custom-call | bytes 3300000 | tf_op jit(solution)/shard_map/outer_term/pallas_call | solution.py:503
  10.3 10.7 %norm.1 = (bf16[512,5120]{1,0:T(8,128)(2,1)}, bf16[512,1024]{1,0:T(8,128)(2,1)}, bf16[512,1024]{1,0:T(8,128)(2,1)}, bf16[512,1024]{1,0:T(8,128)(2,1)}, bf16[512,...) custom-call(s32[6]{0:T(128)} %stack.26.s_ref, bf16[512,8192]{1,0:T(8,128)(2,1)} %bitcast.11, ...), custom_call_target="tpu_custom_call" | custom-call | bytes 26400000 | tf_op jit(solution)/shard_map/norm/pallas_call | solution.py:113
  20.9 1.3 collective-permute-start.3
  22.3 6.2 %collective-permute-done.2.rest_2_.rest_4_.rest_10_ = bf16[512,1024]{1,0:T(8,128)(2,1)} collective-permute-done((bf16[512,1024]{1,0:T(8,128)(2,1)}, bf16[512,1024]{1,0:T(8,128)(2,1)}, u32[]{:S(2)}, u32[]{:S(2)}) %collective-permute-start.2) | collective-permute-done | bytes 1048608 | tf_op jit(solution)/shard_map/ag_zp/ppermute | solution.py:40
  29.7 1.5 collective-permute-start.7
  32.3 1.7 %collective-permute-start.8 = (bf16[512,1024]{1,0:T(8,128)(2,1)}, bf16[512,1024]{1,0:T(8,128)(2,1)}, u32[]{:S(2)}, u32[]{:S(2)}) collective-permute-start(bf16[512,1024]{1,0:T(8,128)(2,1)} %collective-permute-done.rest_3_.rest_5_.rest_7_), channel_id=1, source_target_pairs={{0,12},{1,13},{2,14},{3,15},{4,0},{5,1},{6,2},{7,3},{8,4},{9,5},{1... | collective-permute-start | bytes 3145736 | tf_op jit(solution)/shard_map/ag_B/ppermute | solution.py:40
  34.0 2.9 %collective-permute-start.10 = (f32[512,128]{1,0:T(8,128)S(1)}, f32[512,128]{1,0:T(8,128)S(1)}, u32[]{:S(2)}, u32[]{:S(2)}) collective-permute-start(f32[512,128]{1,0:T(8,128)S(1)} %copy-done.4), channel_id=1, source_target_pairs={{0,16},{16,0},{32,48},{48,32},{64,80},{80,64},{96,112},{112,96},{1... | collective-permute-start | bytes 786440 | tf_op jit(solution)/shard_map/ppermute | solution.py:49
  37.0 16.9 %weight_grad_blocks.1 = (bf16[512,1024]{1,0:T(8,128)(2,1)}, bf16[512,1024]{1,0:T(8,128)(2,1)}, bf16[512,1024]{1,0:T(8,128)(2,1)}, bf16[512,1024]{1,0:T(8,128)(2,...) custom-call(s32[6]{0:T(128)} %stack.26.s_ref, ...), custom_call_target="tpu_custom_call" | custom-call | bytes 52800000 | tf_op jit(solution)/shard_map/weight_grad_blocks/pallas_call | solution.py:186
  55.5 2.0 %collective-permute-done.12.rest_4_.rest_6_.rest_12_ = bf16[512,1024]{1,0:T(8,128)(2,1)} collective-permute-done((bf16[512,1024]{1,0:T(8,128)(2,1)}, bf16[512,1024]{1,0:T(8,128)(2,1)}, u32[]{:S(2)}, u32[]{:S(2)}) %collective-permute-start.12) | collective-permute-done | bytes 1048608 | tf_op jit(solution)/shard_map/ag_A/ppermute | solution.py:40
  57.5 2.7 %collective-permute-start.14 = (bf16[512,1024]{1,0:T(8,128)(2,1)}, bf16[512,1024]{1,0:T(8,128)(2,1)}, u32[]{:S(2)}, u32[]{:S(2)}) collective-permute-start(bf16[512,1024]{1,0:T(8,128)(2,1)} %collective-permute-done.8.rest_5_.rest_7_.rest_9_), channel_id=1, source_target_pairs={{0,12},{1,13},{2,14},{3,15},{4,0},{5,1},{6,2},{7,3},{8,4},{9,5},{1... | collective-permute-start | bytes 3145736 | tf_op jit(solution)/shard_map/ag_D/ppermute | solution.py:40
  60.2 1.3 collective-permute-start.16
  61.5 10.9 %half_near.1 = (bf16[512,1024]{1,0:T(8,128)(2,1)}, bf16[512,1024]{1,0:T(8,128)(2,1)}, bf16[512,1024]{1,0:T(8,128)(2,1)}) custom-call(s32[6]{0:T(128)} %stack.26.s_ref, bf16[512,1024]{1,0:T(8,128)(2,1)} %copy-done.1, f32[1,8192]{1,0:T(1,128)} %gain_ref.7, bf16[512,1024]{1,0:T(8,128)(2,1)} %collective-permute-done.7.rest_5_.rest_7_.rest_0_, ...), custom_call_target="tpu_custom_call" | custom-call | bytes 33000000 | tf_op jit(solution)/shard_map/half_near/pallas_call | solution.py:288
  72.4 5.3 %gain_grad.2.rest_8_ = f32[1,4096]{1,0:T(1,128)} custom-call(s32[6]{0:T(128)} %stack.26.s_ref, bf16[512,1024]{1,0:T(8,128)(2,1)} %get-tuple-element.97.rest_0_.a_ref, bf16[512,1024]{1,0:T(8,128)(2,1)} %get-tuple-element.70.rest_1_.a_ref, bf16[512,1024]{1,0:T(8,128)(2,1)} %get-tuple-element.71.rest_2_.c_ref, bf16[512,1024]{1,0:T(8,128)(2,1)} %get-tuple-element.72.rest_3_, ...), custom_call_target="tpu_custom_call" | custom-call | tf_op jit(solution)/shard_map/gain_grad/pallas_call | solution.py:542
  78.0 3.2 %collective-permute-start.19 = (bf16[512,1024]{1,0:T(8,128)(2,1)}, bf16[512,1024]{1,0:T(8,128)(2,1)}, u32[]{:S(2)}, u32[]{:S(2)}) collective-permute-start(bf16[512,1024]{1,0:T(8,128)(2,1)} %get-tuple-element.91), channel_id=1, source_target_pairs={{0,1},{1,0},{2,3},{3,2},{4,5},{5,4},{6,7},{7,6},{8,9},{9,8},{10,11... | collective-permute-start | bytes 3145736 | tf_op jit(solution)/shard_map/swap_w0/ppermute | solution.py:40
  81.3 2.9 %add_convert_fusion = bf16[512,1024]{1,0:T(8,128)(2,1)} fusion(bf16[512,1024]{1,0:T(8,128)(2,1)} %collective-permute-done.11, bf16[512,1024]{1,0:T(8,128)(2,1)} %get-tuple-element.79.rest_2_), kind=kLoop, calls=%fused_computation | loop fusion | flops 2097152 | bytes 3145728 | tf_op jit(solution)/shard_map/convert_element_type | solution.py:585
  85.2 10.9 %half_far.1 = (bf16[512,1024]{1,0:T(8,128)(2,1)}, bf16[512,1024]{1,0:T(8,128)(2,1)}, bf16[512,1024]{1,0:T(8,128)(2,1)}) custom-call(s32[6]{0:T(128)} %stack.26.s_ref, bf16[512,1024]{1,0:T(8,128)(2,1)} %copy-done.1, f32[1,8192]{1,0:T(1,128)} %gain_ref.7, bf16[512,1024]{1,0:T(8,128)(2,1)} %collective-permute-done.6.rest_2_.rest_4_.rest_0_, ...), custom_call_target="tpu_custom_call" | custom-call | tf_op jit(solution)/shard_map/half_far/pallas_call | solution.py:288
  96.1 5.5 %gain_grad.3 = f32[1,4096]{1,0:T(1,128)} custom-call(s32[6]{0:T(128)} %stack.26.s_ref, bf16[512,1024]{1,0:T(8,128)(2,1)} %get-tuple-element.98.rest_0_, bf16[512,1024]{1,0:T(8,128)(2,1)} %get-tuple-element.73.rest_1_, bf16[512,1024]{1,0:T(8,128)(2,1)} %get-tuple-element.79.rest_2_, bf16[512,1024]{1,0:T(8,128)(2,1)} %get-tuple-element.76.rest_3_, ...), custom_call_target="tpu_custom_call" | custom-call | tf_op jit(solution)/shard_map/gain_grad/pallas_call | solution.py:542
  102.3 2.0 %collective-permute-done.9.b_ref = bf16[512,1024]{1,0:T(8,128)(2,1)} collective-permute-done((bf16[512,1024]{1,0:T(8,128)(2,1)}, bf16[512,1024]{1,0:T(8,128)(2,1)}, u32[]{:S(2)}, u32[]{:S(2)}) %collective-permute-start.9) | collective-permute-done | bytes 1048608 | tf_op jit(solution)/shard_map/rs_C/ppermute | solution.py:40
  104.3 2.1 %collective-permute-start.18 = (bf16[512,1024]{1,0:T(8,128)(2,1)}, bf16[512,1024]{1,0:T(8,128)(2,1)}, u32[]{:S(2)}, u32[]{:S(2)}) collective-permute-start(bf16[512,1024]{1,0:T(8,128)(2,1)} %get-tuple-element.68), channel_id=1, source_target_pairs={{0,1},{1,0},{2,3},{3,2},{4,5},{5,4},{6,7},{7,6},{8,9},{9,8},{10,11... | collective-permute-start | bytes 3145736 | tf_op jit(solution)/shard_map/swap_w0/ppermute | solution.py:40
  107.1 1.3 collective-permute-start.29
  108.4 1.8 %collective-permute-done.29 = f32[1,4096]{1,0:T(1,128)S(1)} collective-permute-done((f32[1,4096]{1,0:T(1,128)S(1)}, f32[1,4096]{1,0:T(1,128)S(1)}, u32[]{:S(2)}, u32[]{:S(2)}) %collective-permute-start.29) | collective-permute-done | bytes 16416 | tf_op jit(solution)/shard_map/ppermute | solution.py:45
  111.5 3.5 %collective-permute-start.30 = (f32[1,4096]{1,0:T(1,128)S(1)}, f32[1,4096]{1,0:T(1,128)S(1)}, u32[]{:S(2)}, u32[]{:S(2)}) collective-permute-start(f32[1,4096]{1,0:T(1,128)S(1)} %add.37), channel_id=1, source_target_pairs={{0,12},{1,13},{2,14},{3,15},{4,8},{5,9},{6,10},{7,11},{8,4},{9,5},... | collective-permute-start | bytes 49160 | tf_op jit(solution)/shard_map/ppermute | solution.py:45
  115.2 4.4 %relay_sums.1 = (bf16[512,1024]{1,0:T(8,128)(2,1)}, bf16[512,1024]{1,0:T(8,128)(2,1)}) custom-call(bf16[512,1024]{1,0:T(8,128)(2,1)} %get-tuple-element.70.rest_1_.a_ref, bf16[512,1024]{1,0:T(8,128)(2,1)} %collective-permute-done.9.b_ref, bf16[512,1024]{1,0:T(8,128)(2,1)} %get-tuple-element.71.rest_2_.c_ref, ...), custom_call_target="tpu_custom_call" | custom-call | bytes 9900000 | tf_op jit(solution)/shard_map/relay_sums/pallas_call | solution.py:565
  119.7 1.4 collective-permute-start.25
  121.1 1.4 collective-permute-start.26
  122.4 2.5 %collective-permute-start.27 = (f32[512,128]{1,0:T(8,128)S(1)}, f32[512,128]{1,0:T(8,128)S(1)}, u32[]{:S(2)}, u32[]{:S(2)}) collective-permute-start(f32[512,128]{1,0:T(8,128)S(1)} %add.33), channel_id=1, source_target_pairs={{0,96},{16,112},{32,64},{48,80},{64,32},{80,48},{96,0},{112,16},{1... | collective-permute-start | bytes 786440 | tf_op jit(solution)/shard_map/ppermute | solution.py:49
  125.0 25.7 %hidden_grad.1 = (bf16[512,1024]{1,0:T(8,128)(2,1)}, bf16[512,8192]{1,0:T(8,128)(2,1)}) custom-call(s32[6]{0:T(128)} %stack.26.s_ref, bf16[512,5120]{1,0:T(8,128)(2,1)} %get-tuple-element.58.x0_ref.c0_ref.x_ref.c_ref, bf16[512,5120]{1,0:T(8,128)(2,1)} %get-tuple-element.58.x0_ref.c0_ref.x_ref.c_ref, f32[1,8192]{1,0:T(1,128)} %gain_ref.7, ...), custom_call_target="tpu_custom_call" | custom-call | bytes 330000000 | tf_op jit(solution)/shard_map/hidden_grad/pallas_call | solution.py:394
  150.7 1.3 collective-permute-start.31
  152.8 5.5 %update.1 = (bf16[512,1024]{1,0:T(8,128)(2,1)}, f32[8,1,64,128]{3,2,1,0:T(8,128)}, f32[8,1,64,128]{3,2,1,0:T(8,128)}) custom-call(s32[6]{0:T(128)} %stack.26.s_ref, bf16[512,1024]{1,0:T(8,128)(2,1)} %bitcast.20, bf16[512,1024]{1,0:T(8,128)(2,1)} %get-tuple-element.97.rest_0_.a_ref, bf16[512,1024]{1,0:T(8,128)(2,1)} %collective-permute-done.24.b_ref, ...), custom_call_target="tpu_custom_call" | custom-call | bytes 9900000 | tf_op jit(solution)/shard_map/update/pallas_call | solution.py:464
  (69 shorter events, 10.7 us)
Async XLA Ops:
  0.6 27.9 %collective-permute-start.2 = (bf16[512,1024]{1,0:T(8,128)(2,1)}, bf16[512,1024]{1,0:T(8,128)(2,1)}, u32[]{:S(2)}, u32[]{:S(2)}) collective-permute-start(bf16[512,1024]{1,0:T(8,128)(2,1)} %bitcast.13), channel_id=1, source_target_pairs={{0,4},{1,5},{2,6},{3,7},{4,8},{5,9},{6,10},{7,11},{8,12},{9,13},{1... | collective-permute-start | bytes 3145736 | tf_op jit(solution)/shard_map/ag_zp/ppermute | solution.py:40
  3.2 26.6 %collective-permute-start.1 = (bf16[512,1024]{1,0:T(8,128)(2,1)}, bf16[512,1024]{1,0:T(8,128)(2,1)}, u32[]{:S(2)}, u32[]{:S(2)}) collective-permute-start(bf16[512,1024]{1,0:T(8,128)(2,1)} %bitcast.14), channel_id=1, source_target_pairs={{0,12},{1,13},{2,14},{3,15},{4,0},{5,1},{6,2},{7,3},{8,4},{9,5},{1... | collective-permute-start | bytes 3145736 | tf_op jit(solution)/shard_map/ag_zm/ppermute | solution.py:40
  5.4 24.4 %collective-permute-start = (bf16[512,1024]{1,0:T(8,128)(2,1)}, bf16[512,1024]{1,0:T(8,128)(2,1)}, u32[]{:S(2)}, u32[]{:S(2)}) collective-permute-start(bf16[512,1024]{1,0:T(8,128)(2,1)} %bitcast.15), channel_id=1, source_target_pairs={{0,2},{1,3},{2,0},{3,1},{4,6},{5,7},{6,4},{7,5},{8,10},{9,11},{10,... | collective-permute-start | bytes 3145736 | tf_op jit(solution)/shard_map/ag_y/ppermute | solution.py:40
  20.9 10.4 %collective-permute-start.3 = (bf16[512,1024]{1,0:T(8,128)(2,1)}, bf16[512,1024]{1,0:T(8,128)(2,1)S(1)}, u32[]{:S(2)}, u32[]{:S(2)}) collective-permute-start(bf16[512,1024]{1,0:T(8,128)(2,1)} %get-tuple-element.59), channel_id=1, source_target_pairs={{0,1},{1,0},{2,3},{3,2},{4,5},{5,4},{6,7},{7,6},{8,9},{9,8},{10,11... | collective-permute-start | bytes 3145736 | tf_op jit(solution)/shard_map/swap_x/ppermute | solution.py:40
  22.2 9.1 %collective-permute-start.4 = (bf16[512,1024]{1,0:T(8,128)(2,1)}, bf16[512,1024]{1,0:T(8,128)(2,1)S(1)}, u32[]{:S(2)}, u32[]{:S(2)}) collective-permute-start(bf16[512,1024]{1,0:T(8,128)(2,1)} %get-tuple-element.60), channel_id=1, source_target_pairs={{0,1},{1,0},{2,3},{3,2},{4,5},{5,4},{6,7},{7,6},{8,9},{9,8},{10,11... | collective-permute-start | bytes 3145736 | tf_op jit(solution)/shard_map/swap_x/ppermute | solution.py:40
  28.5 5.5 %collective-permute-start.5 = (bf16[512,1024]{1,0:T(8,128)(2,1)}, bf16[512,1024]{1,0:T(8,128)(2,1)}, u32[]{:S(2)}, u32[]{:S(2)}) collective-permute-start(bf16[512,1024]{1,0:T(8,128)(2,1)} %get-tuple-element.61), channel_id=1, source_target_pairs={{0,1},{1,0},{2,3},{3,2},{4,5},{5,4},{6,7},{7,6},{8,9},{9,8},{10,11... | collective-permute-start | bytes 3145736 | tf_op jit(solution)/shard_map/swap_x/ppermute | solution.py:40
  29.7 7.2 %collective-permute-start.6 = (bf16[512,1024]{1,0:T(8,128)(2,1)}, bf16[512,1024]{1,0:T(8,128)(2,1)}, u32[]{:S(2)}, u32[]{:S(2)}) collective-permute-start(bf16[512,1024]{1,0:T(8,128)(2,1)} %get-tuple-element.62), channel_id=1, source_target_pairs={{0,1},{1,0},{2,3},{3,2},{4,5},{5,4},{6,7},{7,6},{8,9},{9,8},{10,11... | collective-permute-start | bytes 3145736 | tf_op jit(solution)/shard_map/swap_x/ppermute | solution.py:40
  29.7 7.2 %collective-permute-start.7 = (bf16[512,1024]{1,0:T(8,128)(2,1)}, bf16[512,1024]{1,0:T(8,128)(2,1)}, u32[]{:S(2)}, u32[]{:S(2)}) collective-permute-start(bf16[512,1024]{1,0:T(8,128)(2,1)} %get-tuple-element.63), channel_id=1, source_target_pairs={{0,1},{1,0},{2,3},{3,2},{4,5},{5,4},{6,7},{7,6},{8,9},{9,8},{10,11... | collective-permute-start | bytes 3145736 | tf_op jit(solution)/shard_map/swap_x/ppermute | solution.py:40
  31.3 26.2 %collective-permute-start.12 = (bf16[512,1024]{1,0:T(8,128)(2,1)}, bf16[512,1024]{1,0:T(8,128)(2,1)}, u32[]{:S(2)}, u32[]{:S(2)}) collective-permute-start(bf16[512,1024]{1,0:T(8,128)(2,1)} %collective-permute-done.2.rest_2_.rest_4_.rest_10_), channel_id=1, source_target_pairs={{0,4},{1,5},{2,6},{3,7},{4,8},{5,9},{6,10},{7,11},{8,12},{9,13},{1... | collective-permute-start | bytes 3145736 | tf_op jit(solution)/shard_map/ag_A/ppermute | solution.py:40
  32.3 25.2 %collective-permute-start.8 = (bf16[512,1024]{1,0:T(8,128)(2,1)}, bf16[512,1024]{1,0:T(8,128)(2,1)}, u32[]{:S(2)}, u32[]{:S(2)}) collective-permute-start(bf16[512,1024]{1,0:T(8,128)(2,1)} %collective-permute-done.rest_3_.rest_5_.rest_7_), channel_id=1, source_target_pairs={{0,12},{1,13},{2,14},{3,15},{4,0},{5,1},{6,2},{7,3},{8,4},{9,5},{1... | collective-permute-start | bytes 3145736 | tf_op jit(solution)/shard_map/ag_B/ppermute | solution.py:40
  34.0 19.8 %collective-permute-start.10 = (f32[512,128]{1,0:T(8,128)S(1)}, f32[512,128]{1,0:T(8,128)S(1)}, u32[]{:S(2)}, u32[]{:S(2)}) collective-permute-start(f32[512,128]{1,0:T(8,128)S(1)} %copy-done.4), channel_id=1, source_target_pairs={{0,16},{16,0},{32,48},{48,32},{64,80},{80,64},{96,112},{112,96},{1... | collective-permute-start | bytes 786440 | tf_op jit(solution)/shard_map/ppermute | solution.py:49
  53.9 24.1 %collective-permute-start.11 = (bf16[512,1024]{1,0:T(8,128)(2,1)}, bf16[512,1024]{1,0:T(8,128)(2,1)}, u32[]{:S(2)}, u32[]{:S(2)}) collective-permute-start(bf16[512,1024]{1,0:T(8,128)(2,1)} %get-tuple-element.76.rest_3_), channel_id=1, source_target_pairs={{0,2},{1,3},{2,0},{3,1},{4,6},{5,7},{6,4},{7,5},{8,10},{9,11},{10,... | collective-permute-start | bytes 3145736 | tf_op jit(solution)/shard_map/rs_D/ppermute | solution.py:40
  54.3 23.4 %collective-permute-start.15 = (f32[512,128]{1,0:T(8,128)S(1)}, f32[512,128]{1,0:T(8,128)S(1)}, u32[]{:S(2)}, u32[]{:S(2)}) collective-permute-start(f32[512,128]{1,0:T(8,128)S(1)} %add.32), channel_id=1, source_target_pairs={{0,32},{16,48},{32,0},{48,16},{64,96},{80,112},{96,64},{112,80},{1... | collective-permute-start | bytes 786440 | tf_op jit(solution)/shard_map/ppermute | solution.py:49
  57.5 26.7 %collective-permute-start.13 = (bf16[512,1024]{1,0:T(8,128)(2,1)}, bf16[512,1024]{1,0:T(8,128)(2,1)S(1)}, u32[]{:S(2)}, u32[]{:S(2)}) collective-permute-start(bf16[512,1024]{1,0:T(8,128)(2,1)} %collective-permute-done.rest_3_.rest_5_.rest_7_), channel_id=1, source_target_pairs={{0,4},{1,5},{2,6},{3,7},{4,8},{5,9},{6,10},{7,11},{8,12},{9,13},{1... | collective-permute-start | bytes 3145736 | tf_op jit(solution)/shard_map/ag_C/ppermute | solution.py:40
  57.5 27.0 %collective-permute-start.14 = (bf16[512,1024]{1,0:T(8,128)(2,1)}, bf16[512,1024]{1,0:T(8,128)(2,1)}, u32[]{:S(2)}, u32[]{:S(2)}) collective-permute-start(bf16[512,1024]{1,0:T(8,128)(2,1)} %collective-permute-done.8.rest_5_.rest_7_.rest_9_), channel_id=1, source_target_pairs={{0,12},{1,13},{2,14},{3,15},{4,0},{5,1},{6,2},{7,3},{8,4},{9,5},{1... | collective-permute-start | bytes 3145736 | tf_op jit(solution)/shard_map/ag_D/ppermute | solution.py:40
  60.2 41.4 %collective-permute-start.16 = (bf16[512,1024]{1,0:T(8,128)(2,1)}, bf16[512,1024]{1,0:T(8,128)(2,1)}, u32[]{:S(2)}, u32[]{:S(2)}) collective-permute-start(bf16[512,1024]{1,0:T(8,128)(2,1)} %get-tuple-element.72.rest_3_), channel_id=1, source_target_pairs={{0,2},{1,3},{2,0},{3,1},{4,6},{5,7},{6,4},{7,5},{8,10},{9,11},{10,... | collective-permute-start | bytes 3145736 | tf_op jit(solution)/shard_map/rs_B/ppermute | solution.py:40
  77.7 26.6 %collective-permute-start.9 = (bf16[512,1024]{1,0:T(8,128)(2,1)}, bf16[512,1024]{1,0:T(8,128)(2,1)}, u32[]{:S(2)}, u32[]{:S(2)}) collective-permute-start(bf16[512,1024]{1,0:T(8,128)(2,1)} %get-tuple-element.73.rest_1_), channel_id=1, source_target_pairs={{0,12},{1,13},{2,14},{3,15},{4,0},{5,1},{6,2},{7,3},{8,4},{9,5},{1... | collective-permute-start | bytes 3145736 | tf_op jit(solution)/shard_map/rs_C/ppermute | solution.py:40
  78.0 29.1 %collective-permute-start.19 = (bf16[512,1024]{1,0:T(8,128)(2,1)}, bf16[512,1024]{1,0:T(8,128)(2,1)}, u32[]{:S(2)}, u32[]{:S(2)}) collective-permute-start(bf16[512,1024]{1,0:T(8,128)(2,1)} %get-tuple-element.91), channel_id=1, source_target_pairs={{0,1},{1,0},{2,3},{3,2},{4,5},{5,4},{6,7},{7,6},{8,9},{9,8},{10,11... | collective-permute-start | bytes 3145736 | tf_op jit(solution)/shard_map/swap_w0/ppermute | solution.py:40
  84.2 27.2 %collective-permute-start.22 = (bf16[512,1024]{1,0:T(8,128)(2,1)}, bf16[512,1024]{1,0:T(8,128)(2,1)}, u32[]{:S(2)}, u32[]{:S(2)}) collective-permute-start(bf16[512,1024]{1,0:T(8,128)(2,1)} %get-tuple-element.93), channel_id=1, source_target_pairs={{0,1},{1,0},{2,3},{3,2},{4,5},{5,4},{6,7},{7,6},{8,9},{9,8},{10,11... | collective-permute-start | bytes 3145736 | tf_op jit(solution)/shard_map/swap_w0/ppermute | solution.py:40
  84.5 30.4 %collective-permute-start.17 = (bf16[512,1024]{1,0:T(8,128)(2,1)}, bf16[512,1024]{1,0:T(8,128)(2,1)}, u32[]{:S(2)}, u32[]{:S(2)}) collective-permute-start(bf16[512,1024]{1,0:T(8,128)(2,1)} %add_convert_fusion), channel_id=1, source_target_pairs={{0,4},{1,5},{2,6},{3,7},{4,8},{5,9},{6,10},{7,11},{8,12},{9,13},{1... | collective-permute-start | bytes 3145736 | tf_op jit(solution)/shard_map/rs_A/ppermute | solution.py:40
  101.6 4.7 %collective-permute-start.28 = (f32[1,4096]{1,0:T(1,128)}, f32[1,4096]{1,0:T(1,128)S(1)}, u32[]{:S(2)}, u32[]{:S(2)}) collective-permute-start(f32[1,4096]{1,0:T(1,128)} %gain_grad.3), channel_id=1, source_target_pairs={{0,2},{1,3},{2,0},{3,1},{4,6},{5,7},{6,4},{7,5},{8,10},{9,11},{10,... | collective-permute-start | bytes 49160 | tf_op jit(solution)/shard_map/gain_y/ppermute | solution.py:40
  104.3 15.3 %collective-permute-start.18 = (bf16[512,1024]{1,0:T(8,128)(2,1)}, bf16[512,1024]{1,0:T(8,128)(2,1)}, u32[]{:S(2)}, u32[]{:S(2)}) collective-permute-start(bf16[512,1024]{1,0:T(8,128)(2,1)} %get-tuple-element.68), channel_id=1, source_target_pairs={{0,1},{1,0},{2,3},{3,2},{4,5},{5,4},{6,7},{7,6},{8,9},{9,8},{10,11... | collective-permute-start | bytes 3145736 | tf_op jit(solution)/shard_map/swap_w0/ppermute | solution.py:40
  106.3 14.7 %collective-permute-start.21 = (bf16[512,1024]{1,0:T(8,128)(2,1)}, bf16[512,1024]{1,0:T(8,128)(2,1)}, u32[]{:S(2)}, u32[]{:S(2)}) collective-permute-start(bf16[512,1024]{1,0:T(8,128)(2,1)} %get-tuple-element.92), channel_id=1, source_target_pairs={{0,1},{1,0},{2,3},{3,2},{4,5},{5,4},{6,7},{7,6},{8,9},{9,8},{10,11... | collective-permute-start | bytes 3145736 | tf_op jit(solution)/shard_map/swap_w1/ppermute | solution.py:40
  107.1 3.1 %collective-permute-start.29 = (f32[1,4096]{1,0:T(1,128)S(1)}, f32[1,4096]{1,0:T(1,128)S(1)}, u32[]{:S(2)}, u32[]{:S(2)}) collective-permute-start(f32[1,4096]{1,0:T(1,128)S(1)} %add.36), channel_id=1, source_target_pairs={{0,4},{1,5},{2,6},{3,7},{4,0},{5,1},{6,2},{7,3},{8,12},{9,13},{10,... | collective-permute-start | bytes 49160 | tf_op jit(solution)/shard_map/ppermute | solution.py:45
  110.2 12.3 %collective-permute-start.23 = (bf16[512,1024]{1,0:T(8,128)(2,1)}, bf16[512,1024]{1,0:T(8,128)(2,1)}, u32[]{:S(2)}, u32[]{:S(2)}) collective-permute-start(bf16[512,1024]{1,0:T(8,128)(2,1)} %get-tuple-element.94), channel_id=1, source_target_pairs={{0,1},{1,0},{2,3},{3,2},{4,5},{5,4},{6,7},{7,6},{8,9},{9,8},{10,11... | collective-permute-start | bytes 3145736 | tf_op jit(solution)/shard_map/swap_w1/ppermute | solution.py:40
  111.5 8.2 %collective-permute-start.30 = (f32[1,4096]{1,0:T(1,128)S(1)}, f32[1,4096]{1,0:T(1,128)S(1)}, u32[]{:S(2)}, u32[]{:S(2)}) collective-permute-start(f32[1,4096]{1,0:T(1,128)S(1)} %add.37), channel_id=1, source_target_pairs={{0,12},{1,13},{2,14},{3,15},{4,8},{5,9},{6,10},{7,11},{8,4},{9,5},... | collective-permute-start | bytes 49160 | tf_op jit(solution)/shard_map/ppermute | solution.py:45
  115.0 10.0 %collective-permute-start.20 = (bf16[512,1024]{1,0:T(8,128)(2,1)}, bf16[512,1024]{1,0:T(8,128)(2,1)}, u32[]{:S(2)}, u32[]{:S(2)}) collective-permute-start(bf16[512,1024]{1,0:T(8,128)(2,1)} %get-tuple-element.82), channel_id=1, source_target_pairs={{0,1},{1,0},{2,3},{3,2},{4,5},{5,4},{6,7},{7,6},{8,9},{9,8},{10,11... | collective-permute-start | bytes 3145736 | tf_op jit(solution)/shard_map/swap_w1/ppermute | solution.py:40
  119.6 33.2 %collective-permute-start.24 = (bf16[512,1024]{1,0:T(8,128)(2,1)S(1)}, bf16[512,1024]{1,0:T(8,128)(2,1)}, u32[]{:S(2)}, u32[]{:S(2)}) collective-permute-start(bf16[512,1024]{1,0:T(8,128)(2,1)S(1)} %copy-done.3), channel_id=1, source_target_pairs={{0,12},{1,13},{2,14},{3,15},{4,0},{5,1},{6,2},{7,3},{8,4},{9,5},{1... | collective-permute-start | bytes 3145736 | tf_op jit(solution)/shard_map/rs_zm/ppermute | solution.py:40
  119.7 33.1 %collective-permute-start.25 = (bf16[512,1024]{1,0:T(8,128)(2,1)}, bf16[512,1024]{1,0:T(8,128)(2,1)}, u32[]{:S(2)}, u32[]{:S(2)}) collective-permute-start(bf16[512,1024]{1,0:T(8,128)(2,1)} %get-tuple-element.99), channel_id=1, source_target_pairs={{0,2},{1,3},{2,0},{3,1},{4,6},{5,7},{6,4},{7,5},{8,10},{9,11},{10,... | collective-permute-start | bytes 3145736 | tf_op jit(solution)/shard_map/rs_y/ppermute | solution.py:40
  121.1 31.7 %collective-permute-start.26 = (bf16[512,1024]{1,0:T(8,128)(2,1)}, bf16[512,1024]{1,0:T(8,128)(2,1)}, u32[]{:S(2)}, u32[]{:S(2)}) collective-permute-start(bf16[512,1024]{1,0:T(8,128)(2,1)} %get-tuple-element.100), channel_id=1, source_target_pairs={{0,4},{1,5},{2,6},{3,7},{4,8},{5,9},{6,10},{7,11},{8,12},{9,13},{1... | collective-permute-start | bytes 3145736 | tf_op jit(solution)/shard_map/rs_zp/ppermute | solution.py:40
  122.4 29.6 %collective-permute-start.27 = (f32[512,128]{1,0:T(8,128)S(1)}, f32[512,128]{1,0:T(8,128)S(1)}, u32[]{:S(2)}, u32[]{:S(2)}) collective-permute-start(f32[512,128]{1,0:T(8,128)S(1)} %add.33), channel_id=1, source_target_pairs={{0,96},{16,112},{32,64},{48,80},{64,32},{80,48},{96,0},{112,16},{1... | collective-permute-start | bytes 786440 | tf_op jit(solution)/shard_map/ppermute | solution.py:49
  150.7 7.6 %collective-permute-start.31 = (f32[1,4096]{1,0:T(1,128)S(1)}, f32[1,4096]{1,0:T(1,128)S(1)}, u32[]{:S(2)}, u32[]{:S(2)}) collective-permute-start(f32[1,4096]{1,0:T(1,128)S(1)} %add.38), channel_id=1, source_target_pairs={{0,1},{1,0},{2,3},{3,2},{4,5},{5,4},{6,7},{7,6},{8,9},{9,8},{10,11... | collective-permute-start | bytes 49160 | tf_op jit(solution)/shard_map/gain_c/ppermute | solution.py:40
  (6 other events, 61.8 us)

commit v3 on v2

--- a/solution.py
+++ b/solution.py
@@ -221,46 +221,54 @@
     return copies
 
 
-def half_kernel(depths, s_ref, c_ref, gain_ref, *rest):
+def half_kernel(depths, s_ref, gain_ref, *rest):
     count = len(depths)
-    xs, weights, rest = rest[:count], rest[count : 3 * count], rest[3 * count :]
-    outs, (x, x_sems, held, sems, values, made, out_sems) = rest[: count + 1], rest[count + 1 :]
+    cots, xs, mine_ref, rest = rest[:2], rest[2 : 2 + count], rest[2 + count], rest[3 + count :]
+    weights, outs = rest[: NY * count], rest[NY * count : NY * count + 2 * (count + 1)]
+    x, cot, held, values, made, in_sems, sems, out_sems = rest[NY * count + 2 * (count + 1) :]
     step = pl.program_id(0)
-    loads = [pltpu.make_async_copy(ref, x.at[k], x_sems.at[k]) for k, ref in enumerate(xs)]
     copies = weight_copies(depths, s_ref, weights, held, sems)
-    back = [
-        pltpu.make_async_copy(made.at[k % 2], outs[k], out_sems.at[k % 2]) for k in range(count + 1)
-    ]
+    loads = []
+    for k, ref in enumerate(xs):
+        at = pl.multiple_of(lax.rem(s_ref[Z] + depths[k], NZ) * PAIR, PAIR)
+        own = mine_ref.at[:, pl.ds(at, PAIR)]
+        for n, source in enumerate((ref, own)):
+            to = x.at[k, n * ROWS : (n + 1) * ROWS]
+            loads.append(pltpu.make_async_copy(source, to, in_sems.at[2 * k + n]))
+    for n, ref in enumerate(cots):
+        to = cot.at[n * ROWS : (n + 1) * ROWS]
+        loads.append(pltpu.make_async_copy(ref, to, in_sems.at[2 * count + n]))
+    back = []
+    for k in range(count + 1):
+        for n in range(2):
+            source = made.at[k % 2, n * ROWS : (n + 1) * ROWS]
+            back.append(
+                pltpu.make_async_copy(source, outs[n * (count + 1) + k], out_sems.at[k % 2, n])
+            )
 
     @pl.when(step == 0)
     def _():
         for k in range(count):
-            loads[k].start()
-            copies[NY * k].start()
-            copies[NY * k + 1].start()
+            for copy in (*loads[2 * k : 2 * k + 2], *copies[NY * k : NY * k + NY]):
+                copy.start()
+            if k == 0:
+                for copy in loads[2 * count :]:
+                    copy.start()
+        for copy in loads[2 * count :]:
+            copy.wait()
 
     for k in range(count):
 
         @pl.when(step == k)
         def _(k=k):
-            loads[k].wait()
-            copies[NY * k].wait()
-            copies[NY * k + 1].wait()
+            for copy in (*loads[2 * k : 2 * k + 2], *copies[NY * k : NY * k + NY]):
+                copy.wait()
             if k >= 2:
-                back[k - 2].wait()
+                back[2 * k - 4].wait()
+                back[2 * k - 3].wait()
 
     w = held[step]
-    part = jnp.dot(x[step], w, preferred_element_type=f32)
-
-    @pl.when(step == 0)
-    def _():
-        values[...] = part
-
-    @pl.when(step > 0)
-    def _():
-        values[...] += part
-
-    grad = lax.dot_general(c_ref[...], w, (((1,), (1,)), ((), ())), preferred_element_type=f32)
+    grad = lax.dot_general(cot[...], w, (((1,), (1,)), ((), ())), preferred_element_type=f32)
     first = lax.rem(s_ref[Z] + pick(step, depths), NZ) * NY
     slot = lax.rem(step, 2)
     for k in range(NY):
@@ -272,153 +280,101 @@
 
         @pl.when(step == k)
         def _(k=k):
-            back[k].start()
-            if k == count - 1:
-                if count >= 2:
-                    back[count - 2].wait()
-                made[count % 2] = values[...].astype(bf16)
-                back[count].start()
-                back[count - 1].wait()
-                back[count].wait()
-
-
-def half_call(depths, scalars, x, cot, gain, w, name, estimate):
+            back[2 * k].start()
+            back[2 * k + 1].start()
+
+    part = jnp.dot(x[step], w, preferred_element_type=f32)
+
+    @pl.when(step == 0)
+    def _():
+        values[...] = part
+
+    @pl.when((step > 0) & (step < count - 1))
+    def _():
+        values[...] += part
+
+    @pl.when(step == count - 1)
+    def _():
+        if count >= 2:
+            back[2 * count - 4].wait()
+            back[2 * count - 3].wait()
+        made[count % 2] = (values[...] + part).astype(bf16)
+        for copy in back[2 * count :]:
+            copy.start()
+        for copy in back[2 * count - 2 :]:
+            copy.wait()
+
+
+def half_call(depths, scalars, x, mine, cots, gain, w, name):
     count = len(depths)
     weights = [w[dz, dy] for dz in depths for dy in range(NY)]
-    return pl.pallas_call(
+    made = pl.pallas_call(
         functools.partial(half_kernel, depths),
         grid_spec=pltpu.PrefetchScalarGridSpec(
             num_scalar_prefetch=1,
             grid=(count,),
-            in_specs=[
-                pl.BlockSpec((ROWS, KV), lambda t, s: (0, 0)),
-                pl.BlockSpec((1, D), lambda t, s: (0, 0)),
-            ]
-            + [pl.BlockSpec(memory_space=pltpu.HBM)] * (count + len(weights)),
-            out_specs=[pl.BlockSpec(memory_space=pltpu.HBM)] * (count + 1),
+            in_specs=[pl.BlockSpec((1, D), lambda t, s: (0, 0))]
+            + [pl.BlockSpec(memory_space=pltpu.HBM)] * (3 + count + len(weights)),
+            out_specs=[pl.BlockSpec(memory_space=pltpu.HBM)] * (2 * (count + 1)),
             scratch_shapes=[
-                pltpu.VMEM((count, ROWS, PAIR), bf16),
-                pltpu.SemaphoreType.DMA((count,)),
+                pltpu.VMEM((count, 2 * ROWS, PAIR), bf16),
+                pltpu.VMEM((2 * ROWS, KV), bf16),
                 pltpu.VMEM((count, PAIR, KV), bf16),
+                pltpu.VMEM((2 * ROWS, KV), f32),
+                pltpu.VMEM((2, 2 * ROWS, PAIR), bf16),
+                pltpu.SemaphoreType.DMA((2 * count + 2,)),
                 pltpu.SemaphoreType.DMA((NY * count,)),
-                pltpu.VMEM((ROWS, KV), f32),
-                pltpu.VMEM((2, ROWS, PAIR), bf16),
-                pltpu.SemaphoreType.DMA((2,)),
+                pltpu.SemaphoreType.DMA((2, 2)),
             ],
         ),
-        out_shape=[jax.ShapeDtypeStruct((ROWS, PAIR), bf16)] * (count + 1),
-        compiler_params=params(1),
-        cost_estimate=cost(estimate),
+        out_shape=[jax.ShapeDtypeStruct((ROWS, PAIR), bf16)] * (2 * (count + 1)),
+        compiler_params=params(1),
+        cost_estimate=cost(10),
         name=name,
-    )(scalars, cot, gain, *[x[dz] for dz in depths], *weights)
-
-
-def hidden_kernel(depths, s_ref, x_ref, c_ref, gain_ref, inv_ref, h_ref, *rest):
-    step, count = pl.program_id(0), len(depths)
-    gots, weights, rest = rest[: count + 2], rest[count + 2 : 3 * count + 2], rest[3 * count + 2 :]
-    values_ref, out_ref, held, sems, values, mean, got, got_sems = rest
-    received = [
-        pltpu.make_async_copy(ref, got.at[k], got_sems.at[k]) for k, ref in enumerate(gots)
-    ]
-    copies = weight_copies(depths, s_ref, weights, held, sems)
-
-    @pl.when(step == 0)
-    def _():
-        for copy in copies:
-            copy.start()
-        for copy in (*received[count:], *received[:count]):
-            copy.start()
-
-    for k in range(count):
-
-        @pl.when(step == k)
-        def _(k=k):
-            copies[NY * k].wait()
-            copies[NY * k + 1].wait()
-
-        @pl.when(step == count + k)
-        def _(k=k):
-            received[k].wait()
-
-    @pl.when(step < count)
-    def _():
-        part = jnp.dot(x_ref[...], held[step], preferred_element_type=f32)
-
-        @pl.when(step == 0)
-        def _():
-            values[...] = part
-
-        @pl.when(step > 0)
-        def _():
-            values[...] += part
-
-    @pl.when(step == count)
-    def _():
-        for k in (count, count + 1):
-            received[k].wait()
-            values[...] += got[k].astype(f32)
-        values_ref[...] = values[...].astype(bf16)
-        dots = jnp.sum(values[...] * c_ref[...].astype(f32), axis=1, keepdims=True) / D
-        mean[...] = jnp.broadcast_to(dots, mean.shape) * inv_ref[...]
-
-    def finish(weighted, at):
-        for n in range(ROWS // 128):
-            cols = pl.ds(at + n * 128, 128)
-            v = lanes(weighted, n) - h_ref[:, cols].astype(f32) * mean[...]
-            out_ref[:, cols] = (v * inv_ref[...]).astype(bf16)
-
-    @pl.when(step >= count)
-    def _():
-        core = s_ref[CORE]
-        k = step - count
-        first = 2 * PAIR * lax.rem(s_ref[Z] + pick(k, depths), NZ)
+    )(scalars, gain, *cots, *[x[dz] for dz in depths], mine, *weights)
+    return made[: count + 1], made[count + 1 :]
+
+
+def hidden_kernel(depths, s_ref, x_ref, c_ref, inv_ref, *rest):
+    count = len(depths)
+    owns, gots, tails = rest[:count], rest[count : 2 * count], rest[2 * count : -2]
+    values_ref, out_ref = rest[-2:]
+    core = s_ref[CORE]
+    values = tails[0][...].astype(f32)
+    for tail in tails[1:]:
+        values = values + tail[...].astype(f32)
+    values_ref[...] = values.astype(bf16)
+    mean = jnp.sum(values * c_ref[...].astype(f32), axis=1, keepdims=True) / D
+    inverse = inv_ref[...]
+    mean = jnp.broadcast_to(mean, inverse.shape) * inverse
+    for dz, own_ref, got_ref in zip(depths, owns, gots):
+        first = lax.rem(s_ref[Z] + dz, NZ) * NY
         for y in range(NY):
-            cols = slice(y * ROWS, (y + 1) * ROWS)
-            at = pl.multiple_of((2 * y + core) * ROWS, ROWS)
-            gain = gain_ref[:, pl.ds(pl.multiple_of(first + at, ROWS), ROWS)]
-            grad = lax.dot_general(
-                c_ref[...], held[k, cols], (((1,), (1,)), ((), ())), preferred_element_type=f32
-            )
-            finish(grad * gain, at)
-            at = pl.multiple_of((2 * y + 1 - core) * ROWS, ROWS)
-            finish(got[k, :, cols].astype(f32), at)
-
-
-def hidden_call(depths, scalars, hidden, mine, gain, inverse, gots, w):
-    count = len(depths)
-    weights = [w[dz, dy] for dz in depths for dy in range(NY)]
-
-    def place(t, s):
-        return pair_of(s, jnp.maximum(t - count, 0), depths)
-
+            for parity, w_ref in ((core, own_ref), (1 - core, got_ref)):
+                at = pl.multiple_of((2 * (first + y) + parity) * ROWS, ROWS)
+                x = x_ref[:, pl.ds(at, ROWS)].astype(f32)
+                w = w_ref[:, y * ROWS : (y + 1) * ROWS].astype(f32)
+                for n in range(ROWS // 128):
+                    v = (lanes(w, n) - lanes(x, n) * mean) * inverse
+                    out_ref[:, pl.ds(at + n * 128, 128)] = v.astype(bf16)
+
+
+def hidden_call(depths, scalars, hidden, cot, inverse, owns, gots, tails):
+    tile = 128
+    wide = pl.BlockSpec((tile, D), lambda t, s: (t, 0))
+    row = pl.BlockSpec((tile, KV), lambda t, s: (t, 0))
     return pl.pallas_call(
         functools.partial(hidden_kernel, depths),
         grid_spec=pltpu.PrefetchScalarGridSpec(
             num_scalar_prefetch=1,
-            grid=(2 * count,),
+            grid=(ROWS // tile,),
             in_specs=[
-                pl.BlockSpec(
-                    (ROWS, PAIR), lambda t, s: (0, pair_of(s, jnp.minimum(t, count - 1), depths))
-                ),
-                pl.BlockSpec((ROWS, KV), lambda t, s: (0, HALF // KV)),
-                pl.BlockSpec((1, D), lambda t, s: (0, 0)),
-                pl.BlockSpec((ROWS, 128), lambda t, s: (0, 0)),
-                pl.BlockSpec((ROWS, 2 * PAIR), lambda t, s: (0, place(t, s))),
-            ]
-            + [pl.BlockSpec(memory_space=pltpu.HBM)] * len(gots)
-            + [pl.BlockSpec(memory_space=pltpu.HBM)] * len(weights),
-            out_specs=[
-                pl.BlockSpec((ROWS, KV), lambda t, s: (0, 0)),
-                pl.BlockSpec((ROWS, 2 * PAIR), lambda t, s: (0, place(t, s))),
+                wide,
+                row,
+                pl.BlockSpec((tile, 128), lambda t, s: (t, 0)),
+                *[row] * (2 * len(depths) + len(tails)),
             ],
-            scratch_shapes=[
-                pltpu.VMEM((count, PAIR, KV), bf16),
-                pltpu.SemaphoreType.DMA((NY * count,)),
-                pltpu.VMEM((ROWS, KV), f32),
-                pltpu.VMEM((ROWS, 128), f32),
-                pltpu.VMEM((count + 2, ROWS, PAIR), bf16),
-                pltpu.SemaphoreType.DMA((count + 2,)),
-            ],
+            out_specs=[row, wide],
         ),
         out_shape=[
             jax.ShapeDtypeStruct((ROWS, KV), bf16),
@@ -427,7 +383,7 @@
         compiler_params=params(1),
         cost_estimate=cost(100),
         name="hidden_grad",
-    )(scalars, mine, mine, gain, inverse, hidden, *gots, *weights)
+    )(scalars, hidden, cot, inverse, *owns, *gots, *tails)
 
 
 def update_kernel(rate, s_ref, w_ref, a_ref, b_ref, c_ref, d_ref, total_ref, *rest):
@@ -613,6 +569,7 @@
     mine, *send, inverse = norm_call(
         after(scalars, first_term), hidden, value_cot[0], norm_gain, excluded
     )
+    masked = send[-1]
     recv = [shift(v, 0, 0, 1, "swap_x") for v in send]
     recv_cot = recv.pop()
 
@@ -623,23 +580,23 @@
 
     make([(2, 1), (1, 1), (3, 1), (2, 0), (3, 0), (0, 1), (1, 0), (0, 0)], near, 16)
     far = shift(after(g[2, 1], first_sum), 0, 1, 0, "rs_D")
-    side = shift(g[1, 1], 0, 1, 0, "rs_B")
     w[2, 1] = shift(after(w[1, 1], g[2, 0]), -1, 0, 0, "ag_D")
     w[3, 1] = shift(after(w[0, 1], w[2, 0], g[2, 0]), 1, 0, 0, "ag_C")
 
     near_half, far_half = (0, 1), (3, 2)
-    sent0 = half_call(
-        near_half, after(scalars, g[0, 0]), recv, recv_cot, norm_gain, w, "half_near", 10
+    cots = (recv_cot, masked)
+    sent0, own0 = half_call(
+        near_half, after(scalars, g[0, 0]), recv, mine, cots, norm_gain, w, "half_near"
     )
     got0 = [shift(v, 0, 0, 1, "swap_w0") for v in sent0]
     near_order = [(dz, dy) for dz in near_half for dy in range(NY)]
     far_order = [(dz, dy) for dz in far_half for dy in range(NY)]
     near_sums = gain_call(near_order, after(scalars, sent0[0]), g, w)
-    left = shift(after(g[3, 1], near_sums), -1, 0, 0, "rs_C")
+    side = shift(after(g[1, 1], sent0[0]), 0, 1, 0, "rs_B")
+    left = shift(after(g[3, 1], near_sums, w[2, 1]), -1, 0, 0, "rs_C")
     over = shift(add(g[2, 0], after(far, near_sums)), 1, 0, 0, "rs_A")
-    sent1 = half_call(
-        far_half, after(scalars, sent0[0], far), recv, recv_cot, norm_gain, w,
-        "half_far", 0,
+    sent1, own1 = half_call(
+        far_half, after(scalars, sent0[0], far), recv, mine, cots, norm_gain, w, "half_far"
     )
     got1 = [shift(v, 0, 0, 1, "swap_w1") for v in sent1]
 
@@ -651,9 +608,9 @@
     from_last = shift(to_last, 1, 0, 0, "rs_zp")
 
     values_out, hidden_grad = hidden_call(
-        (*near_half, *far_half),
-        after(scalars, left, side, over), hidden, mine, norm_gain, inverse,
-        [*got0[:-1], *got1[:-1], got0[-1], got1[-1]], w,
+        (*near_half, *far_half), after(scalars, left, side, over), hidden, masked, inverse,
+        (*own0[:-1], *own1[:-1]), (*got0[:-1], *got1[:-1]),
+        (own0[-1], own1[-1], got0[-1], got1[-1]),
     )
 
     partial = partial + shift(partial, 0, 1, 0, "gain_y")

time: 160 us -> 161 us (level)
  waiting for transfers between devices: 12.2 us -> 19.5 us
  Pallas kernels: 97.9 us -> 94.4 us
  starting transfers between devices: 39.9 us -> 37.1 us
    pallas_call x1, Pallas kernels: 25.7 us -> 13.2 us  [hidden_call(): pl.pallas_call(functools.partial(hidden_kernel, depths), grid_spec=pltpu....]
    pallas_call x2, Pallas kernels: 21.8 us -> 30.9 us  [half_call(): pl.pallas_call(functools.partial(half_kernel, depths), grid_spec=pltpu.Pr...]
    ppermute x27, waiting for transfers between devices: 10.4 us -> 16.9 us  [shift(): return lax.ppermute(x, 'fsdp', pairs)]
    ppermute x2, starting transfers between devices: 4.77 us -> 1.61 us  [flip_z(): return lax.ppermute(x, 'fsdp', pairs)]
  transfers between devices with their start and end apart: 32 -> 32, of which waited for: 5 -> 11; matrix products, arithmetic and copies ran while one was open for 3% -> 3% of each run, Pallas kernels for 62% -> 59%
where the time goes in v3:
time: 161 us; the launch traced here: 159 us
  Pallas kernels  94.4 us (59%)
  starting transfers between devices  37.1 us (23%)
  waiting for transfers between devices  19.5 us (12%)
  other arithmetic  4.95 us (3%)
    pallas_call x2, Pallas kernels, half_call(): pl.pallas_call(functools.partial(half_kernel, depths), grid_spec=pltpu.Pr...  30.9 us
    ppermute x27, starting transfers between devices, shift(): return lax.ppermute(x, 'fsdp', pairs)  29.1 us
    ppermute x27, waiting for transfers between devices, shift(): return lax.ppermute(x, 'fsdp', pairs)  16.9 us
    pallas_call x1, Pallas kernels, grad_call(): pl.pallas_call(functools.partial(grad_kernel, places), grid_spec=pltpu.Pr...  16.8 us
    pallas_call x1, Pallas kernels, hidden_call(): pl.pallas_call(functools.partial(hidden_kernel, depths), grid_spec=pltpu....  13.2 us
    pallas_call x2, Pallas kernels, gain_call(): pl.pallas_call(functools.partial(gain_kernel, places, before is not None)...  10.8 us
    pallas_call x1, Pallas kernels, norm_call(): pl.pallas_call(norm_kernel, grid_spec=pltpu.PrefetchScalarGridSpec(num_sc...  10.6 us
    ppermute x3, starting transfers between devices, flip_replica(): return lax.ppermute(x, 'replica', [(i, i ^ mask) for i in range(8)])  6.4 us
  transfers between devices with their start and end apart: 32, of which 11 were waited for; matrix products, arithmetic and copies ran while one was open for 3% of the time, Pallas kernels for 59%

profile of v3, /device:TPU:1, one launch (start us, length us, event | category | flops | bytes accessed | tf_op | source)
XLA Modules:
  0.0 159.1 jit_solution(14801010572804062753)
XLA Ops:
  0.6 2.2 %collective-permute-start = (bf16[512,1024]{1,0:T(8,128)(2,1)}, bf16[512,1024]{1,0:T(8,128)(2,1)}, u32[]{:S(2)}, u32[]{:S(2)}) collective-permute-start(bf16[512,1024]{1,0:T(8,128)(2,1)} %bitcast.13), channel_id=1, source_target_pairs={{0,2},{1,3},{2,0},{3,1},{4,6},{5,7},{6,4},{7,5},{8,10},{9,11},{10,... | collective-permute-start | bytes 3145736 | tf_op jit(solution)/shard_map/ag_y/ppermute | solution.py:40
  2.8 3.8 %collective-permute-start.1 = (bf16[512,1024]{1,0:T(8,128)(2,1)}, bf16[512,1024]{1,0:T(8,128)(2,1)}, u32[]{:S(2)}, u32[]{:S(2)}) collective-permute-start(bf16[512,1024]{1,0:T(8,128)(2,1)} %bitcast.14), channel_id=1, source_target_pairs={{0,12},{1,13},{2,14},{3,15},{4,0},{5,1},{6,2},{7,3},{8,4},{9,5},{1... | collective-permute-start | bytes 3145736 | tf_op jit(solution)/shard_map/ag_zm/ppermute | solution.py:40
  7.9 2.3 %outer_term.1 = f32[512,128]{1,0:T(8,128)} custom-call(s32[6]{0:T(128)} %stack.26.s_ref, bf16[512,1024]{1,0:T(8,128)(2,1)} %bitcast.16, f32[8,1,64,128]{3,2,1,0:T(8,128)} %rest_0_.1, f32[8,1,64,128]{3,2,1,0:T(8,128)} %rest_1_.1), custom_call_target="tpu_custom_call" | custom-call | bytes 3300000 | tf_op jit(solution)/shard_map/outer_term/pallas_call | solution.py:459
  10.2 10.6 %norm.1 = (bf16[512,5120]{1,0:T(8,128)(2,1)}, bf16[512,1024]{1,0:T(8,128)(2,1)}, bf16[512,1024]{1,0:T(8,128)(2,1)}, bf16[512,1024]{1,0:T(8,128)(2,1)}, bf16[512,...) custom-call(s32[6]{0:T(128)} %stack.26.s_ref, bf16[512,8192]{1,0:T(8,128)(2,1)} %bitcast.11, ...), custom_call_target="tpu_custom_call" | custom-call | bytes 26400000 | tf_op jit(solution)/shard_map/norm/pallas_call | solution.py:113
  20.8 1.3 collective-permute-start.3
  22.2 3.4 %collective-permute-done.rest_6_.rest_5_ = bf16[512,1024]{1,0:T(8,128)(2,1)} collective-permute-done((bf16[512,1024]{1,0:T(8,128)(2,1)}, bf16[512,1024]{1,0:T(8,128)(2,1)}, u32[]{:S(2)}, u32[]{:S(2)}) %collective-permute-start) | collective-permute-done | bytes 1048608 | tf_op jit(solution)/shard_map/ag_y/ppermute | solution.py:40
  25.6 1.6 %collective-permute-start.5 = (bf16[512,1024]{1,0:T(8,128)(2,1)}, bf16[512,1024]{1,0:T(8,128)(2,1)}, u32[]{:S(2)}, u32[]{:S(2)}) collective-permute-start(bf16[512,1024]{1,0:T(8,128)(2,1)} %get-tuple-element.68), channel_id=1, source_target_pairs={{0,1},{1,0},{2,3},{3,2},{4,5},{5,4},{6,7},{7,6},{8,9},{9,8},{10,11... | collective-permute-start | bytes 3145736 | tf_op jit(solution)/shard_map/swap_x/ppermute | solution.py:40
  28.4 1.9 %collective-permute-start.6 = (bf16[512,1024]{1,0:T(8,128)(2,1)}, bf16[512,1024]{1,0:T(8,128)(2,1)}, u32[]{:S(2)}, u32[]{:S(2)}) collective-permute-start(bf16[512,1024]{1,0:T(8,128)(2,1)} %get-tuple-element.69), channel_id=1, source_target_pairs={{0,1},{1,0},{2,3},{3,2},{4,5},{5,4},{6,7},{7,6},{8,9},{9,8},{10,11... | collective-permute-start | bytes 3145736 | tf_op jit(solution)/shard_map/swap_x/ppermute | solution.py:40
  31.5 2.2 %collective-permute-start.7 = (bf16[512,1024]{1,0:T(8,128)(2,1)}, bf16[512,1024]{1,0:T(8,128)(2,1)}, u32[]{:S(2)}, u32[]{:S(2)}) collective-permute-start(bf16[512,1024]{1,0:T(8,128)(2,1)} %get-tuple-element.70), channel_id=1, source_target_pairs={{0,1},{1,0},{2,3},{3,2},{4,5},{5,4},{6,7},{7,6},{8,9},{9,8},{10,11... | collective-permute-start | bytes 3145736 | tf_op jit(solution)/shard_map/swap_x/ppermute | solution.py:40
  35.2 2.6 %collective-permute-start.11 = (f32[512,128]{1,0:T(8,128)S(1)}, f32[512,128]{1,0:T(8,128)S(1)}, u32[]{:S(2)}, u32[]{:S(2)}) collective-permute-start(f32[512,128]{1,0:T(8,128)S(1)} %copy-done.4), channel_id=1, source_target_pairs={{0,16},{16,0},{32,48},{48,32},{64,80},{80,64},{96,112},{112,96},{1... | collective-permute-start | bytes 786440 | tf_op jit(solution)/shard_map/ppermute | solution.py:49
  37.9 16.8 %weight_grad_blocks.1 = (bf16[512,1024]{1,0:T(8,128)(2,1)}, bf16[512,1024]{1,0:T(8,128)(2,1)}, bf16[512,1024]{1,0:T(8,128)(2,1)}, bf16[512,1024]{1,0:T(8,128)(2,...) custom-call(s32[6]{0:T(128)} %stack.26.s_ref, ...), custom_call_target="tpu_custom_call" | custom-call | bytes 52800000 | tf_op jit(solution)/shard_map/weight_grad_blocks/pallas_call | solution.py:186
  56.2 2.6 %collective-permute-done.8.rest_8_.rest_7_ = bf16[512,1024]{1,0:T(8,128)(2,1)} collective-permute-done((bf16[512,1024]{1,0:T(8,128)(2,1)}, bf16[512,1024]{1,0:T(8,128)(2,1)}, u32[]{:S(2)}, u32[]{:S(2)}) %collective-permute-start.8) | collective-permute-done | bytes 1048608 | tf_op jit(solution)/shard_map/ag_B/ppermute | solution.py:40
  59.6 1.4 collective-permute-done.13.rest_7_.rest_6_
  61.0 15.4 %half_near.1 = (bf16[512,1024]{1,0:T(8,128)(2,1)}, bf16[512,1024]{1,0:T(8,128)(2,1)}, bf16[512,1024]{1,0:T(8,128)(2,1)}, bf16[512,1024]{1,0:T(8,128)(2,1)}, bf16...) custom-call(s32[6]{0:T(128)} %stack.26.s_ref, f32[1,8192]{1,0:T(1,128)} %gain_ref.5, bf16[512,1024]{1,0:T(8,128)(2,1)} %copy-done.1, ...), custom_call_target="tpu_custom_call" | custom-call | bytes 33000000 | tf_op jit(solution)/shard_map/half_near/pallas_call | solution.py:311
  77.8 5.3 %gain_grad.2.rest_8_ = f32[1,4096]{1,0:T(1,128)} custom-call(s32[6]{0:T(128)} %stack.26.s_ref, bf16[512,1024]{1,0:T(8,128)(2,1)} %get-tuple-element.111.rest_0_.a_ref, bf16[512,1024]{1,0:T(8,128)(2,1)} %get-tuple-element.77.rest_1_.a_ref, bf16[512,1024]{1,0:T(8,128)(2,1)} %get-tuple-element.78.rest_2_.c_ref, bf16[512,1024]{1,0:T(8,128)(2,1)} %get-tuple-element.93.rest_3_, ...), custom_call_target="tpu_custom_call" | custom-call | tf_op jit(solution)/shard_map/gain_grad/pallas_call | solution.py:498
  83.3 2.6 %add_convert_fusion = bf16[512,1024]{1,0:T(8,128)(2,1)} fusion(bf16[512,1024]{1,0:T(8,128)(2,1)} %collective-permute-done.12, bf16[512,1024]{1,0:T(8,128)(2,1)S(1)} %copy-done.2), kind=kLoop, calls=%fused_computation | loop fusion | flops 2097152 | bytes 3145728 | tf_op jit(solution)/shard_map/convert_element_type | solution.py:541
  86.4 2.7 %collective-permute-start.10 = (bf16[512,1024]{1,0:T(8,128)(2,1)}, bf16[512,1024]{1,0:T(8,128)(2,1)}, u32[]{:S(2)}, u32[]{:S(2)}) collective-permute-start(bf16[512,1024]{1,0:T(8,128)(2,1)} %get-tuple-element.82.rest_1_), channel_id=1, source_target_pairs={{0,12},{1,13},{2,14},{3,15},{4,0},{5,1},{6,2},{7,3},{8,4},{9,5},{1... | collective-permute-start | bytes 3145736 | tf_op jit(solution)/shard_map/rs_C/ppermute | solution.py:40
  89.1 15.4 %half_far.1 = (bf16[512,1024]{1,0:T(8,128)(2,1)}, bf16[512,1024]{1,0:T(8,128)(2,1)}, bf16[512,1024]{1,0:T(8,128)(2,1)}, bf16[512,1024]{1,0:T(8,128)(2,1)}, bf16[...) custom-call(s32[6]{0:T(128)} %stack.26.s_ref, f32[1,8192]{1,0:T(1,128)} %gain_ref.5, bf16[512,1024]{1,0:T(8,128)(2,1)} %copy-done.1, ...), custom_call_target="tpu_custom_call" | custom-call | bytes 33000000 | tf_op jit(solution)/shard_map/half_far/pallas_call | solution.py:311
  104.6 5.5 %gain_grad.3 = f32[1,4096]{1,0:T(1,128)} custom-call(s32[6]{0:T(128)} %stack.26.s_ref, bf16[512,1024]{1,0:T(8,128)(2,1)} %get-tuple-element.112.rest_0_, bf16[512,1024]{1,0:T(8,128)(2,1)} %get-tuple-element.82.rest_1_, bf16[512,1024]{1,0:T(8,128)(2,1)} %get-tuple-element.80.rest_2_, bf16[512,1024]{1,0:T(8,128)(2,1)} %get-tuple-element.85.rest_3_, ...), custom_call_target="tpu_custom_call" | custom-call | tf_op jit(solution)/shard_map/gain_grad/pallas_call | solution.py:498
  110.1 1.4 collective-permute-start.28
  113.0 1.9 %collective-permute-start.20 = (bf16[512,1024]{1,0:T(8,128)(2,1)}, bf16[512,1024]{1,0:T(8,128)(2,1)}, u32[]{:S(2)}, u32[]{:S(2)}) collective-permute-start(bf16[512,1024]{1,0:T(8,128)(2,1)} %get-tuple-element.89), channel_id=1, source_target_pairs={{0,1},{1,0},{2,3},{3,2},{4,5},{5,4},{6,7},{7,6},{8,9},{9,8},{10,11... | collective-permute-start | bytes 3145736 | tf_op jit(solution)/shard_map/swap_w1/ppermute | solution.py:40
  115.7 2.6 %collective-permute-done.29 = f32[1,4096]{1,0:T(1,128)S(1)} collective-permute-done((f32[1,4096]{1,0:T(1,128)S(1)}, f32[1,4096]{1,0:T(1,128)S(1)}, u32[]{:S(2)}, u32[]{:S(2)}) %collective-permute-start.29) | collective-permute-done | bytes 16416 | tf_op jit(solution)/shard_map/ppermute | solution.py:45
  119.5 1.5 collective-permute-start.30
  121.0 4.3 %relay_sums.1 = (bf16[512,1024]{1,0:T(8,128)(2,1)}, bf16[512,1024]{1,0:T(8,128)(2,1)}) custom-call(bf16[512,1024]{1,0:T(8,128)(2,1)} %get-tuple-element.77.rest_1_.a_ref, bf16[512,1024]{1,0:T(8,128)(2,1)} %collective-permute-done.10.b_ref, bf16[512,1024]{1,0:T(8,128)(2,1)} %get-tuple-element.78.rest_2_.c_ref, ...), custom_call_target="tpu_custom_call" | custom-call | bytes 9900000 | tf_op jit(solution)/shard_map/relay_sums/pallas_call | solution.py:521
  125.4 1.3 collective-permute-start.24
  126.7 1.3 collective-permute-start.25
  128.2 2.5 %collective-permute-start.27 = (f32[512,128]{1,0:T(8,128)S(1)}, f32[512,128]{1,0:T(8,128)S(1)}, u32[]{:S(2)}, u32[]{:S(2)}) collective-permute-start(f32[512,128]{1,0:T(8,128)S(1)} %add.33), channel_id=1, source_target_pairs={{0,96},{16,112},{32,64},{48,80},{64,32},{80,48},{96,0},{112,16},{1... | collective-permute-start | bytes 786440 | tf_op jit(solution)/shard_map/ppermute | solution.py:49
  130.8 13.2 %hidden_grad.1 = (bf16[512,1024]{1,0:T(8,128)(2,1)}, bf16[512,8192]{1,0:T(8,128)(2,1)}) custom-call(s32[6]{0:T(128)} %stack.26.s_ref, bf16[512,8192]{1,0:T(8,128)(2,1)} %bitcast.12, bf16[512,1024]{1,0:T(8,128)(2,1)} %get-tuple-element.66.rest_1_.c_ref, f32[512,128]{1,0:T(8,128)} %get-tuple-element.98.inv_ref, bf16[512,1024]{1,0:T(8,128)(2,1)} %get-tuple-element.99.rest_0_, ...), custom_call_target="tpu_custom_call" | custom-call | bytes 330000000 | tf_op jit(solution)/shard_map/hidden_grad/pallas_call | solution.py:366
  144.0 2.0 %collective-permute-start.31 = (f32[1,4096]{1,0:T(1,128)S(1)}, f32[1,4096]{1,0:T(1,128)S(1)}, u32[]{:S(2)}, u32[]{:S(2)}) collective-permute-start(f32[1,4096]{1,0:T(1,128)S(1)} %add.38), channel_id=1, source_target_pairs={{0,1},{1,0},{2,3},{3,2},{4,5},{5,4},{6,7},{7,6},{8,9},{9,8},{10,11... | collective-permute-start | bytes 49160 | tf_op jit(solution)/shard_map/gain_c/ppermute | solution.py:40
  146.7 2.7 %collective-permute-done.24.b_ref = bf16[512,1024]{1,0:T(8,128)(2,1)} collective-permute-done((bf16[512,1024]{1,0:T(8,128)(2,1)S(1)}, bf16[512,1024]{1,0:T(8,128)(2,1)}, u32[]{:S(2)}, u32[]{:S(2)}) %collective-permute-start.24) | collective-permute-done | bytes 1048608 | tf_op jit(solution)/shard_map/rs_zm/ppermute | solution.py:40
  150.6 2.2 %collective-permute-done.26.d_ref = bf16[512,1024]{1,0:T(8,128)(2,1)} collective-permute-done((bf16[512,1024]{1,0:T(8,128)(2,1)}, bf16[512,1024]{1,0:T(8,128)(2,1)}, u32[]{:S(2)}, u32[]{:S(2)}) %collective-permute-start.26) | collective-permute-done | bytes 1048608 | tf_op jit(solution)/shard_map/rs_zp/ppermute | solution.py:40
  152.8 5.3 %update.1 = (bf16[512,1024]{1,0:T(8,128)(2,1)}, f32[8,1,64,128]{3,2,1,0:T(8,128)}, f32[8,1,64,128]{3,2,1,0:T(8,128)}) custom-call(s32[6]{0:T(128)} %stack.26.s_ref, bf16[512,1024]{1,0:T(8,128)(2,1)} %bitcast.19, bf16[512,1024]{1,0:T(8,128)(2,1)} %get-tuple-element.111.rest_0_.a_ref, bf16[512,1024]{1,0:T(8,128)(2,1)} %collective-permute-done.24.b_ref, ...), custom_call_target="tpu_custom_call" | custom-call | bytes 9900000 | tf_op jit(solution)/shard_map/update/pallas_call | solution.py:420
  (69 shorter events, 15.4 us)
Async XLA Ops:
  0.6 25.0 %collective-permute-start = (bf16[512,1024]{1,0:T(8,128)(2,1)}, bf16[512,1024]{1,0:T(8,128)(2,1)}, u32[]{:S(2)}, u32[]{:S(2)}) collective-permute-start(bf16[512,1024]{1,0:T(8,128)(2,1)} %bitcast.13), channel_id=1, source_target_pairs={{0,2},{1,3},{2,0},{3,1},{4,6},{5,7},{6,4},{7,5},{8,10},{9,11},{10,... | collective-permute-start | bytes 3145736 | tf_op jit(solution)/shard_map/ag_y/ppermute | solution.py:40
  2.8 25.6 %collective-permute-start.1 = (bf16[512,1024]{1,0:T(8,128)(2,1)}, bf16[512,1024]{1,0:T(8,128)(2,1)}, u32[]{:S(2)}, u32[]{:S(2)}) collective-permute-start(bf16[512,1024]{1,0:T(8,128)(2,1)} %bitcast.14), channel_id=1, source_target_pairs={{0,12},{1,13},{2,14},{3,15},{4,0},{5,1},{6,2},{7,3},{8,4},{9,5},{1... | collective-permute-start | bytes 3145736 | tf_op jit(solution)/shard_map/ag_zm/ppermute | solution.py:40
  6.6 24.9 %collective-permute-start.2 = (bf16[512,1024]{1,0:T(8,128)(2,1)}, bf16[512,1024]{1,0:T(8,128)(2,1)}, u32[]{:S(2)}, u32[]{:S(2)}) collective-permute-start(bf16[512,1024]{1,0:T(8,128)(2,1)} %bitcast.15), channel_id=1, source_target_pairs={{0,4},{1,5},{2,6},{3,7},{4,8},{5,9},{6,10},{7,11},{8,12},{9,13},{1... | collective-permute-start | bytes 3145736 | tf_op jit(solution)/shard_map/ag_zp/ppermute | solution.py:40
  20.8 12.9 %collective-permute-start.3 = (bf16[512,1024]{1,0:T(8,128)(2,1)}, bf16[512,1024]{1,0:T(8,128)(2,1)S(1)}, u32[]{:S(2)}, u32[]{:S(2)}) collective-permute-start(bf16[512,1024]{1,0:T(8,128)(2,1)} %get-tuple-element.66.rest_1_.c_ref), channel_id=1, source_target_pairs={{0,1},{1,0},{2,3},{3,2},{4,5},{5,4},{6,7},{7,6},{8,9},{9,8},{10,11... | collective-permute-start | bytes 3145736 | tf_op jit(solution)/shard_map/swap_x/ppermute | solution.py:40
  22.1 11.7 %collective-permute-start.4 = (bf16[512,1024]{1,0:T(8,128)(2,1)}, bf16[512,1024]{1,0:T(8,128)(2,1)S(1)}, u32[]{:S(2)}, u32[]{:S(2)}) collective-permute-start(bf16[512,1024]{1,0:T(8,128)(2,1)} %get-tuple-element.67), channel_id=1, source_target_pairs={{0,1},{1,0},{2,3},{3,2},{4,5},{5,4},{6,7},{7,6},{8,9},{9,8},{10,11... | collective-permute-start | bytes 3145736 | tf_op jit(solution)/shard_map/swap_x/ppermute | solution.py:40
  25.6 9.6 %collective-permute-start.5 = (bf16[512,1024]{1,0:T(8,128)(2,1)}, bf16[512,1024]{1,0:T(8,128)(2,1)}, u32[]{:S(2)}, u32[]{:S(2)}) collective-permute-start(bf16[512,1024]{1,0:T(8,128)(2,1)} %get-tuple-element.68), channel_id=1, source_target_pairs={{0,1},{1,0},{2,3},{3,2},{4,5},{5,4},{6,7},{7,6},{8,9},{9,8},{10,11... | collective-permute-start | bytes 3145736 | tf_op jit(solution)/shard_map/swap_x/ppermute | solution.py:40
  28.4 9.5 %collective-permute-start.6 = (bf16[512,1024]{1,0:T(8,128)(2,1)}, bf16[512,1024]{1,0:T(8,128)(2,1)}, u32[]{:S(2)}, u32[]{:S(2)}) collective-permute-start(bf16[512,1024]{1,0:T(8,128)(2,1)} %get-tuple-element.69), channel_id=1, source_target_pairs={{0,1},{1,0},{2,3},{3,2},{4,5},{5,4},{6,7},{7,6},{8,9},{9,8},{10,11... | collective-permute-start | bytes 3145736 | tf_op jit(solution)/shard_map/swap_x/ppermute | solution.py:40
  31.5 6.3 %collective-permute-start.7 = (bf16[512,1024]{1,0:T(8,128)(2,1)}, bf16[512,1024]{1,0:T(8,128)(2,1)}, u32[]{:S(2)}, u32[]{:S(2)}) collective-permute-start(bf16[512,1024]{1,0:T(8,128)(2,1)} %get-tuple-element.70), channel_id=1, source_target_pairs={{0,1},{1,0},{2,3},{3,2},{4,5},{5,4},{6,7},{7,6},{8,9},{9,8},{10,11... | collective-permute-start | bytes 3145736 | tf_op jit(solution)/shard_map/swap_x/ppermute | solution.py:40
  33.7 25.0 %collective-permute-start.8 = (bf16[512,1024]{1,0:T(8,128)(2,1)}, bf16[512,1024]{1,0:T(8,128)(2,1)}, u32[]{:S(2)}, u32[]{:S(2)}) collective-permute-start(bf16[512,1024]{1,0:T(8,128)(2,1)} %collective-permute-done.rest_6_.rest_5_), channel_id=1, source_target_pairs={{0,12},{1,13},{2,14},{3,15},{4,0},{5,1},{6,2},{7,3},{8,4},{9,5},{1... | collective-permute-start | bytes 3145736 | tf_op jit(solution)/shard_map/ag_B/ppermute | solution.py:40
  34.7 26.3 %collective-permute-start.13 = (bf16[512,1024]{1,0:T(8,128)(2,1)}, bf16[512,1024]{1,0:T(8,128)(2,1)}, u32[]{:S(2)}, u32[]{:S(2)}) collective-permute-start(bf16[512,1024]{1,0:T(8,128)(2,1)} %collective-permute-done.2.rest_5_.rest_4_), channel_id=1, source_target_pairs={{0,4},{1,5},{2,6},{3,7},{4,8},{5,9},{6,10},{7,11},{8,12},{9,13},{1... | collective-permute-start | bytes 3145736 | tf_op jit(solution)/shard_map/ag_A/ppermute | solution.py:40
  35.2 19.5 %collective-permute-start.11 = (f32[512,128]{1,0:T(8,128)S(1)}, f32[512,128]{1,0:T(8,128)S(1)}, u32[]{:S(2)}, u32[]{:S(2)}) collective-permute-start(f32[512,128]{1,0:T(8,128)S(1)} %copy-done.4), channel_id=1, source_target_pairs={{0,16},{16,0},{32,48},{48,32},{64,80},{80,64},{96,112},{112,96},{1... | collective-permute-start | bytes 786440 | tf_op jit(solution)/shard_map/ppermute | solution.py:49
  54.8 28.4 %collective-permute-start.12 = (bf16[512,1024]{1,0:T(8,128)(2,1)}, bf16[512,1024]{1,0:T(8,128)(2,1)}, u32[]{:S(2)}, u32[]{:S(2)}) collective-permute-start(bf16[512,1024]{1,0:T(8,128)(2,1)} %get-tuple-element.85.rest_3_), channel_id=1, source_target_pairs={{0,2},{1,3},{2,0},{3,1},{4,6},{5,7},{6,4},{7,5},{8,10},{9,11},{10,... | collective-permute-start | bytes 3145736 | tf_op jit(solution)/shard_map/rs_D/ppermute | solution.py:40
  54.9 21.9 %collective-permute-start.15 = (f32[512,128]{1,0:T(8,128)S(1)}, f32[512,128]{1,0:T(8,128)S(1)}, u32[]{:S(2)}, u32[]{:S(2)}) collective-permute-start(f32[512,128]{1,0:T(8,128)S(1)} %add.32), channel_id=1, source_target_pairs={{0,32},{16,48},{32,0},{48,16},{64,96},{80,112},{96,64},{112,80},{1... | collective-permute-start | bytes 786440 | tf_op jit(solution)/shard_map/ppermute | solution.py:49
  58.7 27.2 %collective-permute-start.9 = (bf16[512,1024]{1,0:T(8,128)(2,1)}, bf16[512,1024]{1,0:T(8,128)(2,1)}, u32[]{:S(2)}, u32[]{:S(2)}) collective-permute-start(bf16[512,1024]{1,0:T(8,128)(2,1)} %collective-permute-done.8.rest_8_.rest_7_), channel_id=1, source_target_pairs={{0,12},{1,13},{2,14},{3,15},{4,0},{5,1},{6,2},{7,3},{8,4},{9,5},{1... | collective-permute-start | bytes 3145736 | tf_op jit(solution)/shard_map/ag_D/ppermute | solution.py:40
  61.0 25.4 %collective-permute-start.14 = (bf16[512,1024]{1,0:T(8,128)(2,1)}, bf16[512,1024]{1,0:T(8,128)(2,1)}, u32[]{:S(2)}, u32[]{:S(2)}) collective-permute-start(bf16[512,1024]{1,0:T(8,128)(2,1)} %collective-permute-done.rest_6_.rest_5_), channel_id=1, source_target_pairs={{0,4},{1,5},{2,6},{3,7},{4,8},{5,9},{6,10},{7,11},{8,12},{9,13},{1... | collective-permute-start | bytes 3145736 | tf_op jit(solution)/shard_map/ag_C/ppermute | solution.py:40
  76.5 33.6 %collective-permute-start.16 = (bf16[512,1024]{1,0:T(8,128)(2,1)}, bf16[512,1024]{1,0:T(8,128)(2,1)}, u32[]{:S(2)}, u32[]{:S(2)}) collective-permute-start(bf16[512,1024]{1,0:T(8,128)(2,1)} %get-tuple-element.93.rest_3_), channel_id=1, source_target_pairs={{0,2},{1,3},{2,0},{3,1},{4,6},{5,7},{6,4},{7,5},{8,10},{9,11},{10,... | collective-permute-start | bytes 3145736 | tf_op jit(solution)/shard_map/rs_B/ppermute | solution.py:40
  76.7 34.8 %collective-permute-start.18 = (bf16[512,1024]{1,0:T(8,128)(2,1)}, bf16[512,1024]{1,0:T(8,128)(2,1)}, u32[]{:S(2)}, u32[]{:S(2)}) collective-permute-start(bf16[512,1024]{1,0:T(8,128)(2,1)} %get-tuple-element.75), channel_id=1, source_target_pairs={{0,1},{1,0},{2,3},{3,2},{4,5},{5,4},{6,7},{7,6},{8,9},{9,8},{10,11... | collective-permute-start | bytes 3145736 | tf_op jit(solution)/shard_map/swap_w0/ppermute | solution.py:40
  83.2 32.5 %collective-permute-start.19 = (bf16[512,1024]{1,0:T(8,128)(2,1)}, bf16[512,1024]{1,0:T(8,128)(2,1)}, u32[]{:S(2)}, u32[]{:S(2)}) collective-permute-start(bf16[512,1024]{1,0:T(8,128)(2,1)} %get-tuple-element.103), channel_id=1, source_target_pairs={{0,1},{1,0},{2,3},{3,2},{4,5},{5,4},{6,7},{7,6},{8,9},{9,8},{10,11... | collective-permute-start | bytes 3145736 | tf_op jit(solution)/shard_map/swap_w0/ppermute | solution.py:40
  85.9 33.6 %collective-permute-start.17 = (bf16[512,1024]{1,0:T(8,128)(2,1)}, bf16[512,1024]{1,0:T(8,128)(2,1)}, u32[]{:S(2)}, u32[]{:S(2)}) collective-permute-start(bf16[512,1024]{1,0:T(8,128)(2,1)} %add_convert_fusion), channel_id=1, source_target_pairs={{0,4},{1,5},{2,6},{3,7},{4,8},{5,9},{6,10},{7,11},{8,12},{9,13},{1... | collective-permute-start | bytes 3145736 | tf_op jit(solution)/shard_map/rs_A/ppermute | solution.py:40
  86.4 33.1 %collective-permute-start.10 = (bf16[512,1024]{1,0:T(8,128)(2,1)}, bf16[512,1024]{1,0:T(8,128)(2,1)}, u32[]{:S(2)}, u32[]{:S(2)}) collective-permute-start(bf16[512,1024]{1,0:T(8,128)(2,1)} %get-tuple-element.82.rest_1_), channel_id=1, source_target_pairs={{0,12},{1,13},{2,14},{3,15},{4,0},{5,1},{6,2},{7,3},{8,4},{9,5},{1... | collective-permute-start | bytes 3145736 | tf_op jit(solution)/shard_map/rs_C/ppermute | solution.py:40
  110.1 2.9 %collective-permute-start.28 = (f32[1,4096]{1,0:T(1,128)}, f32[1,4096]{1,0:T(1,128)S(1)}, u32[]{:S(2)}, u32[]{:S(2)}) collective-permute-start(f32[1,4096]{1,0:T(1,128)} %gain_grad.3), channel_id=1, source_target_pairs={{0,2},{1,3},{2,0},{3,1},{4,6},{5,7},{6,4},{7,5},{8,10},{9,11},{10,... | collective-permute-start | bytes 49160 | tf_op jit(solution)/shard_map/gain_y/ppermute | solution.py:40
  111.5 13.9 %collective-permute-start.22 = (bf16[512,1024]{1,0:T(8,128)(2,1)}, bf16[512,1024]{1,0:T(8,128)(2,1)}, u32[]{:S(2)}, u32[]{:S(2)}) collective-permute-start(bf16[512,1024]{1,0:T(8,128)(2,1)} %get-tuple-element.107), channel_id=1, source_target_pairs={{0,1},{1,0},{2,3},{3,2},{4,5},{5,4},{6,7},{7,6},{8,9},{9,8},{10,11... | collective-permute-start | bytes 3145736 | tf_op jit(solution)/shard_map/swap_w0/ppermute | solution.py:40
  113.0 15.0 %collective-permute-start.20 = (bf16[512,1024]{1,0:T(8,128)(2,1)}, bf16[512,1024]{1,0:T(8,128)(2,1)}, u32[]{:S(2)}, u32[]{:S(2)}) collective-permute-start(bf16[512,1024]{1,0:T(8,128)(2,1)} %get-tuple-element.89), channel_id=1, source_target_pairs={{0,1},{1,0},{2,3},{3,2},{4,5},{5,4},{6,7},{7,6},{8,9},{9,8},{10,11... | collective-permute-start | bytes 3145736 | tf_op jit(solution)/shard_map/swap_w1/ppermute | solution.py:40
  115.7 2.7 %collective-permute-start.29 = (f32[1,4096]{1,0:T(1,128)S(1)}, f32[1,4096]{1,0:T(1,128)S(1)}, u32[]{:S(2)}, u32[]{:S(2)}) collective-permute-start(f32[1,4096]{1,0:T(1,128)S(1)} %add.36), channel_id=1, source_target_pairs={{0,4},{1,5},{2,6},{3,7},{4,0},{5,1},{6,2},{7,3},{8,12},{9,13},{10,... | collective-permute-start | bytes 49160 | tf_op jit(solution)/shard_map/ppermute | solution.py:45
  118.3 9.9 %collective-permute-start.21 = (bf16[512,1024]{1,0:T(8,128)(2,1)}, bf16[512,1024]{1,0:T(8,128)(2,1)}, u32[]{:S(2)}, u32[]{:S(2)}) collective-permute-start(bf16[512,1024]{1,0:T(8,128)(2,1)} %get-tuple-element.104), channel_id=1, source_target_pairs={{0,1},{1,0},{2,3},{3,2},{4,5},{5,4},{6,7},{7,6},{8,9},{9,8},{10,11... | collective-permute-start | bytes 3145736 | tf_op jit(solution)/shard_map/swap_w1/ppermute | solution.py:40
  119.5 11.3 %collective-permute-start.23 = (bf16[512,1024]{1,0:T(8,128)(2,1)}, bf16[512,1024]{1,0:T(8,128)(2,1)}, u32[]{:S(2)}, u32[]{:S(2)}) collective-permute-start(bf16[512,1024]{1,0:T(8,128)(2,1)} %get-tuple-element.108), channel_id=1, source_target_pairs={{0,1},{1,0},{2,3},{3,2},{4,5},{5,4},{6,7},{7,6},{8,9},{9,8},{10,11... | collective-permute-start | bytes 3145736 | tf_op jit(solution)/shard_map/swap_w1/ppermute | solution.py:40
  119.5 7.2 %collective-permute-start.30 = (f32[1,4096]{1,0:T(1,128)S(1)}, f32[1,4096]{1,0:T(1,128)S(1)}, u32[]{:S(2)}, u32[]{:S(2)}) collective-permute-start(f32[1,4096]{1,0:T(1,128)S(1)} %add.37), channel_id=1, source_target_pairs={{0,12},{1,13},{2,14},{3,15},{4,8},{5,9},{6,10},{7,11},{8,4},{9,5},... | collective-permute-start | bytes 49160 | tf_op jit(solution)/shard_map/ppermute | solution.py:45
  125.4 24.1 %collective-permute-start.24 = (bf16[512,1024]{1,0:T(8,128)(2,1)S(1)}, bf16[512,1024]{1,0:T(8,128)(2,1)}, u32[]{:S(2)}, u32[]{:S(2)}) collective-permute-start(bf16[512,1024]{1,0:T(8,128)(2,1)S(1)} %copy-done.3), channel_id=1, source_target_pairs={{0,12},{1,13},{2,14},{3,15},{4,0},{5,1},{6,2},{7,3},{8,4},{9,5},{1... | collective-permute-start | bytes 3145736 | tf_op jit(solution)/shard_map/rs_zm/ppermute | solution.py:40
  126.7 23.9 %collective-permute-start.25 = (bf16[512,1024]{1,0:T(8,128)(2,1)}, bf16[512,1024]{1,0:T(8,128)(2,1)}, u32[]{:S(2)}, u32[]{:S(2)}) collective-permute-start(bf16[512,1024]{1,0:T(8,128)(2,1)} %get-tuple-element.113), channel_id=1, source_target_pairs={{0,2},{1,3},{2,0},{3,1},{4,6},{5,7},{6,4},{7,5},{8,10},{9,11},{10,... | collective-permute-start | bytes 3145736 | tf_op jit(solution)/shard_map/rs_y/ppermute | solution.py:40
  128.0 24.8 %collective-permute-start.26 = (bf16[512,1024]{1,0:T(8,128)(2,1)}, bf16[512,1024]{1,0:T(8,128)(2,1)}, u32[]{:S(2)}, u32[]{:S(2)}) collective-permute-start(bf16[512,1024]{1,0:T(8,128)(2,1)} %get-tuple-element.114), channel_id=1, source_target_pairs={{0,4},{1,5},{2,6},{3,7},{4,8},{5,9},{6,10},{7,11},{8,12},{9,13},{1... | collective-permute-start | bytes 3145736 | tf_op jit(solution)/shard_map/rs_zp/ppermute | solution.py:40
  128.2 17.7 %collective-permute-start.27 = (f32[512,128]{1,0:T(8,128)S(1)}, f32[512,128]{1,0:T(8,128)S(1)}, u32[]{:S(2)}, u32[]{:S(2)}) collective-permute-start(f32[512,128]{1,0:T(8,128)S(1)} %add.33), channel_id=1, source_target_pairs={{0,96},{16,112},{32,64},{48,80},{64,32},{80,48},{96,0},{112,16},{1... | collective-permute-start | bytes 786440 | tf_op jit(solution)/shard_map/ppermute | solution.py:49
  144.0 14.2 %collective-permute-start.31 = (f32[1,4096]{1,0:T(1,128)S(1)}, f32[1,4096]{1,0:T(1,128)S(1)}, u32[]{:S(2)}, u32[]{:S(2)}) collective-permute-start(f32[1,4096]{1,0:T(1,128)S(1)} %add.38), channel_id=1, source_target_pairs={{0,1},{1,0},{2,3},{3,2},{4,5},{5,4},{6,7},{7,6},{8,9},{9,8},{10,11... | collective-permute-start | bytes 49160 | tf_op jit(solution)/shard_map/gain_c/ppermute | solution.py:40
  (6 other events, 71.2 us)

commit v4 on v3

--- a/solution.py
+++ b/solution.py
@@ -598,9 +598,9 @@
     sent1, own1 = half_call(
         far_half, after(scalars, sent0[0], far), recv, mine, cots, norm_gain, w, "half_far"
     )
-    got1 = [shift(v, 0, 0, 1, "swap_w1") for v in sent1]
 
     partial = gain_call(far_order, after(scalars, sent1[0], second_sum), g, w, near_sums)
+    got1 = [shift(after(v, partial), 0, 0, 1, "swap_w1") for v in sent1]
     left, side, over = (after(v, partial) for v in (left, side, over))
     from_next = shift(after(g[3, 0], left), -1, 0, 0, "rs_zm")
     to_side, to_last = relay_call(g[0, 1], left, g[1, 0], side, over)
@@ -613,7 +613,7 @@
         (own0[-1], own1[-1], got0[-1], got1[-1]),
     )
 
-    partial = partial + shift(partial, 0, 1, 0, "gain_y")
+    partial = partial + shift(after(partial, to_last), 0, 1, 0, "gain_y")
     partial = partial + flip_z(partial, 1)
     partial = partial + flip_z(partial, 3)
     other = shift(after(partial, hidden_grad), 0, 0, 1, "gain_c")

time: 161 us -> 177 us (1.099)
  waiting for transfers between devices: 19.5 us -> 36.7 us
    ppermute x2, waiting for transfers between devices: 2.58 us -> 20.4 us  [flip_z(): return lax.ppermute(x, 'fsdp', pairs)]
    ppermute x27, waiting for transfers between devices: 16.9 us -> 12.1 us  [shift(): return lax.ppermute(x, 'fsdp', pairs)]
    ppermute x3, waiting for transfers between devices: 0.01 us -> 4.19 us  [flip_replica(): return lax.ppermute(x, 'replica', [(i, i ^ mask) for i in range(8)])]
    ppermute x2, starting transfers between devices: 1.61 us -> 3.48 us  [flip_z(): return lax.ppermute(x, 'fsdp', pairs)]
  transfers between devices with their start and end apart: 32 -> 32, of which waited for: 11 -> 8; matrix products, arithmetic and copies ran while one was open for 3% -> 2% of each run, Pallas kernels for 59% -> 53%
where the time goes in v4:
time: 177 us
  Pallas kernels  94.4 us (53%)
  starting transfers between devices  38.1 us (22%)
  waiting for transfers between devices  36.7 us (21%)
  other arithmetic  4.24 us (2%)
    pallas_call x2, Pallas kernels, half_call(): pl.pallas_call(functools.partial(half_kernel, depths), grid_spec=pltpu.Pr...  30.9 us
    ppermute x27, starting transfers between devices, shift(): return lax.ppermute(x, 'fsdp', pairs)  28.2 us
    ppermute x2, waiting for transfers between devices, flip_z(): return lax.ppermute(x, 'fsdp', pairs)  20.4 us
    pallas_call x1, Pallas kernels, grad_call(): pl.pallas_call(functools.partial(grad_kernel, places), grid_spec=pltpu.Pr...  16.8 us
    pallas_call x1, Pallas kernels, hidden_call(): pl.pallas_call(functools.partial(hidden_kernel, depths), grid_spec=pltpu....  13.2 us
    ppermute x27, waiting for transfers between devices, shift(): return lax.ppermute(x, 'fsdp', pairs)  12.1 us
    pallas_call x2, Pallas kernels, gain_call(): pl.pallas_call(functools.partial(gain_kernel, places, before is not None)...  10.8 us
    pallas_call x1, Pallas kernels, norm_call(): pl.pallas_call(norm_kernel, grid_spec=pltpu.PrefetchScalarGridSpec(num_sc...  10.7 us
  transfers between devices with their start and end apart: 32, of which 8 were waited for; matrix products, arithmetic and copies ran while one was open for 2% of the time, Pallas kernels for 53%

profile of v4, /device:TPU:1, one launch (start us, length us, event | category | flops | bytes accessed | tf_op | source)
XLA Modules:
  0.0 176.5 jit_solution(8572085182229817942)
XLA Ops:
  0.6 2.2 %collective-permute-start = (bf16[512,1024]{1,0:T(8,128)(2,1)}, bf16[512,1024]{1,0:T(8,128)(2,1)}, u32[]{:S(2)}, u32[]{:S(2)}) collective-permute-start(bf16[512,1024]{1,0:T(8,128)(2,1)} %bitcast.13), channel_id=1, source_target_pairs={{0,2},{1,3},{2,0},{3,1},{4,6},{5,7},{6,4},{7,5},{8,10},{9,11},{10,... | collective-permute-start | bytes 3145736 | tf_op jit(solution)/shard_map/ag_y/ppermute | solution.py:40
  2.8 3.8 %collective-permute-start.1 = (bf16[512,1024]{1,0:T(8,128)(2,1)}, bf16[512,1024]{1,0:T(8,128)(2,1)}, u32[]{:S(2)}, u32[]{:S(2)}) collective-permute-start(bf16[512,1024]{1,0:T(8,128)(2,1)} %bitcast.14), channel_id=1, source_target_pairs={{0,12},{1,13},{2,14},{3,15},{4,0},{5,1},{6,2},{7,3},{8,4},{9,5},{1... | collective-permute-start | bytes 3145736 | tf_op jit(solution)/shard_map/ag_zm/ppermute | solution.py:40
  7.8 2.3 %outer_term.1 = f32[512,128]{1,0:T(8,128)} custom-call(s32[6]{0:T(128)} %stack.26.s_ref, bf16[512,1024]{1,0:T(8,128)(2,1)} %bitcast.16, f32[8,1,64,128]{3,2,1,0:T(8,128)} %rest_0_.1, f32[8,1,64,128]{3,2,1,0:T(8,128)} %rest_1_.1), custom_call_target="tpu_custom_call" | custom-call | bytes 3300000 | tf_op jit(solution)/shard_map/outer_term/pallas_call | solution.py:459
  10.2 10.7 %norm.1 = (bf16[512,5120]{1,0:T(8,128)(2,1)}, bf16[512,1024]{1,0:T(8,128)(2,1)}, bf16[512,1024]{1,0:T(8,128)(2,1)}, bf16[512,1024]{1,0:T(8,128)(2,1)}, bf16[512,...) custom-call(s32[6]{0:T(128)} %stack.26.s_ref, bf16[512,8192]{1,0:T(8,128)(2,1)} %bitcast.11, ...), custom_call_target="tpu_custom_call" | custom-call | bytes 26400000 | tf_op jit(solution)/shard_map/norm/pallas_call | solution.py:113
  20.8 1.3 collective-permute-start.3
  22.2 3.4 %collective-permute-done.rest_6_.rest_5_ = bf16[512,1024]{1,0:T(8,128)(2,1)} collective-permute-done((bf16[512,1024]{1,0:T(8,128)(2,1)}, bf16[512,1024]{1,0:T(8,128)(2,1)}, u32[]{:S(2)}, u32[]{:S(2)}) %collective-permute-start) | collective-permute-done | bytes 1048608 | tf_op jit(solution)/shard_map/ag_y/ppermute | solution.py:40
  25.6 1.6 collective-permute-start.5
  27.3 1.1 collective-permute-done.1.rest_7_.rest_6_
  28.4 1.9 %collective-permute-start.6 = (bf16[512,1024]{1,0:T(8,128)(2,1)}, bf16[512,1024]{1,0:T(8,128)(2,1)}, u32[]{:S(2)}, u32[]{:S(2)}) collective-permute-start(bf16[512,1024]{1,0:T(8,128)(2,1)} %get-tuple-element.73), channel_id=1, source_target_pairs={{0,1},{1,0},{2,3},{3,2},{4,5},{5,4},{6,7},{7,6},{8,9},{9,8},{10,11... | collective-permute-start | bytes 3145736 | tf_op jit(solution)/shard_map/swap_x/ppermute | solution.py:40
  30.3 1.2 collective-permute-done.2.rest_5_.rest_4_
  31.5 2.2 %collective-permute-start.7 = (bf16[512,1024]{1,0:T(8,128)(2,1)}, bf16[512,1024]{1,0:T(8,128)(2,1)}, u32[]{:S(2)}, u32[]{:S(2)}) collective-permute-start(bf16[512,1024]{1,0:T(8,128)(2,1)} %get-tuple-element.74), channel_id=1, source_target_pairs={{0,1},{1,0},{2,3},{3,2},{4,5},{5,4},{6,7},{7,6},{8,9},{9,8},{10,11... | collective-permute-start | bytes 3145736 | tf_op jit(solution)/shard_map/swap_x/ppermute | solution.py:40
  35.2 2.6 %collective-permute-start.11 = (f32[512,128]{1,0:T(8,128)S(1)}, f32[512,128]{1,0:T(8,128)S(1)}, u32[]{:S(2)}, u32[]{:S(2)}) collective-permute-start(f32[512,128]{1,0:T(8,128)S(1)} %copy-done.4), channel_id=1, source_target_pairs={{0,16},{16,0},{32,48},{48,32},{64,80},{80,64},{96,112},{112,96},{1... | collective-permute-start | bytes 786440 | tf_op jit(solution)/shard_map/ppermute | solution.py:49
  37.9 16.8 %weight_grad_blocks.1 = (bf16[512,1024]{1,0:T(8,128)(2,1)}, bf16[512,1024]{1,0:T(8,128)(2,1)}, bf16[512,1024]{1,0:T(8,128)(2,1)}, bf16[512,1024]{1,0:T(8,128)(2,...) custom-call(s32[6]{0:T(128)} %stack.26.s_ref, ...), custom_call_target="tpu_custom_call" | custom-call | bytes 52800000 | tf_op jit(solution)/shard_map/weight_grad_blocks/pallas_call | solution.py:186
  54.9 3.9 %collective-permute-done.8.rest_8_.rest_7_ = bf16[512,1024]{1,0:T(8,128)(2,1)} collective-permute-done((bf16[512,1024]{1,0:T(8,128)(2,1)}, bf16[512,1024]{1,0:T(8,128)(2,1)}, u32[]{:S(2)}, u32[]{:S(2)}) %collective-permute-start.8) | collective-permute-done | bytes 1048608 | tf_op jit(solution)/shard_map/ag_B/ppermute | solution.py:40
  59.6 1.4 collective-permute-done.13.rest_7_.rest_6_
  61.0 15.4 %half_near.1 = (bf16[512,1024]{1,0:T(8,128)(2,1)}, bf16[512,1024]{1,0:T(8,128)(2,1)}, bf16[512,1024]{1,0:T(8,128)(2,1)}, bf16[512,1024]{1,0:T(8,128)(2,1)}, bf16...) custom-call(s32[6]{0:T(128)} %stack.26.s_ref, f32[1,8192]{1,0:T(1,128)} %gain_ref.5, bf16[512,1024]{1,0:T(8,128)(2,1)} %copy-done.1, ...), custom_call_target="tpu_custom_call" | custom-call | bytes 33000000 | tf_op jit(solution)/shard_map/half_near/pallas_call | solution.py:311
  77.8 5.3 %gain_grad.2.rest_8_ = f32[1,4096]{1,0:T(1,128)} custom-call(s32[6]{0:T(128)} %stack.26.s_ref, bf16[512,1024]{1,0:T(8,128)(2,1)} %get-tuple-element.118.rest_0_.a_ref, bf16[512,1024]{1,0:T(8,128)(2,1)} %get-tuple-element.81.rest_1_.a_ref, bf16[512,1024]{1,0:T(8,128)(2,1)} %get-tuple-element.82.rest_2_.c_ref, bf16[512,1024]{1,0:T(8,128)(2,1)} %get-tuple-element.97.rest_3_, ...), custom_call_target="tpu_custom_call" | custom-call | tf_op jit(solution)/shard_map/gain_grad/pallas_call | solution.py:498
  83.1 1.3 collective-permute-start.15
  84.4 2.6 %add_convert_fusion = bf16[512,1024]{1,0:T(8,128)(2,1)} fusion(bf16[512,1024]{1,0:T(8,128)(2,1)} %collective-permute-done.12, bf16[512,1024]{1,0:T(8,128)(2,1)S(1)} %copy-done.2), kind=kLoop, calls=%fused_computation | loop fusion | flops 2097152 | bytes 3145728 | tf_op jit(solution)/shard_map/convert_element_type | solution.py:541
  87.1 4.2 %collective-permute-done.15 = f32[512,128]{1,0:T(8,128)S(1)} collective-permute-done((f32[512,128]{1,0:T(8,128)S(1)}, f32[512,128]{1,0:T(8,128)S(1)}, u32[]{:S(2)}, u32[]{:S(2)}) %collective-permute-start.15) | collective-permute-done | bytes 262176 | tf_op jit(solution)/shard_map/ppermute | solution.py:49
  91.2 2.9 %collective-permute-start.10 = (bf16[512,1024]{1,0:T(8,128)(2,1)}, bf16[512,1024]{1,0:T(8,128)(2,1)}, u32[]{:S(2)}, u32[]{:S(2)}) collective-permute-start(bf16[512,1024]{1,0:T(8,128)(2,1)} %get-tuple-element.86.rest_1_), channel_id=1, source_target_pairs={{0,12},{1,13},{2,14},{3,15},{4,0},{5,1},{6,2},{7,3},{8,4},{9,5},{1... | collective-permute-start | bytes 3145736 | tf_op jit(solution)/shard_map/rs_C/ppermute | solution.py:40
  95.2 15.5 %half_far.1 = (bf16[512,1024]{1,0:T(8,128)(2,1)}, bf16[512,1024]{1,0:T(8,128)(2,1)}, bf16[512,1024]{1,0:T(8,128)(2,1)}, bf16[512,1024]{1,0:T(8,128)(2,1)}, bf16[...) custom-call(s32[6]{0:T(128)} %stack.26.s_ref, f32[1,8192]{1,0:T(1,128)} %gain_ref.5, bf16[512,1024]{1,0:T(8,128)(2,1)} %copy-done.1, ...), custom_call_target="tpu_custom_call" | custom-call | bytes 33000000 | tf_op jit(solution)/shard_map/half_far/pallas_call | solution.py:311
  110.7 5.5 %gain_grad.3 = f32[1,4096]{1,0:T(1,128)} custom-call(s32[6]{0:T(128)} %stack.26.s_ref, bf16[512,1024]{1,0:T(8,128)(2,1)} %get-tuple-element.119.rest_0_, bf16[512,1024]{1,0:T(8,128)(2,1)} %get-tuple-element.86.rest_1_, bf16[512,1024]{1,0:T(8,128)(2,1)} %get-tuple-element.84.rest_2_, bf16[512,1024]{1,0:T(8,128)(2,1)} %get-tuple-element.89.rest_3_, ...), custom_call_target="tpu_custom_call" | custom-call | tf_op jit(solution)/shard_map/gain_grad/pallas_call | solution.py:498
  117.9 4.3 %relay_sums.1 = (bf16[512,1024]{1,0:T(8,128)(2,1)}, bf16[512,1024]{1,0:T(8,128)(2,1)}) custom-call(bf16[512,1024]{1,0:T(8,128)(2,1)} %get-tuple-element.81.rest_1_.a_ref, bf16[512,1024]{1,0:T(8,128)(2,1)} %collective-permute-done.10.b_ref, bf16[512,1024]{1,0:T(8,128)(2,1)} %get-tuple-element.82.rest_2_.c_ref, ...), custom_call_target="tpu_custom_call" | custom-call | bytes 9900000 | tf_op jit(solution)/shard_map/relay_sums/pallas_call | solution.py:521
  122.2 1.4 collective-permute-start.28
  124.9 3.4 %collective-permute-start.24 = (bf16[512,1024]{1,0:T(8,128)(2,1)S(1)}, bf16[512,1024]{1,0:T(8,128)(2,1)}, u32[]{:S(2)}, u32[]{:S(2)}) collective-permute-start(bf16[512,1024]{1,0:T(8,128)(2,1)S(1)} %copy-done.3), channel_id=1, source_target_pairs={{0,12},{1,13},{2,14},{3,15},{4,0},{5,1},{6,2},{7,3},{8,4},{9,5},{1... | collective-permute-start | bytes 3145736 | tf_op jit(solution)/shard_map/rs_zm/ppermute | solution.py:40
  128.4 20.4 %collective-permute-done.29 = f32[1,4096]{1,0:T(1,128)S(1)} collective-permute-done((f32[1,4096]{1,0:T(1,128)S(1)}, f32[1,4096]{1,0:T(1,128)S(1)}, u32[]{:S(2)}, u32[]{:S(2)}) %collective-permute-start.29) | collective-permute-done | bytes 16416 | tf_op jit(solution)/shard_map/ppermute | solution.py:45
  148.8 2.5 %collective-permute-start.27 = (f32[512,128]{1,0:T(8,128)S(1)}, f32[512,128]{1,0:T(8,128)S(1)}, u32[]{:S(2)}, u32[]{:S(2)}) collective-permute-start(f32[512,128]{1,0:T(8,128)S(1)} %add.33), channel_id=1, source_target_pairs={{0,96},{16,112},{32,64},{48,80},{64,32},{80,48},{96,0},{112,16},{1... | collective-permute-start | bytes 786440 | tf_op jit(solution)/shard_map/ppermute | solution.py:49
  151.3 3.4 %collective-permute-start.30 = (f32[1,4096]{1,0:T(1,128)S(1)}, f32[1,4096]{1,0:T(1,128)S(1)}, u32[]{:S(2)}, u32[]{:S(2)}) collective-permute-start(f32[1,4096]{1,0:T(1,128)S(1)} %add.37), channel_id=1, source_target_pairs={{0,12},{1,13},{2,14},{3,15},{4,8},{5,9},{6,10},{7,11},{8,4},{9,5},... | collective-permute-start | bytes 49160 | tf_op jit(solution)/shard_map/ppermute | solution.py:45
  154.7 13.2 %hidden_grad.1 = (bf16[512,1024]{1,0:T(8,128)(2,1)}, bf16[512,8192]{1,0:T(8,128)(2,1)}) custom-call(s32[6]{0:T(128)} %stack.26.s_ref, bf16[512,8192]{1,0:T(8,128)(2,1)} %bitcast.12, bf16[512,1024]{1,0:T(8,128)(2,1)} %get-tuple-element.70.rest_1_.c_ref, f32[512,128]{1,0:T(8,128)} %get-tuple-element.102.inv_ref, bf16[512,1024]{1,0:T(8,128)(2,1)} %get-tuple-element.103.rest_0_, ...), custom_call_target="tpu_custom_call" | custom-call | bytes 330000000 | tf_op jit(solution)/shard_map/hidden_grad/pallas_call | solution.py:366
  168.0 1.6 collective-permute-start.31
  170.4 5.2 %update.1 = (bf16[512,1024]{1,0:T(8,128)(2,1)}, f32[8,1,64,128]{3,2,1,0:T(8,128)}, f32[8,1,64,128]{3,2,1,0:T(8,128)}) custom-call(s32[6]{0:T(128)} %stack.26.s_ref, bf16[512,1024]{1,0:T(8,128)(2,1)} %bitcast.19, bf16[512,1024]{1,0:T(8,128)(2,1)} %get-tuple-element.118.rest_0_.a_ref, bf16[512,1024]{1,0:T(8,128)(2,1)} %collective-permute-done.24.b_ref, ...), custom_call_target="tpu_custom_call" | custom-call | bytes 9900000 | tf_op jit(solution)/shard_map/update/pallas_call | solution.py:420
  (71 shorter events, 10.3 us)
Async XLA Ops:
  0.6 25.0 %collective-permute-start = (bf16[512,1024]{1,0:T(8,128)(2,1)}, bf16[512,1024]{1,0:T(8,128)(2,1)}, u32[]{:S(2)}, u32[]{:S(2)}) collective-permute-start(bf16[512,1024]{1,0:T(8,128)(2,1)} %bitcast.13), channel_id=1, source_target_pairs={{0,2},{1,3},{2,0},{3,1},{4,6},{5,7},{6,4},{7,5},{8,10},{9,11},{10,... | collective-permute-start | bytes 3145736 | tf_op jit(solution)/shard_map/ag_y/ppermute | solution.py:40
  2.8 25.6 %collective-permute-start.1 = (bf16[512,1024]{1,0:T(8,128)(2,1)}, bf16[512,1024]{1,0:T(8,128)(2,1)}, u32[]{:S(2)}, u32[]{:S(2)}) collective-permute-start(bf16[512,1024]{1,0:T(8,128)(2,1)} %bitcast.14), channel_id=1, source_target_pairs={{0,12},{1,13},{2,14},{3,15},{4,0},{5,1},{6,2},{7,3},{8,4},{9,5},{1... | collective-permute-start | bytes 3145736 | tf_op jit(solution)/shard_map/ag_zm/ppermute | solution.py:40
  6.6 24.9 %collective-permute-start.2 = (bf16[512,1024]{1,0:T(8,128)(2,1)}, bf16[512,1024]{1,0:T(8,128)(2,1)}, u32[]{:S(2)}, u32[]{:S(2)}) collective-permute-start(bf16[512,1024]{1,0:T(8,128)(2,1)} %bitcast.15), channel_id=1, source_target_pairs={{0,4},{1,5},{2,6},{3,7},{4,8},{5,9},{6,10},{7,11},{8,12},{9,13},{1... | collective-permute-start | bytes 3145736 | tf_op jit(solution)/shard_map/ag_zp/ppermute | solution.py:40
  20.8 12.9 %collective-permute-start.3 = (bf16[512,1024]{1,0:T(8,128)(2,1)}, bf16[512,1024]{1,0:T(8,128)(2,1)S(1)}, u32[]{:S(2)}, u32[]{:S(2)}) collective-permute-start(bf16[512,1024]{1,0:T(8,128)(2,1)} %get-tuple-element.70.rest_1_.c_ref), channel_id=1, source_target_pairs={{0,1},{1,0},{2,3},{3,2},{4,5},{5,4},{6,7},{7,6},{8,9},{9,8},{10,11... | collective-permute-start | bytes 3145736 | tf_op jit(solution)/shard_map/swap_x/ppermute | solution.py:40
  22.1 11.7 %collective-permute-start.4 = (bf16[512,1024]{1,0:T(8,128)(2,1)}, bf16[512,1024]{1,0:T(8,128)(2,1)S(1)}, u32[]{:S(2)}, u32[]{:S(2)}) collective-permute-start(bf16[512,1024]{1,0:T(8,128)(2,1)} %get-tuple-element.71), channel_id=1, source_target_pairs={{0,1},{1,0},{2,3},{3,2},{4,5},{5,4},{6,7},{7,6},{8,9},{9,8},{10,11... | collective-permute-start | bytes 3145736 | tf_op jit(solution)/shard_map/swap_x/ppermute | solution.py:40
  25.6 9.6 %collective-permute-start.5 = (bf16[512,1024]{1,0:T(8,128)(2,1)}, bf16[512,1024]{1,0:T(8,128)(2,1)}, u32[]{:S(2)}, u32[]{:S(2)}) collective-permute-start(bf16[512,1024]{1,0:T(8,128)(2,1)} %get-tuple-element.72), channel_id=1, source_target_pairs={{0,1},{1,0},{2,3},{3,2},{4,5},{5,4},{6,7},{7,6},{8,9},{9,8},{10,11... | collective-permute-start | bytes 3145736 | tf_op jit(solution)/shard_map/swap_x/ppermute | solution.py:40
  28.4 9.5 %collective-permute-start.6 = (bf16[512,1024]{1,0:T(8,128)(2,1)}, bf16[512,1024]{1,0:T(8,128)(2,1)}, u32[]{:S(2)}, u32[]{:S(2)}) collective-permute-start(bf16[512,1024]{1,0:T(8,128)(2,1)} %get-tuple-element.73), channel_id=1, source_target_pairs={{0,1},{1,0},{2,3},{3,2},{4,5},{5,4},{6,7},{7,6},{8,9},{9,8},{10,11... | collective-permute-start | bytes 3145736 | tf_op jit(solution)/shard_map/swap_x/ppermute | solution.py:40
  31.5 6.3 %collective-permute-start.7 = (bf16[512,1024]{1,0:T(8,128)(2,1)}, bf16[512,1024]{1,0:T(8,128)(2,1)}, u32[]{:S(2)}, u32[]{:S(2)}) collective-permute-start(bf16[512,1024]{1,0:T(8,128)(2,1)} %get-tuple-element.74), channel_id=1, source_target_pairs={{0,1},{1,0},{2,3},{3,2},{4,5},{5,4},{6,7},{7,6},{8,9},{9,8},{10,11... | collective-permute-start | bytes 3145736 | tf_op jit(solution)/shard_map/swap_x/ppermute | solution.py:40
  33.7 25.0 %collective-permute-start.8 = (bf16[512,1024]{1,0:T(8,128)(2,1)}, bf16[512,1024]{1,0:T(8,128)(2,1)}, u32[]{:S(2)}, u32[]{:S(2)}) collective-permute-start(bf16[512,1024]{1,0:T(8,128)(2,1)} %collective-permute-done.rest_6_.rest_5_), channel_id=1, source_target_pairs={{0,12},{1,13},{2,14},{3,15},{4,0},{5,1},{6,2},{7,3},{8,4},{9,5},{1... | collective-permute-start | bytes 3145736 | tf_op jit(solution)/shard_map/ag_B/ppermute | solution.py:40
  34.7 26.3 %collective-permute-start.13 = (bf16[512,1024]{1,0:T(8,128)(2,1)}, bf16[512,1024]{1,0:T(8,128)(2,1)}, u32[]{:S(2)}, u32[]{:S(2)}) collective-permute-start(bf16[512,1024]{1,0:T(8,128)(2,1)} %collective-permute-done.2.rest_5_.rest_4_), channel_id=1, source_target_pairs={{0,4},{1,5},{2,6},{3,7},{4,8},{5,9},{6,10},{7,11},{8,12},{9,13},{1... | collective-permute-start | bytes 3145736 | tf_op jit(solution)/shard_map/ag_A/ppermute | solution.py:40
  35.2 19.5 %collective-permute-start.11 = (f32[512,128]{1,0:T(8,128)S(1)}, f32[512,128]{1,0:T(8,128)S(1)}, u32[]{:S(2)}, u32[]{:S(2)}) collective-permute-start(f32[512,128]{1,0:T(8,128)S(1)} %copy-done.4), channel_id=1, source_target_pairs={{0,16},{16,0},{32,48},{48,32},{64,80},{80,64},{96,112},{112,96},{1... | collective-permute-start | bytes 786440 | tf_op jit(solution)/shard_map/ppermute | solution.py:49
  54.8 28.4 %collective-permute-start.12 = (bf16[512,1024]{1,0:T(8,128)(2,1)}, bf16[512,1024]{1,0:T(8,128)(2,1)}, u32[]{:S(2)}, u32[]{:S(2)}) collective-permute-start(bf16[512,1024]{1,0:T(8,128)(2,1)} %get-tuple-element.89.rest_3_), channel_id=1, source_target_pairs={{0,2},{1,3},{2,0},{3,1},{4,6},{5,7},{6,4},{7,5},{8,10},{9,11},{10,... | collective-permute-start | bytes 3145736 | tf_op jit(solution)/shard_map/rs_D/ppermute | solution.py:40
  58.7 28.3 %collective-permute-start.9 = (bf16[512,1024]{1,0:T(8,128)(2,1)}, bf16[512,1024]{1,0:T(8,128)(2,1)}, u32[]{:S(2)}, u32[]{:S(2)}) collective-permute-start(bf16[512,1024]{1,0:T(8,128)(2,1)} %collective-permute-done.8.rest_8_.rest_7_), channel_id=1, source_target_pairs={{0,12},{1,13},{2,14},{3,15},{4,0},{5,1},{6,2},{7,3},{8,4},{9,5},{1... | collective-permute-start | bytes 3145736 | tf_op jit(solution)/shard_map/ag_D/ppermute | solution.py:40
  61.0 33.2 %collective-permute-start.14 = (bf16[512,1024]{1,0:T(8,128)(2,1)}, bf16[512,1024]{1,0:T(8,128)(2,1)}, u32[]{:S(2)}, u32[]{:S(2)}) collective-permute-start(bf16[512,1024]{1,0:T(8,128)(2,1)} %collective-permute-done.rest_6_.rest_5_), channel_id=1, source_target_pairs={{0,4},{1,5},{2,6},{3,7},{4,8},{5,9},{6,10},{7,11},{8,12},{9,13},{1... | collective-permute-start | bytes 3145736 | tf_op jit(solution)/shard_map/ag_C/ppermute | solution.py:40
  76.5 39.7 %collective-permute-start.16 = (bf16[512,1024]{1,0:T(8,128)(2,1)}, bf16[512,1024]{1,0:T(8,128)(2,1)}, u32[]{:S(2)}, u32[]{:S(2)}) collective-permute-start(bf16[512,1024]{1,0:T(8,128)(2,1)} %get-tuple-element.97.rest_3_), channel_id=1, source_target_pairs={{0,2},{1,3},{2,0},{3,1},{4,6},{5,7},{6,4},{7,5},{8,10},{9,11},{10,... | collective-permute-start | bytes 3145736 | tf_op jit(solution)/shard_map/rs_B/ppermute | solution.py:40
  76.7 39.6 %collective-permute-start.18 = (bf16[512,1024]{1,0:T(8,128)(2,1)}, bf16[512,1024]{1,0:T(8,128)(2,1)}, u32[]{:S(2)}, u32[]{:S(2)}) collective-permute-start(bf16[512,1024]{1,0:T(8,128)(2,1)} %get-tuple-element.79), channel_id=1, source_target_pairs={{0,1},{1,0},{2,3},{3,2},{4,5},{5,4},{6,7},{7,6},{8,9},{9,8},{10,11... | collective-permute-start | bytes 3145736 | tf_op jit(solution)/shard_map/swap_w0/ppermute | solution.py:40
  83.1 8.1 %collective-permute-start.15 = (f32[512,128]{1,0:T(8,128)S(1)}, f32[512,128]{1,0:T(8,128)S(1)}, u32[]{:S(2)}, u32[]{:S(2)}) collective-permute-start(f32[512,128]{1,0:T(8,128)S(1)} %add.32), channel_id=1, source_target_pairs={{0,32},{16,48},{32,0},{48,16},{64,96},{80,112},{96,64},{112,80},{1... | collective-permute-start | bytes 786440 | tf_op jit(solution)/shard_map/ppermute | solution.py:49
  87.0 29.7 %collective-permute-start.17 = (bf16[512,1024]{1,0:T(8,128)(2,1)}, bf16[512,1024]{1,0:T(8,128)(2,1)}, u32[]{:S(2)}, u32[]{:S(2)}) collective-permute-start(bf16[512,1024]{1,0:T(8,128)(2,1)} %add_convert_fusion), channel_id=1, source_target_pairs={{0,4},{1,5},{2,6},{3,7},{4,8},{5,9},{6,10},{7,11},{8,12},{9,13},{1... | collective-permute-start | bytes 3145736 | tf_op jit(solution)/shard_map/rs_A/ppermute | solution.py:40
  91.2 25.7 %collective-permute-start.10 = (bf16[512,1024]{1,0:T(8,128)(2,1)}, bf16[512,1024]{1,0:T(8,128)(2,1)}, u32[]{:S(2)}, u32[]{:S(2)}) collective-permute-start(bf16[512,1024]{1,0:T(8,128)(2,1)} %get-tuple-element.86.rest_1_), channel_id=1, source_target_pairs={{0,12},{1,13},{2,14},{3,15},{4,0},{5,1},{6,2},{7,3},{8,4},{9,5},{1... | collective-permute-start | bytes 3145736 | tf_op jit(solution)/shard_map/rs_C/ppermute | solution.py:40
  94.2 28.0 %collective-permute-start.19 = (bf16[512,1024]{1,0:T(8,128)(2,1)}, bf16[512,1024]{1,0:T(8,128)(2,1)}, u32[]{:S(2)}, u32[]{:S(2)}) collective-permute-start(bf16[512,1024]{1,0:T(8,128)(2,1)} %get-tuple-element.107), channel_id=1, source_target_pairs={{0,1},{1,0},{2,3},{3,2},{4,5},{5,4},{6,7},{7,6},{8,9},{9,8},{10,11... | collective-permute-start | bytes 3145736 | tf_op jit(solution)/shard_map/swap_w0/ppermute | solution.py:40
  116.2 7.4 %collective-permute-start.22 = (bf16[512,1024]{1,0:T(8,128)(2,1)}, bf16[512,1024]{1,0:T(8,128)(2,1)}, u32[]{:S(2)}, u32[]{:S(2)}) collective-permute-start(bf16[512,1024]{1,0:T(8,128)(2,1)} %get-tuple-element.113), channel_id=1, source_target_pairs={{0,1},{1,0},{2,3},{3,2},{4,5},{5,4},{6,7},{7,6},{8,9},{9,8},{10,11... | collective-permute-start | bytes 3145736 | tf_op jit(solution)/shard_map/swap_w0/ppermute | solution.py:40
  116.3 7.3 %collective-permute-start.23 = (bf16[512,1024]{1,0:T(8,128)(2,1)}, bf16[512,1024]{1,0:T(8,128)(2,1)}, u32[]{:S(2)}, u32[]{:S(2)}) collective-permute-start(bf16[512,1024]{1,0:T(8,128)(2,1)} %get-tuple-element.115), channel_id=1, source_target_pairs={{0,1},{1,0},{2,3},{3,2},{4,5},{5,4},{6,7},{7,6},{8,9},{9,8},{10,11... | collective-permute-start | bytes 3145736 | tf_op jit(solution)/shard_map/swap_w1/ppermute | solution.py:40
  116.8 11.5 %collective-permute-start.21 = (bf16[512,1024]{1,0:T(8,128)(2,1)}, bf16[512,1024]{1,0:T(8,128)(2,1)}, u32[]{:S(2)}, u32[]{:S(2)}) collective-permute-start(bf16[512,1024]{1,0:T(8,128)(2,1)} %get-tuple-element.110), channel_id=1, source_target_pairs={{0,1},{1,0},{2,3},{3,2},{4,5},{5,4},{6,7},{7,6},{8,9},{9,8},{10,11... | collective-permute-start | bytes 3145736 | tf_op jit(solution)/shard_map/swap_w1/ppermute | solution.py:40
  116.9 34.5 %collective-permute-start.20 = (bf16[512,1024]{1,0:T(8,128)(2,1)}, bf16[512,1024]{1,0:T(8,128)(2,1)}, u32[]{:S(2)}, u32[]{:S(2)}) collective-permute-start(bf16[512,1024]{1,0:T(8,128)(2,1)} %get-tuple-element.108), channel_id=1, source_target_pairs={{0,1},{1,0},{2,3},{3,2},{4,5},{5,4},{6,7},{7,6},{8,9},{9,8},{10,11... | collective-permute-start | bytes 3145736 | tf_op jit(solution)/shard_map/swap_w1/ppermute | solution.py:40
  122.2 2.7 %collective-permute-start.28 = (f32[1,4096]{1,0:T(1,128)S(1)}, f32[1,4096]{1,0:T(1,128)S(1)}, u32[]{:S(2)}, u32[]{:S(2)}) collective-permute-start(f32[1,4096]{1,0:T(1,128)S(1)} %copy-done.6), channel_id=1, source_target_pairs={{0,2},{1,3},{2,0},{3,1},{4,6},{5,7},{6,4},{7,5},{8,10},{9,11},{10,... | collective-permute-start | bytes 49160 | tf_op jit(solution)/shard_map/gain_y/ppermute | solution.py:40
  123.6 46.8 %collective-permute-start.26 = (bf16[512,1024]{1,0:T(8,128)(2,1)}, bf16[512,1024]{1,0:T(8,128)(2,1)}, u32[]{:S(2)}, u32[]{:S(2)}) collective-permute-start(bf16[512,1024]{1,0:T(8,128)(2,1)} %get-tuple-element.121), channel_id=1, source_target_pairs={{0,4},{1,5},{2,6},{3,7},{4,8},{5,9},{6,10},{7,11},{8,12},{9,13},{1... | collective-permute-start | bytes 3145736 | tf_op jit(solution)/shard_map/rs_zp/ppermute | solution.py:40
  123.6 46.8 %collective-permute-start.25 = (bf16[512,1024]{1,0:T(8,128)(2,1)}, bf16[512,1024]{1,0:T(8,128)(2,1)}, u32[]{:S(2)}, u32[]{:S(2)}) collective-permute-start(bf16[512,1024]{1,0:T(8,128)(2,1)} %get-tuple-element.120), channel_id=1, source_target_pairs={{0,2},{1,3},{2,0},{3,1},{4,6},{5,7},{6,4},{7,5},{8,10},{9,11},{10,... | collective-permute-start | bytes 3145736 | tf_op jit(solution)/shard_map/rs_y/ppermute | solution.py:40
  124.9 45.5 %collective-permute-start.24 = (bf16[512,1024]{1,0:T(8,128)(2,1)S(1)}, bf16[512,1024]{1,0:T(8,128)(2,1)}, u32[]{:S(2)}, u32[]{:S(2)}) collective-permute-start(bf16[512,1024]{1,0:T(8,128)(2,1)S(1)} %copy-done.3), channel_id=1, source_target_pairs={{0,12},{1,13},{2,14},{3,15},{4,0},{5,1},{6,2},{7,3},{8,4},{9,5},{1... | collective-permute-start | bytes 3145736 | tf_op jit(solution)/shard_map/rs_zm/ppermute | solution.py:40
  128.3 20.5 %collective-permute-start.29 = (f32[1,4096]{1,0:T(1,128)S(1)}, f32[1,4096]{1,0:T(1,128)S(1)}, u32[]{:S(2)}, u32[]{:S(2)}) collective-permute-start(f32[1,4096]{1,0:T(1,128)S(1)} %add.36), channel_id=1, source_target_pairs={{0,4},{1,5},{2,6},{3,7},{4,0},{5,1},{6,2},{7,3},{8,12},{9,13},{10,... | collective-permute-start | bytes 49160 | tf_op jit(solution)/shard_map/ppermute | solution.py:45
  148.8 20.8 %collective-permute-start.27 = (f32[512,128]{1,0:T(8,128)S(1)}, f32[512,128]{1,0:T(8,128)S(1)}, u32[]{:S(2)}, u32[]{:S(2)}) collective-permute-start(f32[512,128]{1,0:T(8,128)S(1)} %add.33), channel_id=1, source_target_pairs={{0,96},{16,112},{32,64},{48,80},{64,32},{80,48},{96,0},{112,16},{1... | collective-permute-start | bytes 786440 | tf_op jit(solution)/shard_map/ppermute | solution.py:49
  151.3 16.6 %collective-permute-start.30 = (f32[1,4096]{1,0:T(1,128)S(1)}, f32[1,4096]{1,0:T(1,128)S(1)}, u32[]{:S(2)}, u32[]{:S(2)}) collective-permute-start(f32[1,4096]{1,0:T(1,128)S(1)} %add.37), channel_id=1, source_target_pairs={{0,12},{1,13},{2,14},{3,15},{4,8},{5,9},{6,10},{7,11},{8,4},{9,5},... | collective-permute-start | bytes 49160 | tf_op jit(solution)/shard_map/ppermute | solution.py:45
  168.0 7.6 %collective-permute-start.31 = (f32[1,4096]{1,0:T(1,128)S(1)}, f32[1,4096]{1,0:T(1,128)S(1)}, u32[]{:S(2)}, u32[]{:S(2)}) collective-permute-start(f32[1,4096]{1,0:T(1,128)S(1)} %add.38), channel_id=1, source_target_pairs={{0,1},{1,0},{2,3},{3,2},{4,5},{5,4},{6,7},{7,6},{8,9},{9,8},{10,11... | collective-permute-start | bytes 49160 | tf_op jit(solution)/shard_map/gain_c/ppermute | solution.py:40
  (7 other events, 65.4 us)

commit v5 on v3

--- a/solution.py
+++ b/solution.py
@@ -592,16 +592,17 @@
     near_order = [(dz, dy) for dz in near_half for dy in range(NY)]
     far_order = [(dz, dy) for dz in far_half for dy in range(NY)]
     near_sums = gain_call(near_order, after(scalars, sent0[0]), g, w)
-    side = shift(after(g[1, 1], sent0[0]), 0, 1, 0, "rs_B")
+    side = shift(after(g[1, 1], near_sums, w[2, 1]), 0, 1, 0, "rs_B")
     left = shift(after(g[3, 1], near_sums, w[2, 1]), -1, 0, 0, "rs_C")
     over = shift(add(g[2, 0], after(far, near_sums)), 1, 0, 0, "rs_A")
+    partial = gain_call(far_order, after(scalars, near_sums, second_sum), g, w, near_sums)
     sent1, own1 = half_call(
-        far_half, after(scalars, sent0[0], far), recv, mine, cots, norm_gain, w, "half_far"
+        far_half, after(scalars, sent0[0], far, partial), recv, mine, cots, norm_gain, w, "half_far"
     )
     got1 = [shift(v, 0, 0, 1, "swap_w1") for v in sent1]
 
-    partial = gain_call(far_order, after(scalars, sent1[0], second_sum), g, w, near_sums)
-    left, side, over = (after(v, partial) for v in (left, side, over))
+    partial = partial + shift(partial, 0, 1, 0, "gain_y")
+    partial = partial + flip_z(after(partial, sent1[0]), 1)
     from_next = shift(after(g[3, 0], left), -1, 0, 0, "rs_zm")
     to_side, to_last = relay_call(g[0, 1], left, g[1, 0], side, over)
     from_side = shift(to_side, 0, 1, 0, "rs_y")
@@ -613,9 +614,7 @@
         (own0[-1], own1[-1], got0[-1], got1[-1]),
     )
 
-    partial = partial + shift(partial, 0, 1, 0, "gain_y")
-    partial = partial + flip_z(partial, 1)
-    partial = partial + flip_z(partial, 3)
+    partial = partial + flip_z(after(partial, to_last), 3)
     other = shift(after(partial, hidden_grad), 0, 0, 1, "gain_c")
     new_weight, anchor_out, momentum_out = update_call(
         inner_rate,

time: 161 us -> 160 us (level)
  waiting for transfers between devices: 19.5 us -> 22.1 us
    ppermute x27, waiting for transfers between devices: 16.9 us -> 11 us  [shift(): return lax.ppermute(x, 'fsdp', pairs)]
    ppermute x2, waiting for transfers between devices: 2.58 us -> 7.42 us  [flip_z(): return lax.ppermute(x, 'fsdp', pairs)]
    ppermute x3, waiting for transfers between devices: 0.01 us -> 3.67 us  [flip_replica(): return lax.ppermute(x, 'replica', [(i, i ^ mask) for i in range(8)])]
  transfers between devices with their start and end apart: 32 -> 32, of which waited for: 11 -> 7; matrix products, arithmetic and copies ran while one was open for 3% -> 3% of each run, Pallas kernels for 59% -> 59%
where the time goes in v5:
time: 160 us
  Pallas kernels  94.4 us (59%)
  starting transfers between devices  35.7 us (22%)
  waiting for transfers between devices  22.1 us (14%)
  other arithmetic  4.17 us (3%)
  local copies, waits for them, and re-layouts  1.69 us (1%)
    pallas_call x2, Pallas kernels, half_call(): pl.pallas_call(functools.partial(half_kernel, depths), grid_spec=pltpu.Pr...  31 us
    ppermute x27, starting transfers between devices, shift(): return lax.ppermute(x, 'fsdp', pairs)  27.6 us
    pallas_call x1, Pallas kernels, grad_call(): pl.pallas_call(functools.partial(grad_kernel, places), grid_spec=pltpu.Pr...  16.8 us
    pallas_call x1, Pallas kernels, hidden_call(): pl.pallas_call(functools.partial(hidden_kernel, depths), grid_spec=pltpu....  13.2 us
    ppermute x27, waiting for transfers between devices, shift(): return lax.ppermute(x, 'fsdp', pairs)  11 us
    pallas_call x2, Pallas kernels, gain_call(): pl.pallas_call(functools.partial(gain_kernel, places, before is not None)...  10.7 us
    pallas_call x1, Pallas kernels, norm_call(): pl.pallas_call(norm_kernel, grid_spec=pltpu.PrefetchScalarGridSpec(num_sc...  10.6 us
    ppermute x2, waiting for transfers between devices, flip_z(): return lax.ppermute(x, 'fsdp', pairs)  7.42 us
  transfers between devices with their start and end apart: 32, of which 7 were waited for; matrix products, arithmetic and copies ran while one was open for 3% of the time, Pallas kernels for 59%

profile of v5, /device:TPU:1, one launch (start us, length us, event | category | flops | bytes accessed | tf_op | source)
XLA Modules:
  0.0 159.6 jit_solution(10963509669743738759)
XLA Ops:
  0.6 2.2 %collective-permute-start = (bf16[512,1024]{1,0:T(8,128)(2,1)}, bf16[512,1024]{1,0:T(8,128)(2,1)}, u32[]{:S(2)}, u32[]{:S(2)}) collective-permute-start(bf16[512,1024]{1,0:T(8,128)(2,1)} %bitcast.13), channel_id=1, source_target_pairs={{0,2},{1,3},{2,0},{3,1},{4,6},{5,7},{6,4},{7,5},{8,10},{9,11},{10,... | collective-permute-start | bytes 3145736 | tf_op jit(solution)/shard_map/ag_y/ppermute | solution.py:40
  2.8 3.8 %collective-permute-start.1 = (bf16[512,1024]{1,0:T(8,128)(2,1)}, bf16[512,1024]{1,0:T(8,128)(2,1)}, u32[]{:S(2)}, u32[]{:S(2)}) collective-permute-start(bf16[512,1024]{1,0:T(8,128)(2,1)} %bitcast.14), channel_id=1, source_target_pairs={{0,12},{1,13},{2,14},{3,15},{4,0},{5,1},{6,2},{7,3},{8,4},{9,5},{1... | collective-permute-start | bytes 3145736 | tf_op jit(solution)/shard_map/ag_zm/ppermute | solution.py:40
  7.9 2.3 %outer_term.1 = f32[512,128]{1,0:T(8,128)} custom-call(s32[6]{0:T(128)} %stack.26.s_ref, bf16[512,1024]{1,0:T(8,128)(2,1)} %bitcast.16, f32[8,1,64,128]{3,2,1,0:T(8,128)} %rest_0_.1, f32[8,1,64,128]{3,2,1,0:T(8,128)} %rest_1_.1), custom_call_target="tpu_custom_call" | custom-call | bytes 3300000 | tf_op jit(solution)/shard_map/outer_term/pallas_call | solution.py:459
  10.3 10.6 %norm.1 = (bf16[512,5120]{1,0:T(8,128)(2,1)}, bf16[512,1024]{1,0:T(8,128)(2,1)}, bf16[512,1024]{1,0:T(8,128)(2,1)}, bf16[512,1024]{1,0:T(8,128)(2,1)}, bf16[512,...) custom-call(s32[6]{0:T(128)} %stack.26.s_ref, bf16[512,8192]{1,0:T(8,128)(2,1)} %bitcast.11, ...), custom_call_target="tpu_custom_call" | custom-call | bytes 26400000 | tf_op jit(solution)/shard_map/norm/pallas_call | solution.py:113
  20.9 1.3 collective-permute-start.3
  22.3 3.3 %collective-permute-done.rest_6_.rest_5_ = bf16[512,1024]{1,0:T(8,128)(2,1)} collective-permute-done((bf16[512,1024]{1,0:T(8,128)(2,1)}, bf16[512,1024]{1,0:T(8,128)(2,1)}, u32[]{:S(2)}, u32[]{:S(2)}) %collective-permute-start) | collective-permute-done | bytes 1048608 | tf_op jit(solution)/shard_map/ag_y/ppermute | solution.py:40
  25.6 1.6 %collective-permute-start.5 = (bf16[512,1024]{1,0:T(8,128)(2,1)}, bf16[512,1024]{1,0:T(8,128)(2,1)}, u32[]{:S(2)}, u32[]{:S(2)}) collective-permute-start(bf16[512,1024]{1,0:T(8,128)(2,1)} %get-tuple-element.67), channel_id=1, source_target_pairs={{0,1},{1,0},{2,3},{3,2},{4,5},{5,4},{6,7},{7,6},{8,9},{9,8},{10,11... | collective-permute-start | bytes 3145736 | tf_op jit(solution)/shard_map/swap_x/ppermute | solution.py:40
  28.4 1.9 %collective-permute-start.6 = (bf16[512,1024]{1,0:T(8,128)(2,1)}, bf16[512,1024]{1,0:T(8,128)(2,1)}, u32[]{:S(2)}, u32[]{:S(2)}) collective-permute-start(bf16[512,1024]{1,0:T(8,128)(2,1)} %get-tuple-element.68), channel_id=1, source_target_pairs={{0,1},{1,0},{2,3},{3,2},{4,5},{5,4},{6,7},{7,6},{8,9},{9,8},{10,11... | collective-permute-start | bytes 3145736 | tf_op jit(solution)/shard_map/swap_x/ppermute | solution.py:40
  30.3 1.2 collective-permute-done.2.rest_4_.rest_5_
  31.5 2.2 %collective-permute-start.7 = (bf16[512,1024]{1,0:T(8,128)(2,1)}, bf16[512,1024]{1,0:T(8,128)(2,1)}, u32[]{:S(2)}, u32[]{:S(2)}) collective-permute-start(bf16[512,1024]{1,0:T(8,128)(2,1)} %get-tuple-element.69), channel_id=1, source_target_pairs={{0,1},{1,0},{2,3},{3,2},{4,5},{5,4},{6,7},{7,6},{8,9},{9,8},{10,11... | collective-permute-start | bytes 3145736 | tf_op jit(solution)/shard_map/swap_x/ppermute | solution.py:40
  35.2 2.6 %collective-permute-start.12 = (f32[512,128]{1,0:T(8,128)S(1)}, f32[512,128]{1,0:T(8,128)S(1)}, u32[]{:S(2)}, u32[]{:S(2)}) collective-permute-start(f32[512,128]{1,0:T(8,128)S(1)} %copy-done.4), channel_id=1, source_target_pairs={{0,16},{16,0},{32,48},{48,32},{64,80},{80,64},{96,112},{112,96},{1... | collective-permute-start | bytes 786440 | tf_op jit(solution)/shard_map/ppermute | solution.py:49
  37.9 16.8 %weight_grad_blocks.1 = (bf16[512,1024]{1,0:T(8,128)(2,1)}, bf16[512,1024]{1,0:T(8,128)(2,1)}, bf16[512,1024]{1,0:T(8,128)(2,1)}, bf16[512,1024]{1,0:T(8,128)(2,...) custom-call(s32[6]{0:T(128)} %stack.26.s_ref, ...), custom_call_target="tpu_custom_call" | custom-call | bytes 52800000 | tf_op jit(solution)/shard_map/weight_grad_blocks/pallas_call | solution.py:186
  54.9 3.8 %collective-permute-done.8.rest_8_.rest_7_ = bf16[512,1024]{1,0:T(8,128)(2,1)} collective-permute-done((bf16[512,1024]{1,0:T(8,128)(2,1)}, bf16[512,1024]{1,0:T(8,128)(2,1)}, u32[]{:S(2)}, u32[]{:S(2)}) %collective-permute-start.8) | collective-permute-done | bytes 1048608 | tf_op jit(solution)/shard_map/ag_B/ppermute | solution.py:40
  59.6 1.4 collective-permute-done.16.rest_6_.rest_7_
  61.0 15.5 %half_near.1 = (bf16[512,1024]{1,0:T(8,128)(2,1)}, bf16[512,1024]{1,0:T(8,128)(2,1)}, bf16[512,1024]{1,0:T(8,128)(2,1)}, bf16[512,1024]{1,0:T(8,128)(2,1)}, bf16...) custom-call(s32[6]{0:T(128)} %stack.26.s_ref, f32[1,8192]{1,0:T(1,128)} %gain_ref.5, bf16[512,1024]{1,0:T(8,128)(2,1)} %copy-done.1, ...), custom_call_target="tpu_custom_call" | custom-call | bytes 33000000 | tf_op jit(solution)/shard_map/half_near/pallas_call | solution.py:311
  77.5 5.3 %gain_grad.2.rest_8_ = f32[1,4096]{1,0:T(1,128)} custom-call(s32[6]{0:T(128)} %stack.26.s_ref, bf16[512,1024]{1,0:T(8,128)(2,1)} %get-tuple-element.107.rest_0_.a_ref, bf16[512,1024]{1,0:T(8,128)(2,1)} %get-tuple-element.76.rest_1_.a_ref, bf16[512,1024]{1,0:T(8,128)(2,1)} %get-tuple-element.77.rest_2_.c_ref, bf16[512,1024]{1,0:T(8,128)(2,1)} %get-tuple-element.82.rest_3_, ...), custom_call_target="tpu_custom_call" | custom-call | tf_op jit(solution)/shard_map/gain_grad/pallas_call | solution.py:498
  82.8 1.3 collective-permute-start.15
  84.1 2.6 %add_convert_fusion = bf16[512,1024]{1,0:T(8,128)(2,1)} fusion(bf16[512,1024]{1,0:T(8,128)(2,1)} %collective-permute-done.13, bf16[512,1024]{1,0:T(8,128)(2,1)S(1)} %copy-done.2), kind=kLoop, calls=%fused_computation | loop fusion | flops 2097152 | bytes 3145728 | tf_op jit(solution)/shard_map/convert_element_type | solution.py:541
  86.7 3.7 %collective-permute-done.15 = f32[512,128]{1,0:T(8,128)S(1)} collective-permute-done((f32[512,128]{1,0:T(8,128)S(1)}, f32[512,128]{1,0:T(8,128)S(1)}, u32[]{:S(2)}, u32[]{:S(2)}) %collective-permute-start.15) | collective-permute-done | bytes 262176 | tf_op jit(solution)/shard_map/ppermute | solution.py:49
  90.4 3.0 %collective-permute-start.10 = (bf16[512,1024]{1,0:T(8,128)(2,1)}, bf16[512,1024]{1,0:T(8,128)(2,1)}, u32[]{:S(2)}, u32[]{:S(2)}) collective-permute-start(bf16[512,1024]{1,0:T(8,128)(2,1)} %get-tuple-element.81.rest_1_), channel_id=1, source_target_pairs={{0,12},{1,13},{2,14},{3,15},{4,0},{5,1},{6,2},{7,3},{8,4},{9,5},{1... | collective-permute-start | bytes 3145736 | tf_op jit(solution)/shard_map/rs_C/ppermute | solution.py:40
  93.6 5.3 %gain_grad.3 = f32[1,4096]{1,0:T(1,128)} custom-call(s32[6]{0:T(128)} %stack.26.s_ref, bf16[512,1024]{1,0:T(8,128)(2,1)} %get-tuple-element.108.rest_0_, bf16[512,1024]{1,0:T(8,128)(2,1)} %get-tuple-element.81.rest_1_, bf16[512,1024]{1,0:T(8,128)(2,1)} %get-tuple-element.79.rest_2_, bf16[512,1024]{1,0:T(8,128)(2,1)} %get-tuple-element.85.rest_3_, ...), custom_call_target="tpu_custom_call" | custom-call | tf_op jit(solution)/shard_map/gain_grad/pallas_call | solution.py:498
  98.9 1.4 collective-permute-start.28
  100.3 2.1 %collective-permute-start.22 = (bf16[512,1024]{1,0:T(8,128)(2,1)}, bf16[512,1024]{1,0:T(8,128)(2,1)}, u32[]{:S(2)}, u32[]{:S(2)}) collective-permute-start(bf16[512,1024]{1,0:T(8,128)(2,1)} %get-tuple-element.103), channel_id=1, source_target_pairs={{0,1},{1,0},{2,3},{3,2},{4,5},{5,4},{6,7},{7,6},{8,9},{9,8},{10,11... | collective-permute-start | bytes 3145736 | tf_op jit(solution)/shard_map/swap_w0/ppermute | solution.py:40
  102.4 15.5 %half_far.1 = (bf16[512,1024]{1,0:T(8,128)(2,1)}, bf16[512,1024]{1,0:T(8,128)(2,1)}, bf16[512,1024]{1,0:T(8,128)(2,1)}, bf16[512,1024]{1,0:T(8,128)(2,1)}, bf16[...) custom-call(s32[6]{0:T(128)} %stack.26.s_ref, f32[1,8192]{1,0:T(1,128)} %gain_ref.5, bf16[512,1024]{1,0:T(8,128)(2,1)} %copy-done.1, ...), custom_call_target="tpu_custom_call" | custom-call | bytes 33000000 | tf_op jit(solution)/shard_map/half_far/pallas_call | solution.py:311
  117.9 1.7 %collective-permute-start.20 = (bf16[512,1024]{1,0:T(8,128)(2,1)}, bf16[512,1024]{1,0:T(8,128)(2,1)}, u32[]{:S(2)}, u32[]{:S(2)}) collective-permute-start(bf16[512,1024]{1,0:T(8,128)(2,1)} %get-tuple-element.99), channel_id=1, source_target_pairs={{0,1},{1,0},{2,3},{3,2},{4,5},{5,4},{6,7},{7,6},{8,9},{9,8},{10,11... | collective-permute-start | bytes 3145736 | tf_op jit(solution)/shard_map/swap_w1/ppermute | solution.py:40
  120.2 4.3 %relay_sums.1 = (bf16[512,1024]{1,0:T(8,128)(2,1)}, bf16[512,1024]{1,0:T(8,128)(2,1)}) custom-call(bf16[512,1024]{1,0:T(8,128)(2,1)} %get-tuple-element.76.rest_1_.a_ref, bf16[512,1024]{1,0:T(8,128)(2,1)} %collective-permute-done.10.b_ref, bf16[512,1024]{1,0:T(8,128)(2,1)} %get-tuple-element.77.rest_2_.c_ref, ...), custom_call_target="tpu_custom_call" | custom-call | bytes 9900000 | tf_op jit(solution)/shard_map/relay_sums/pallas_call | solution.py:521
  126.4 2.6 %collective-permute-start.27 = (f32[512,128]{1,0:T(8,128)S(1)}, f32[512,128]{1,0:T(8,128)S(1)}, u32[]{:S(2)}, u32[]{:S(2)}) collective-permute-start(f32[512,128]{1,0:T(8,128)S(1)} %add.34), channel_id=1, source_target_pairs={{0,96},{16,112},{32,64},{48,80},{64,32},{80,48},{96,0},{112,16},{1... | collective-permute-start | bytes 786440 | tf_op jit(solution)/shard_map/ppermute | solution.py:49
  129.0 1.5 collective-permute-start.30
  130.5 13.2 %hidden_grad.1 = (bf16[512,1024]{1,0:T(8,128)(2,1)}, bf16[512,8192]{1,0:T(8,128)(2,1)}) custom-call(s32[6]{0:T(128)} %stack.26.s_ref, bf16[512,8192]{1,0:T(8,128)(2,1)} %bitcast.12, bf16[512,1024]{1,0:T(8,128)(2,1)} %get-tuple-element.65.rest_1_.c_ref, f32[512,128]{1,0:T(8,128)} %get-tuple-element.88.inv_ref, bf16[512,1024]{1,0:T(8,128)(2,1)} %get-tuple-element.89.rest_0_, ...), custom_call_target="tpu_custom_call" | custom-call | bytes 330000000 | tf_op jit(solution)/shard_map/hidden_grad/pallas_call | solution.py:366
  143.7 7.4 %collective-permute-done.30 = f32[1,4096]{1,0:T(1,128)S(1)} collective-permute-done((f32[1,4096]{1,0:T(1,128)S(1)}, f32[1,4096]{1,0:T(1,128)S(1)}, u32[]{:S(2)}, u32[]{:S(2)}) %collective-permute-start.30) | collective-permute-done | bytes 16416 | tf_op jit(solution)/shard_map/ppermute | solution.py:45
  151.2 1.4 collective-permute-start.31
  153.3 5.4 %update.1 = (bf16[512,1024]{1,0:T(8,128)(2,1)}, f32[8,1,64,128]{3,2,1,0:T(8,128)}, f32[8,1,64,128]{3,2,1,0:T(8,128)}) custom-call(s32[6]{0:T(128)} %stack.26.s_ref, bf16[512,1024]{1,0:T(8,128)(2,1)} %bitcast.19, bf16[512,1024]{1,0:T(8,128)(2,1)} %get-tuple-element.107.rest_0_.a_ref, bf16[512,1024]{1,0:T(8,128)(2,1)} %collective-permute-done.24.b_ref, ...), custom_call_target="tpu_custom_call" | custom-call | bytes 9900000 | tf_op jit(solution)/shard_map/update/pallas_call | solution.py:420
  (71 shorter events, 9.8 us)
Async XLA Ops:
  0.6 25.0 %collective-permute-start = (bf16[512,1024]{1,0:T(8,128)(2,1)}, bf16[512,1024]{1,0:T(8,128)(2,1)}, u32[]{:S(2)}, u32[]{:S(2)}) collective-permute-start(bf16[512,1024]{1,0:T(8,128)(2,1)} %bitcast.13), channel_id=1, source_target_pairs={{0,2},{1,3},{2,0},{3,1},{4,6},{5,7},{6,4},{7,5},{8,10},{9,11},{10,... | collective-permute-start | bytes 3145736 | tf_op jit(solution)/shard_map/ag_y/ppermute | solution.py:40
  2.8 25.6 %collective-permute-start.1 = (bf16[512,1024]{1,0:T(8,128)(2,1)}, bf16[512,1024]{1,0:T(8,128)(2,1)}, u32[]{:S(2)}, u32[]{:S(2)}) collective-permute-start(bf16[512,1024]{1,0:T(8,128)(2,1)} %bitcast.14), channel_id=1, source_target_pairs={{0,12},{1,13},{2,14},{3,15},{4,0},{5,1},{6,2},{7,3},{8,4},{9,5},{1... | collective-permute-start | bytes 3145736 | tf_op jit(solution)/shard_map/ag_zm/ppermute | solution.py:40
  6.6 24.9 %collective-permute-start.2 = (bf16[512,1024]{1,0:T(8,128)(2,1)}, bf16[512,1024]{1,0:T(8,128)(2,1)}, u32[]{:S(2)}, u32[]{:S(2)}) collective-permute-start(bf16[512,1024]{1,0:T(8,128)(2,1)} %bitcast.15), channel_id=1, source_target_pairs={{0,4},{1,5},{2,6},{3,7},{4,8},{5,9},{6,10},{7,11},{8,12},{9,13},{1... | collective-permute-start | bytes 3145736 | tf_op jit(solution)/shard_map/ag_zp/ppermute | solution.py:40
  20.9 12.8 %collective-permute-start.3 = (bf16[512,1024]{1,0:T(8,128)(2,1)}, bf16[512,1024]{1,0:T(8,128)(2,1)S(1)}, u32[]{:S(2)}, u32[]{:S(2)}) collective-permute-start(bf16[512,1024]{1,0:T(8,128)(2,1)} %get-tuple-element.65.rest_1_.c_ref), channel_id=1, source_target_pairs={{0,1},{1,0},{2,3},{3,2},{4,5},{5,4},{6,7},{7,6},{8,9},{9,8},{10,11... | collective-permute-start | bytes 3145736 | tf_op jit(solution)/shard_map/swap_x/ppermute | solution.py:40
  22.2 11.6 %collective-permute-start.4 = (bf16[512,1024]{1,0:T(8,128)(2,1)}, bf16[512,1024]{1,0:T(8,128)(2,1)S(1)}, u32[]{:S(2)}, u32[]{:S(2)}) collective-permute-start(bf16[512,1024]{1,0:T(8,128)(2,1)} %get-tuple-element.66), channel_id=1, source_target_pairs={{0,1},{1,0},{2,3},{3,2},{4,5},{5,4},{6,7},{7,6},{8,9},{9,8},{10,11... | collective-permute-start | bytes 3145736 | tf_op jit(solution)/shard_map/swap_x/ppermute | solution.py:40
  25.6 9.6 %collective-permute-start.5 = (bf16[512,1024]{1,0:T(8,128)(2,1)}, bf16[512,1024]{1,0:T(8,128)(2,1)}, u32[]{:S(2)}, u32[]{:S(2)}) collective-permute-start(bf16[512,1024]{1,0:T(8,128)(2,1)} %get-tuple-element.67), channel_id=1, source_target_pairs={{0,1},{1,0},{2,3},{3,2},{4,5},{5,4},{6,7},{7,6},{8,9},{9,8},{10,11... | collective-permute-start | bytes 3145736 | tf_op jit(solution)/shard_map/swap_x/ppermute | solution.py:40
  28.4 9.5 %collective-permute-start.6 = (bf16[512,1024]{1,0:T(8,128)(2,1)}, bf16[512,1024]{1,0:T(8,128)(2,1)}, u32[]{:S(2)}, u32[]{:S(2)}) collective-permute-start(bf16[512,1024]{1,0:T(8,128)(2,1)} %get-tuple-element.68), channel_id=1, source_target_pairs={{0,1},{1,0},{2,3},{3,2},{4,5},{5,4},{6,7},{7,6},{8,9},{9,8},{10,11... | collective-permute-start | bytes 3145736 | tf_op jit(solution)/shard_map/swap_x/ppermute | solution.py:40
  31.5 6.3 %collective-permute-start.7 = (bf16[512,1024]{1,0:T(8,128)(2,1)}, bf16[512,1024]{1,0:T(8,128)(2,1)}, u32[]{:S(2)}, u32[]{:S(2)}) collective-permute-start(bf16[512,1024]{1,0:T(8,128)(2,1)} %get-tuple-element.69), channel_id=1, source_target_pairs={{0,1},{1,0},{2,3},{3,2},{4,5},{5,4},{6,7},{7,6},{8,9},{9,8},{10,11... | collective-permute-start | bytes 3145736 | tf_op jit(solution)/shard_map/swap_x/ppermute | solution.py:40
  33.7 25.0 %collective-permute-start.8 = (bf16[512,1024]{1,0:T(8,128)(2,1)}, bf16[512,1024]{1,0:T(8,128)(2,1)}, u32[]{:S(2)}, u32[]{:S(2)}) collective-permute-start(bf16[512,1024]{1,0:T(8,128)(2,1)} %collective-permute-done.rest_6_.rest_5_), channel_id=1, source_target_pairs={{0,12},{1,13},{2,14},{3,15},{4,0},{5,1},{6,2},{7,3},{8,4},{9,5},{1... | collective-permute-start | bytes 3145736 | tf_op jit(solution)/shard_map/ag_B/ppermute | solution.py:40
  34.7 26.3 %collective-permute-start.16 = (bf16[512,1024]{1,0:T(8,128)(2,1)}, bf16[512,1024]{1,0:T(8,128)(2,1)}, u32[]{:S(2)}, u32[]{:S(2)}) collective-permute-start(bf16[512,1024]{1,0:T(8,128)(2,1)} %collective-permute-done.2.rest_4_.rest_5_), channel_id=1, source_target_pairs={{0,4},{1,5},{2,6},{3,7},{4,8},{5,9},{6,10},{7,11},{8,12},{9,13},{1... | collective-permute-start | bytes 3145736 | tf_op jit(solution)/shard_map/ag_A/ppermute | solution.py:40
  35.2 19.5 %collective-permute-start.12 = (f32[512,128]{1,0:T(8,128)S(1)}, f32[512,128]{1,0:T(8,128)S(1)}, u32[]{:S(2)}, u32[]{:S(2)}) collective-permute-start(f32[512,128]{1,0:T(8,128)S(1)} %copy-done.4), channel_id=1, source_target_pairs={{0,16},{16,0},{32,48},{48,32},{64,80},{80,64},{96,112},{112,96},{1... | collective-permute-start | bytes 786440 | tf_op jit(solution)/shard_map/ppermute | solution.py:49
  54.8 28.0 %collective-permute-start.13 = (bf16[512,1024]{1,0:T(8,128)(2,1)}, bf16[512,1024]{1,0:T(8,128)(2,1)}, u32[]{:S(2)}, u32[]{:S(2)}) collective-permute-start(bf16[512,1024]{1,0:T(8,128)(2,1)} %get-tuple-element.85.rest_3_), channel_id=1, source_target_pairs={{0,2},{1,3},{2,0},{3,1},{4,6},{5,7},{6,4},{7,5},{8,10},{9,11},{10,... | collective-permute-start | bytes 3145736 | tf_op jit(solution)/shard_map/rs_D/ppermute | solution.py:40
  58.7 28.0 %collective-permute-start.9 = (bf16[512,1024]{1,0:T(8,128)(2,1)}, bf16[512,1024]{1,0:T(8,128)(2,1)}, u32[]{:S(2)}, u32[]{:S(2)}) collective-permute-start(bf16[512,1024]{1,0:T(8,128)(2,1)} %collective-permute-done.8.rest_8_.rest_7_), channel_id=1, source_target_pairs={{0,12},{1,13},{2,14},{3,15},{4,0},{5,1},{6,2},{7,3},{8,4},{9,5},{1... | collective-permute-start | bytes 3145736 | tf_op jit(solution)/shard_map/ag_D/ppermute | solution.py:40
  61.0 32.3 %collective-permute-start.17 = (bf16[512,1024]{1,0:T(8,128)(2,1)}, bf16[512,1024]{1,0:T(8,128)(2,1)}, u32[]{:S(2)}, u32[]{:S(2)}) collective-permute-start(bf16[512,1024]{1,0:T(8,128)(2,1)} %collective-permute-done.rest_6_.rest_5_), channel_id=1, source_target_pairs={{0,4},{1,5},{2,6},{3,7},{4,8},{5,9},{6,10},{7,11},{8,12},{9,13},{1... | collective-permute-start | bytes 3145736 | tf_op jit(solution)/shard_map/ag_C/ppermute | solution.py:40
  76.5 22.4 %collective-permute-start.18 = (bf16[512,1024]{1,0:T(8,128)(2,1)}, bf16[512,1024]{1,0:T(8,128)(2,1)}, u32[]{:S(2)}, u32[]{:S(2)}) collective-permute-start(bf16[512,1024]{1,0:T(8,128)(2,1)} %get-tuple-element.74), channel_id=1, source_target_pairs={{0,1},{1,0},{2,3},{3,2},{4,5},{5,4},{6,7},{7,6},{8,9},{9,8},{10,11... | collective-permute-start | bytes 3145736 | tf_op jit(solution)/shard_map/swap_w0/ppermute | solution.py:40
  77.4 22.9 %collective-permute-start.19 = (bf16[512,1024]{1,0:T(8,128)(2,1)}, bf16[512,1024]{1,0:T(8,128)(2,1)}, u32[]{:S(2)}, u32[]{:S(2)}) collective-permute-start(bf16[512,1024]{1,0:T(8,128)(2,1)} %get-tuple-element.98), channel_id=1, source_target_pairs={{0,1},{1,0},{2,3},{3,2},{4,5},{5,4},{6,7},{7,6},{8,9},{9,8},{10,11... | collective-permute-start | bytes 3145736 | tf_op jit(solution)/shard_map/swap_w0/ppermute | solution.py:40
  82.8 7.5 %collective-permute-start.15 = (f32[512,128]{1,0:T(8,128)S(1)}, f32[512,128]{1,0:T(8,128)S(1)}, u32[]{:S(2)}, u32[]{:S(2)}) collective-permute-start(f32[512,128]{1,0:T(8,128)S(1)} %add.32), channel_id=1, source_target_pairs={{0,32},{16,48},{32,0},{48,16},{64,96},{80,112},{96,64},{112,80},{1... | collective-permute-start | bytes 786440 | tf_op jit(solution)/shard_map/ppermute | solution.py:49
  86.7 32.9 %collective-permute-start.14 = (bf16[512,1024]{1,0:T(8,128)(2,1)}, bf16[512,1024]{1,0:T(8,128)(2,1)}, u32[]{:S(2)}, u32[]{:S(2)}) collective-permute-start(bf16[512,1024]{1,0:T(8,128)(2,1)} %add_convert_fusion), channel_id=1, source_target_pairs={{0,4},{1,5},{2,6},{3,7},{4,8},{5,9},{6,10},{7,11},{8,12},{9,13},{1... | collective-permute-start | bytes 3145736 | tf_op jit(solution)/shard_map/rs_A/ppermute | solution.py:40
  90.4 29.2 %collective-permute-start.10 = (bf16[512,1024]{1,0:T(8,128)(2,1)}, bf16[512,1024]{1,0:T(8,128)(2,1)}, u32[]{:S(2)}, u32[]{:S(2)}) collective-permute-start(bf16[512,1024]{1,0:T(8,128)(2,1)} %get-tuple-element.81.rest_1_), channel_id=1, source_target_pairs={{0,12},{1,13},{2,14},{3,15},{4,0},{5,1},{6,2},{7,3},{8,4},{9,5},{1... | collective-permute-start | bytes 3145736 | tf_op jit(solution)/shard_map/rs_C/ppermute | solution.py:40
  93.3 26.8 %collective-permute-start.11 = (bf16[512,1024]{1,0:T(8,128)(2,1)}, bf16[512,1024]{1,0:T(8,128)(2,1)}, u32[]{:S(2)}, u32[]{:S(2)}) collective-permute-start(bf16[512,1024]{1,0:T(8,128)(2,1)} %get-tuple-element.82.rest_3_), channel_id=1, source_target_pairs={{0,2},{1,3},{2,0},{3,1},{4,6},{5,7},{6,4},{7,5},{8,10},{9,11},{10,... | collective-permute-start | bytes 3145736 | tf_op jit(solution)/shard_map/rs_B/ppermute | solution.py:40
  98.9 19.0 %collective-permute-start.28 = (f32[1,4096]{1,0:T(1,128)}, f32[1,4096]{1,0:T(1,128)S(1)}, u32[]{:S(2)}, u32[]{:S(2)}) collective-permute-start(f32[1,4096]{1,0:T(1,128)} %gain_grad.3), channel_id=1, source_target_pairs={{0,2},{1,3},{2,0},{3,1},{4,6},{5,7},{6,4},{7,5},{8,10},{9,11},{10,... | collective-permute-start | bytes 49160 | tf_op jit(solution)/shard_map/gain_y/ppermute | solution.py:40
  100.3 24.2 %collective-permute-start.22 = (bf16[512,1024]{1,0:T(8,128)(2,1)}, bf16[512,1024]{1,0:T(8,128)(2,1)}, u32[]{:S(2)}, u32[]{:S(2)}) collective-permute-start(bf16[512,1024]{1,0:T(8,128)(2,1)} %get-tuple-element.103), channel_id=1, source_target_pairs={{0,1},{1,0},{2,3},{3,2},{4,5},{5,4},{6,7},{7,6},{8,9},{9,8},{10,11... | collective-permute-start | bytes 3145736 | tf_op jit(solution)/shard_map/swap_w0/ppermute | solution.py:40
  117.9 7.2 %collective-permute-start.20 = (bf16[512,1024]{1,0:T(8,128)(2,1)}, bf16[512,1024]{1,0:T(8,128)(2,1)}, u32[]{:S(2)}, u32[]{:S(2)}) collective-permute-start(bf16[512,1024]{1,0:T(8,128)(2,1)} %get-tuple-element.99), channel_id=1, source_target_pairs={{0,1},{1,0},{2,3},{3,2},{4,5},{5,4},{6,7},{7,6},{8,9},{9,8},{10,11... | collective-permute-start | bytes 3145736 | tf_op jit(solution)/shard_map/swap_w1/ppermute | solution.py:40
  119.6 6.8 %collective-permute-start.21 = (bf16[512,1024]{1,0:T(8,128)(2,1)}, bf16[512,1024]{1,0:T(8,128)(2,1)}, u32[]{:S(2)}, u32[]{:S(2)}) collective-permute-start(bf16[512,1024]{1,0:T(8,128)(2,1)} %get-tuple-element.100), channel_id=1, source_target_pairs={{0,1},{1,0},{2,3},{3,2},{4,5},{5,4},{6,7},{7,6},{8,9},{9,8},{10,11... | collective-permute-start | bytes 3145736 | tf_op jit(solution)/shard_map/swap_w1/ppermute | solution.py:40
  119.6 9.4 %collective-permute-start.23 = (bf16[512,1024]{1,0:T(8,128)(2,1)}, bf16[512,1024]{1,0:T(8,128)(2,1)}, u32[]{:S(2)}, u32[]{:S(2)}) collective-permute-start(bf16[512,1024]{1,0:T(8,128)(2,1)} %get-tuple-element.104), channel_id=1, source_target_pairs={{0,1},{1,0},{2,3},{3,2},{4,5},{5,4},{6,7},{7,6},{8,9},{9,8},{10,11... | collective-permute-start | bytes 3145736 | tf_op jit(solution)/shard_map/swap_w1/ppermute | solution.py:40
  120.1 4.8 %collective-permute-start.29 = (f32[1,4096]{1,0:T(1,128)S(1)}, f32[1,4096]{1,0:T(1,128)S(1)}, u32[]{:S(2)}, u32[]{:S(2)}) collective-permute-start(f32[1,4096]{1,0:T(1,128)S(1)} %add.36), channel_id=1, source_target_pairs={{0,4},{1,5},{2,6},{3,7},{4,0},{5,1},{6,2},{7,3},{8,12},{9,13},{10,... | collective-permute-start | bytes 49160 | tf_op jit(solution)/shard_map/ppermute | solution.py:45
  124.6 28.7 %collective-permute-start.24 = (bf16[512,1024]{1,0:T(8,128)(2,1)S(1)}, bf16[512,1024]{1,0:T(8,128)(2,1)}, u32[]{:S(2)}, u32[]{:S(2)}) collective-permute-start(bf16[512,1024]{1,0:T(8,128)(2,1)S(1)} %copy-done.3), channel_id=1, source_target_pairs={{0,12},{1,13},{2,14},{3,15},{4,0},{5,1},{6,2},{7,3},{8,4},{9,5},{1... | collective-permute-start | bytes 3145736 | tf_op jit(solution)/shard_map/rs_zm/ppermute | solution.py:40
  125.0 28.4 %collective-permute-start.25 = (bf16[512,1024]{1,0:T(8,128)(2,1)}, bf16[512,1024]{1,0:T(8,128)(2,1)}, u32[]{:S(2)}, u32[]{:S(2)}) collective-permute-start(bf16[512,1024]{1,0:T(8,128)(2,1)} %get-tuple-element.109), channel_id=1, source_target_pairs={{0,2},{1,3},{2,0},{3,1},{4,6},{5,7},{6,4},{7,5},{8,10},{9,11},{10,... | collective-permute-start | bytes 3145736 | tf_op jit(solution)/shard_map/rs_y/ppermute | solution.py:40
  125.1 28.2 %collective-permute-start.26 = (bf16[512,1024]{1,0:T(8,128)(2,1)}, bf16[512,1024]{1,0:T(8,128)(2,1)}, u32[]{:S(2)}, u32[]{:S(2)}) collective-permute-start(bf16[512,1024]{1,0:T(8,128)(2,1)} %get-tuple-element.110), channel_id=1, source_target_pairs={{0,4},{1,5},{2,6},{3,7},{4,8},{5,9},{6,10},{7,11},{8,12},{9,13},{1... | collective-permute-start | bytes 3145736 | tf_op jit(solution)/shard_map/rs_zp/ppermute | solution.py:40
  126.4 26.2 %collective-permute-start.27 = (f32[512,128]{1,0:T(8,128)S(1)}, f32[512,128]{1,0:T(8,128)S(1)}, u32[]{:S(2)}, u32[]{:S(2)}) collective-permute-start(f32[512,128]{1,0:T(8,128)S(1)} %add.34), channel_id=1, source_target_pairs={{0,96},{16,112},{32,64},{48,80},{64,32},{80,48},{96,0},{112,16},{1... | collective-permute-start | bytes 786440 | tf_op jit(solution)/shard_map/ppermute | solution.py:49
  129.0 22.2 %collective-permute-start.30 = (f32[1,4096]{1,0:T(1,128)S(1)}, f32[1,4096]{1,0:T(1,128)S(1)}, u32[]{:S(2)}, u32[]{:S(2)}) collective-permute-start(f32[1,4096]{1,0:T(1,128)S(1)} %add.37), channel_id=1, source_target_pairs={{0,12},{1,13},{2,14},{3,15},{4,8},{5,9},{6,10},{7,11},{8,4},{9,5},... | collective-permute-start | bytes 49160 | tf_op jit(solution)/shard_map/ppermute | solution.py:45
  151.2 7.5 %collective-permute-start.31 = (f32[1,4096]{1,0:T(1,128)S(1)}, f32[1,4096]{1,0:T(1,128)S(1)}, u32[]{:S(2)}, u32[]{:S(2)}) collective-permute-start(f32[1,4096]{1,0:T(1,128)S(1)} %add.38), channel_id=1, source_target_pairs={{0,1},{1,0},{2,3},{3,2},{4,5},{5,4},{6,7},{7,6},{8,9},{9,8},{10,11... | collective-permute-start | bytes 49160 | tf_op jit(solution)/shard_map/gain_c/ppermute | solution.py:40
  (7 other events, 78.4 us)

commit v6 on v5

--- a/solution.py
+++ b/solution.py
@@ -591,11 +591,11 @@
     got0 = [shift(v, 0, 0, 1, "swap_w0") for v in sent0]
     near_order = [(dz, dy) for dz in near_half for dy in range(NY)]
     far_order = [(dz, dy) for dz in far_half for dy in range(NY)]
-    near_sums = gain_call(near_order, after(scalars, sent0[0]), g, w)
+    near_sums = gain_call(near_order, after(scalars, sent0[0], second_sum), g, w)
     side = shift(after(g[1, 1], near_sums, w[2, 1]), 0, 1, 0, "rs_B")
     left = shift(after(g[3, 1], near_sums, w[2, 1]), -1, 0, 0, "rs_C")
     over = shift(add(g[2, 0], after(far, near_sums)), 1, 0, 0, "rs_A")
-    partial = gain_call(far_order, after(scalars, near_sums, second_sum), g, w, near_sums)
+    partial = gain_call(far_order, after(scalars, near_sums), g, w, near_sums)
     sent1, own1 = half_call(
         far_half, after(scalars, sent0[0], far, partial), recv, mine, cots, norm_gain, w, "half_far"
     )

time: 160 us -> 156 us (0.975)
  waiting for transfers between devices: 22.1 us -> 17.9 us
    ppermute x3, waiting for transfers between devices: 3.67 us -> 0.01 us  [flip_replica(): return lax.ppermute(x, 'replica', [(i, i ^ mask) for i in range(8)])]
  transfers between devices with their start and end apart: 32 -> 32, of which waited for: 7 -> 7; matrix products, arithmetic and copies ran while one was open for 3% -> 3% of each run, Pallas kernels for 59% -> 61%
where the time goes in v6:
time: 156 us
  Pallas kernels  94.4 us (61%)
  starting transfers between devices  36.1 us (23%)
  waiting for transfers between devices  17.9 us (11%)
  other arithmetic  4.17 us (3%)
  local copies, waits for them, and re-layouts  1.69 us (1%)
    pallas_call x2, Pallas kernels, half_call(): pl.pallas_call(functools.partial(half_kernel, depths), grid_spec=pltpu.Pr...  31 us
    ppermute x27, starting transfers between devices, shift(): return lax.ppermute(x, 'fsdp', pairs)  26.9 us
    pallas_call x1, Pallas kernels, grad_call(): pl.pallas_call(functools.partial(grad_kernel, places), grid_spec=pltpu.Pr...  16.8 us
    pallas_call x1, Pallas kernels, hidden_call(): pl.pallas_call(functools.partial(hidden_kernel, depths), grid_spec=pltpu....  13.2 us
    ppermute x27, waiting for transfers between devices, shift(): return lax.ppermute(x, 'fsdp', pairs)  10.8 us
    pallas_call x2, Pallas kernels, gain_call(): pl.pallas_call(functools.partial(gain_kernel, places, before is not None)...  10.7 us
    pallas_call x1, Pallas kernels, norm_call(): pl.pallas_call(norm_kernel, grid_spec=pltpu.PrefetchScalarGridSpec(num_sc...  10.6 us
    ppermute x2, waiting for transfers between devices, flip_z(): return lax.ppermute(x, 'fsdp', pairs)  7.13 us
  transfers between devices with their start and end apart: 32, of which 7 were waited for; matrix products, arithmetic and copies ran while one was open for 3% of the time, Pallas kernels for 61%

profile of v6, /device:TPU:1, one launch (start us, length us, event | category | flops | bytes accessed | tf_op | source)
XLA Modules:
  0.0 155.8 jit_solution(5570183251029591008)
XLA Ops:
  0.6 2.2 %collective-permute-start = (bf16[512,1024]{1,0:T(8,128)(2,1)}, bf16[512,1024]{1,0:T(8,128)(2,1)}, u32[]{:S(2)}, u32[]{:S(2)}) collective-permute-start(bf16[512,1024]{1,0:T(8,128)(2,1)} %bitcast.13), channel_id=1, source_target_pairs={{0,2},{1,3},{2,0},{3,1},{4,6},{5,7},{6,4},{7,5},{8,10},{9,11},{10,... | collective-permute-start | bytes 3145736 | tf_op jit(solution)/shard_map/ag_y/ppermute | solution.py:40
  2.8 3.8 %collective-permute-start.1 = (bf16[512,1024]{1,0:T(8,128)(2,1)}, bf16[512,1024]{1,0:T(8,128)(2,1)}, u32[]{:S(2)}, u32[]{:S(2)}) collective-permute-start(bf16[512,1024]{1,0:T(8,128)(2,1)} %bitcast.14), channel_id=1, source_target_pairs={{0,12},{1,13},{2,14},{3,15},{4,0},{5,1},{6,2},{7,3},{8,4},{9,5},{1... | collective-permute-start | bytes 3145736 | tf_op jit(solution)/shard_map/ag_zm/ppermute | solution.py:40
  7.9 2.3 %outer_term.1 = f32[512,128]{1,0:T(8,128)} custom-call(s32[6]{0:T(128)} %stack.26.s_ref, bf16[512,1024]{1,0:T(8,128)(2,1)} %bitcast.16, f32[8,1,64,128]{3,2,1,0:T(8,128)} %rest_0_.1, f32[8,1,64,128]{3,2,1,0:T(8,128)} %rest_1_.1), custom_call_target="tpu_custom_call" | custom-call | bytes 3300000 | tf_op jit(solution)/shard_map/outer_term/pallas_call | solution.py:459
  10.3 10.6 %norm.1 = (bf16[512,5120]{1,0:T(8,128)(2,1)}, bf16[512,1024]{1,0:T(8,128)(2,1)}, bf16[512,1024]{1,0:T(8,128)(2,1)}, bf16[512,1024]{1,0:T(8,128)(2,1)}, bf16[512,...) custom-call(s32[6]{0:T(128)} %stack.26.s_ref, bf16[512,8192]{1,0:T(8,128)(2,1)} %bitcast.11, ...), custom_call_target="tpu_custom_call" | custom-call | bytes 26400000 | tf_op jit(solution)/shard_map/norm/pallas_call | solution.py:113
  20.9 1.3 collective-permute-start.3
  22.3 3.3 %collective-permute-done.rest_6_.rest_5_ = bf16[512,1024]{1,0:T(8,128)(2,1)} collective-permute-done((bf16[512,1024]{1,0:T(8,128)(2,1)}, bf16[512,1024]{1,0:T(8,128)(2,1)}, u32[]{:S(2)}, u32[]{:S(2)}) %collective-permute-start) | collective-permute-done | bytes 1048608 | tf_op jit(solution)/shard_map/ag_y/ppermute | solution.py:40
  25.6 1.6 %collective-permute-start.5 = (bf16[512,1024]{1,0:T(8,128)(2,1)}, bf16[512,1024]{1,0:T(8,128)(2,1)}, u32[]{:S(2)}, u32[]{:S(2)}) collective-permute-start(bf16[512,1024]{1,0:T(8,128)(2,1)} %get-tuple-element.67), channel_id=1, source_target_pairs={{0,1},{1,0},{2,3},{3,2},{4,5},{5,4},{6,7},{7,6},{8,9},{9,8},{10,11... | collective-permute-start | bytes 3145736 | tf_op jit(solution)/shard_map/swap_x/ppermute | solution.py:40
  28.4 1.9 %collective-permute-start.6 = (bf16[512,1024]{1,0:T(8,128)(2,1)}, bf16[512,1024]{1,0:T(8,128)(2,1)}, u32[]{:S(2)}, u32[]{:S(2)}) collective-permute-start(bf16[512,1024]{1,0:T(8,128)(2,1)} %get-tuple-element.68), channel_id=1, source_target_pairs={{0,1},{1,0},{2,3},{3,2},{4,5},{5,4},{6,7},{7,6},{8,9},{9,8},{10,11... | collective-permute-start | bytes 3145736 | tf_op jit(solution)/shard_map/swap_x/ppermute | solution.py:40
  30.3 1.2 collective-permute-done.2.rest_4_.rest_5_
  31.5 2.2 %collective-permute-start.7 = (bf16[512,1024]{1,0:T(8,128)(2,1)}, bf16[512,1024]{1,0:T(8,128)(2,1)}, u32[]{:S(2)}, u32[]{:S(2)}) collective-permute-start(bf16[512,1024]{1,0:T(8,128)(2,1)} %get-tuple-element.69), channel_id=1, source_target_pairs={{0,1},{1,0},{2,3},{3,2},{4,5},{5,4},{6,7},{7,6},{8,9},{9,8},{10,11... | collective-permute-start | bytes 3145736 | tf_op jit(solution)/shard_map/swap_x/ppermute | solution.py:40
  35.2 2.6 %collective-permute-start.9 = (f32[512,128]{1,0:T(8,128)S(1)}, f32[512,128]{1,0:T(8,128)S(1)}, u32[]{:S(2)}, u32[]{:S(2)}) collective-permute-start(f32[512,128]{1,0:T(8,128)S(1)} %copy-done.4), channel_id=1, source_target_pairs={{0,16},{16,0},{32,48},{48,32},{64,80},{80,64},{96,112},{112,96},{1... | collective-permute-start | bytes 786440 | tf_op jit(solution)/shard_map/ppermute | solution.py:49
  37.9 16.8 %weight_grad_blocks.1 = (bf16[512,1024]{1,0:T(8,128)(2,1)}, bf16[512,1024]{1,0:T(8,128)(2,1)}, bf16[512,1024]{1,0:T(8,128)(2,1)}, bf16[512,1024]{1,0:T(8,128)(2,...) custom-call(s32[6]{0:T(128)} %stack.26.s_ref, ...), custom_call_target="tpu_custom_call" | custom-call | bytes 52800000 | tf_op jit(solution)/shard_map/weight_grad_blocks/pallas_call | solution.py:186
  54.9 1.3 collective-permute-start.10
  56.2 2.6 %collective-permute-done.8.rest_8_.rest_7_ = bf16[512,1024]{1,0:T(8,128)(2,1)} collective-permute-done((bf16[512,1024]{1,0:T(8,128)(2,1)}, bf16[512,1024]{1,0:T(8,128)(2,1)}, u32[]{:S(2)}, u32[]{:S(2)}) %collective-permute-start.8) | collective-permute-done | bytes 1048608 | tf_op jit(solution)/shard_map/ag_B/ppermute | solution.py:40
  59.6 1.4 collective-permute-done.16.rest_6_.rest_7_
  61.0 15.5 %half_near.1 = (bf16[512,1024]{1,0:T(8,128)(2,1)}, bf16[512,1024]{1,0:T(8,128)(2,1)}, bf16[512,1024]{1,0:T(8,128)(2,1)}, bf16[512,1024]{1,0:T(8,128)(2,1)}, bf16...) custom-call(s32[6]{0:T(128)} %stack.26.s_ref, f32[1,8192]{1,0:T(1,128)} %gain_ref.5, bf16[512,1024]{1,0:T(8,128)(2,1)} %copy-done.1, ...), custom_call_target="tpu_custom_call" | custom-call | bytes 33000000 | tf_op jit(solution)/shard_map/half_near/pallas_call | solution.py:311
  77.5 5.3 %gain_grad.2.rest_8_ = f32[1,4096]{1,0:T(1,128)} custom-call(s32[6]{0:T(128)} %stack.26.s_ref, bf16[512,1024]{1,0:T(8,128)(2,1)} %get-tuple-element.107.rest_0_.a_ref, bf16[512,1024]{1,0:T(8,128)(2,1)} %get-tuple-element.77.rest_1_.a_ref, bf16[512,1024]{1,0:T(8,128)(2,1)} %get-tuple-element.78.rest_2_.c_ref, bf16[512,1024]{1,0:T(8,128)(2,1)} %get-tuple-element.83.rest_3_, ...), custom_call_target="tpu_custom_call" | custom-call | tf_op jit(solution)/shard_map/gain_grad/pallas_call | solution.py:498
  82.9 2.6 %add_convert_fusion = bf16[512,1024]{1,0:T(8,128)(2,1)} fusion(bf16[512,1024]{1,0:T(8,128)(2,1)} %collective-permute-done.14, bf16[512,1024]{1,0:T(8,128)(2,1)S(1)} %copy-done.2), kind=kLoop, calls=%fused_computation | loop fusion | flops 2097152 | bytes 3145728 | tf_op jit(solution)/shard_map/convert_element_type | solution.py:541
  85.5 3.0 %collective-permute-start.12 = (bf16[512,1024]{1,0:T(8,128)(2,1)}, bf16[512,1024]{1,0:T(8,128)(2,1)}, u32[]{:S(2)}, u32[]{:S(2)}) collective-permute-start(bf16[512,1024]{1,0:T(8,128)(2,1)} %get-tuple-element.82.rest_1_), channel_id=1, source_target_pairs={{0,12},{1,13},{2,14},{3,15},{4,0},{5,1},{6,2},{7,3},{8,4},{9,5},{1... | collective-permute-start | bytes 3145736 | tf_op jit(solution)/shard_map/rs_C/ppermute | solution.py:40
  88.6 5.3 %gain_grad.3 = f32[1,4096]{1,0:T(1,128)} custom-call(s32[6]{0:T(128)} %stack.26.s_ref, bf16[512,1024]{1,0:T(8,128)(2,1)} %get-tuple-element.108.rest_0_, bf16[512,1024]{1,0:T(8,128)(2,1)} %get-tuple-element.82.rest_1_, bf16[512,1024]{1,0:T(8,128)(2,1)} %get-tuple-element.80.rest_2_, bf16[512,1024]{1,0:T(8,128)(2,1)} %get-tuple-element.85.rest_3_, ...), custom_call_target="tpu_custom_call" | custom-call | tf_op jit(solution)/shard_map/gain_grad/pallas_call | solution.py:498
  93.9 1.4 collective-permute-start.28
  95.3 1.3 collective-permute-start.22
  96.6 15.5 %half_far.1 = (bf16[512,1024]{1,0:T(8,128)(2,1)}, bf16[512,1024]{1,0:T(8,128)(2,1)}, bf16[512,1024]{1,0:T(8,128)(2,1)}, bf16[512,1024]{1,0:T(8,128)(2,1)}, bf16[...) custom-call(s32[6]{0:T(128)} %stack.26.s_ref, f32[1,8192]{1,0:T(1,128)} %gain_ref.5, bf16[512,1024]{1,0:T(8,128)(2,1)} %copy-done.1, ...), custom_call_target="tpu_custom_call" | custom-call | bytes 33000000 | tf_op jit(solution)/shard_map/half_far/pallas_call | solution.py:311
  113.1 1.5 collective-permute-start.20
  115.2 4.3 %relay_sums.1 = (bf16[512,1024]{1,0:T(8,128)(2,1)}, bf16[512,1024]{1,0:T(8,128)(2,1)}) custom-call(bf16[512,1024]{1,0:T(8,128)(2,1)} %get-tuple-element.77.rest_1_.a_ref, bf16[512,1024]{1,0:T(8,128)(2,1)} %collective-permute-done.12.b_ref, bf16[512,1024]{1,0:T(8,128)(2,1)} %get-tuple-element.78.rest_2_.c_ref, ...), custom_call_target="tpu_custom_call" | custom-call | bytes 9900000 | tf_op jit(solution)/shard_map/relay_sums/pallas_call | solution.py:521
  119.6 1.6 %collective-permute-start.24 = (bf16[512,1024]{1,0:T(8,128)(2,1)S(1)}, bf16[512,1024]{1,0:T(8,128)(2,1)}, u32[]{:S(2)}, u32[]{:S(2)}) collective-permute-start(bf16[512,1024]{1,0:T(8,128)(2,1)S(1)} %copy-done.3), channel_id=1, source_target_pairs={{0,12},{1,13},{2,14},{3,15},{4,0},{5,1},{6,2},{7,3},{8,4},{9,5},{1... | collective-permute-start | bytes 3145736 | tf_op jit(solution)/shard_map/rs_zm/ppermute | solution.py:40
  121.4 2.5 %collective-permute-start.27 = (f32[512,128]{1,0:T(8,128)S(1)}, f32[512,128]{1,0:T(8,128)S(1)}, u32[]{:S(2)}, u32[]{:S(2)}) collective-permute-start(f32[512,128]{1,0:T(8,128)S(1)} %add.33), channel_id=1, source_target_pairs={{0,96},{16,112},{32,64},{48,80},{64,32},{80,48},{96,0},{112,16},{1... | collective-permute-start | bytes 786440 | tf_op jit(solution)/shard_map/ppermute | solution.py:49
  123.9 2.7 %collective-permute-start.30 = (f32[1,4096]{1,0:T(1,128)S(1)}, f32[1,4096]{1,0:T(1,128)S(1)}, u32[]{:S(2)}, u32[]{:S(2)}) collective-permute-start(f32[1,4096]{1,0:T(1,128)S(1)} %add.37), channel_id=1, source_target_pairs={{0,12},{1,13},{2,14},{3,15},{4,8},{5,9},{6,10},{7,11},{8,4},{9,5},... | collective-permute-start | bytes 49160 | tf_op jit(solution)/shard_map/ppermute | solution.py:45
  126.6 13.2 %hidden_grad.1 = (bf16[512,1024]{1,0:T(8,128)(2,1)}, bf16[512,8192]{1,0:T(8,128)(2,1)}) custom-call(s32[6]{0:T(128)} %stack.26.s_ref, bf16[512,8192]{1,0:T(8,128)(2,1)} %bitcast.12, bf16[512,1024]{1,0:T(8,128)(2,1)} %get-tuple-element.65.rest_1_.c_ref, f32[512,128]{1,0:T(8,128)} %get-tuple-element.88.inv_ref, bf16[512,1024]{1,0:T(8,128)(2,1)} %get-tuple-element.89.rest_0_, ...), custom_call_target="tpu_custom_call" | custom-call | bytes 330000000 | tf_op jit(solution)/shard_map/hidden_grad/pallas_call | solution.py:366
  139.8 7.1 %collective-permute-done.30 = f32[1,4096]{1,0:T(1,128)S(1)} collective-permute-done((f32[1,4096]{1,0:T(1,128)S(1)}, f32[1,4096]{1,0:T(1,128)S(1)}, u32[]{:S(2)}, u32[]{:S(2)}) %collective-permute-start.30) | collective-permute-done | bytes 16416 | tf_op jit(solution)/shard_map/ppermute | solution.py:45
  147.0 1.8 %collective-permute-start.31 = (f32[1,4096]{1,0:T(1,128)S(1)}, f32[1,4096]{1,0:T(1,128)S(1)}, u32[]{:S(2)}, u32[]{:S(2)}) collective-permute-start(f32[1,4096]{1,0:T(1,128)S(1)} %add.38), channel_id=1, source_target_pairs={{0,1},{1,0},{2,3},{3,2},{4,5},{5,4},{6,7},{7,6},{8,9},{9,8},{10,11... | collective-permute-start | bytes 49160 | tf_op jit(solution)/shard_map/gain_c/ppermute | solution.py:40
  149.5 5.4 %update.1 = (bf16[512,1024]{1,0:T(8,128)(2,1)}, f32[8,1,64,128]{3,2,1,0:T(8,128)}, f32[8,1,64,128]{3,2,1,0:T(8,128)}) custom-call(s32[6]{0:T(128)} %stack.26.s_ref, bf16[512,1024]{1,0:T(8,128)(2,1)} %bitcast.19, bf16[512,1024]{1,0:T(8,128)(2,1)} %get-tuple-element.107.rest_0_.a_ref, bf16[512,1024]{1,0:T(8,128)(2,1)} %collective-permute-done.24.b_ref, ...), custom_call_target="tpu_custom_call" | custom-call | bytes 9900000 | tf_op jit(solution)/shard_map/update/pallas_call | solution.py:420
  (71 shorter events, 9.2 us)
Async XLA Ops:
  0.6 25.0 %collective-permute-start = (bf16[512,1024]{1,0:T(8,128)(2,1)}, bf16[512,1024]{1,0:T(8,128)(2,1)}, u32[]{:S(2)}, u32[]{:S(2)}) collective-permute-start(bf16[512,1024]{1,0:T(8,128)(2,1)} %bitcast.13), channel_id=1, source_target_pairs={{0,2},{1,3},{2,0},{3,1},{4,6},{5,7},{6,4},{7,5},{8,10},{9,11},{10,... | collective-permute-start | bytes 3145736 | tf_op jit(solution)/shard_map/ag_y/ppermute | solution.py:40
  2.8 25.6 %collective-permute-start.1 = (bf16[512,1024]{1,0:T(8,128)(2,1)}, bf16[512,1024]{1,0:T(8,128)(2,1)}, u32[]{:S(2)}, u32[]{:S(2)}) collective-permute-start(bf16[512,1024]{1,0:T(8,128)(2,1)} %bitcast.14), channel_id=1, source_target_pairs={{0,12},{1,13},{2,14},{3,15},{4,0},{5,1},{6,2},{7,3},{8,4},{9,5},{1... | collective-permute-start | bytes 3145736 | tf_op jit(solution)/shard_map/ag_zm/ppermute | solution.py:40
  6.6 24.9 %collective-permute-start.2 = (bf16[512,1024]{1,0:T(8,128)(2,1)}, bf16[512,1024]{1,0:T(8,128)(2,1)}, u32[]{:S(2)}, u32[]{:S(2)}) collective-permute-start(bf16[512,1024]{1,0:T(8,128)(2,1)} %bitcast.15), channel_id=1, source_target_pairs={{0,4},{1,5},{2,6},{3,7},{4,8},{5,9},{6,10},{7,11},{8,12},{9,13},{1... | collective-permute-start | bytes 3145736 | tf_op jit(solution)/shard_map/ag_zp/ppermute | solution.py:40
  20.9 12.8 %collective-permute-start.3 = (bf16[512,1024]{1,0:T(8,128)(2,1)}, bf16[512,1024]{1,0:T(8,128)(2,1)S(1)}, u32[]{:S(2)}, u32[]{:S(2)}) collective-permute-start(bf16[512,1024]{1,0:T(8,128)(2,1)} %get-tuple-element.65.rest_1_.c_ref), channel_id=1, source_target_pairs={{0,1},{1,0},{2,3},{3,2},{4,5},{5,4},{6,7},{7,6},{8,9},{9,8},{10,11... | collective-permute-start | bytes 3145736 | tf_op jit(solution)/shard_map/swap_x/ppermute | solution.py:40
  22.2 11.6 %collective-permute-start.4 = (bf16[512,1024]{1,0:T(8,128)(2,1)}, bf16[512,1024]{1,0:T(8,128)(2,1)S(1)}, u32[]{:S(2)}, u32[]{:S(2)}) collective-permute-start(bf16[512,1024]{1,0:T(8,128)(2,1)} %get-tuple-element.66), channel_id=1, source_target_pairs={{0,1},{1,0},{2,3},{3,2},{4,5},{5,4},{6,7},{7,6},{8,9},{9,8},{10,11... | collective-permute-start | bytes 3145736 | tf_op jit(solution)/shard_map/swap_x/ppermute | solution.py:40
  25.6 9.6 %collective-permute-start.5 = (bf16[512,1024]{1,0:T(8,128)(2,1)}, bf16[512,1024]{1,0:T(8,128)(2,1)}, u32[]{:S(2)}, u32[]{:S(2)}) collective-permute-start(bf16[512,1024]{1,0:T(8,128)(2,1)} %get-tuple-element.67), channel_id=1, source_target_pairs={{0,1},{1,0},{2,3},{3,2},{4,5},{5,4},{6,7},{7,6},{8,9},{9,8},{10,11... | collective-permute-start | bytes 3145736 | tf_op jit(solution)/shard_map/swap_x/ppermute | solution.py:40
  28.4 9.5 %collective-permute-start.6 = (bf16[512,1024]{1,0:T(8,128)(2,1)}, bf16[512,1024]{1,0:T(8,128)(2,1)}, u32[]{:S(2)}, u32[]{:S(2)}) collective-permute-start(bf16[512,1024]{1,0:T(8,128)(2,1)} %get-tuple-element.68), channel_id=1, source_target_pairs={{0,1},{1,0},{2,3},{3,2},{4,5},{5,4},{6,7},{7,6},{8,9},{9,8},{10,11... | collective-permute-start | bytes 3145736 | tf_op jit(solution)/shard_map/swap_x/ppermute | solution.py:40
  31.5 6.3 %collective-permute-start.7 = (bf16[512,1024]{1,0:T(8,128)(2,1)}, bf16[512,1024]{1,0:T(8,128)(2,1)}, u32[]{:S(2)}, u32[]{:S(2)}) collective-permute-start(bf16[512,1024]{1,0:T(8,128)(2,1)} %get-tuple-element.69), channel_id=1, source_target_pairs={{0,1},{1,0},{2,3},{3,2},{4,5},{5,4},{6,7},{7,6},{8,9},{9,8},{10,11... | collective-permute-start | bytes 3145736 | tf_op jit(solution)/shard_map/swap_x/ppermute | solution.py:40
  33.7 25.0 %collective-permute-start.8 = (bf16[512,1024]{1,0:T(8,128)(2,1)}, bf16[512,1024]{1,0:T(8,128)(2,1)}, u32[]{:S(2)}, u32[]{:S(2)}) collective-permute-start(bf16[512,1024]{1,0:T(8,128)(2,1)} %collective-permute-done.rest_6_.rest_5_), channel_id=1, source_target_pairs={{0,12},{1,13},{2,14},{3,15},{4,0},{5,1},{6,2},{7,3},{8,4},{9,5},{1... | collective-permute-start | bytes 3145736 | tf_op jit(solution)/shard_map/ag_B/ppermute | solution.py:40
  34.7 26.3 %collective-permute-start.16 = (bf16[512,1024]{1,0:T(8,128)(2,1)}, bf16[512,1024]{1,0:T(8,128)(2,1)}, u32[]{:S(2)}, u32[]{:S(2)}) collective-permute-start(bf16[512,1024]{1,0:T(8,128)(2,1)} %collective-permute-done.2.rest_4_.rest_5_), channel_id=1, source_target_pairs={{0,4},{1,5},{2,6},{3,7},{4,8},{5,9},{6,10},{7,11},{8,12},{9,13},{1... | collective-permute-start | bytes 3145736 | tf_op jit(solution)/shard_map/ag_A/ppermute | solution.py:40
  35.2 19.5 %collective-permute-start.9 = (f32[512,128]{1,0:T(8,128)S(1)}, f32[512,128]{1,0:T(8,128)S(1)}, u32[]{:S(2)}, u32[]{:S(2)}) collective-permute-start(f32[512,128]{1,0:T(8,128)S(1)} %copy-done.4), channel_id=1, source_target_pairs={{0,16},{16,0},{32,48},{48,32},{64,80},{80,64},{96,112},{112,96},{1... | collective-permute-start | bytes 786440 | tf_op jit(solution)/shard_map/ppermute | solution.py:49
  54.8 28.1 %collective-permute-start.14 = (bf16[512,1024]{1,0:T(8,128)(2,1)}, bf16[512,1024]{1,0:T(8,128)(2,1)}, u32[]{:S(2)}, u32[]{:S(2)}) collective-permute-start(bf16[512,1024]{1,0:T(8,128)(2,1)} %get-tuple-element.85.rest_3_), channel_id=1, source_target_pairs={{0,2},{1,3},{2,0},{3,1},{4,6},{5,7},{6,4},{7,5},{8,10},{9,11},{10,... | collective-permute-start | bytes 3145736 | tf_op jit(solution)/shard_map/rs_D/ppermute | solution.py:40
  54.9 22.5 %collective-permute-start.10 = (f32[512,128]{1,0:T(8,128)S(1)}, f32[512,128]{1,0:T(8,128)S(1)}, u32[]{:S(2)}, u32[]{:S(2)}) collective-permute-start(f32[512,128]{1,0:T(8,128)S(1)} %add.32), channel_id=1, source_target_pairs={{0,32},{16,48},{32,0},{48,16},{64,96},{80,112},{96,64},{112,80},{1... | collective-permute-start | bytes 786440 | tf_op jit(solution)/shard_map/ppermute | solution.py:49
  58.7 26.7 %collective-permute-start.11 = (bf16[512,1024]{1,0:T(8,128)(2,1)}, bf16[512,1024]{1,0:T(8,128)(2,1)}, u32[]{:S(2)}, u32[]{:S(2)}) collective-permute-start(bf16[512,1024]{1,0:T(8,128)(2,1)} %collective-permute-done.8.rest_8_.rest_7_), channel_id=1, source_target_pairs={{0,12},{1,13},{2,14},{3,15},{4,0},{5,1},{6,2},{7,3},{8,4},{9,5},{1... | collective-permute-start | bytes 3145736 | tf_op jit(solution)/shard_map/ag_D/ppermute | solution.py:40
  61.0 27.4 %collective-permute-start.17 = (bf16[512,1024]{1,0:T(8,128)(2,1)}, bf16[512,1024]{1,0:T(8,128)(2,1)}, u32[]{:S(2)}, u32[]{:S(2)}) collective-permute-start(bf16[512,1024]{1,0:T(8,128)(2,1)} %collective-permute-done.rest_6_.rest_5_), channel_id=1, source_target_pairs={{0,4},{1,5},{2,6},{3,7},{4,8},{5,9},{6,10},{7,11},{8,12},{9,13},{1... | collective-permute-start | bytes 3145736 | tf_op jit(solution)/shard_map/ag_C/ppermute | solution.py:40
  76.5 17.4 %collective-permute-start.18 = (bf16[512,1024]{1,0:T(8,128)(2,1)}, bf16[512,1024]{1,0:T(8,128)(2,1)}, u32[]{:S(2)}, u32[]{:S(2)}) collective-permute-start(bf16[512,1024]{1,0:T(8,128)(2,1)} %get-tuple-element.74), channel_id=1, source_target_pairs={{0,1},{1,0},{2,3},{3,2},{4,5},{5,4},{6,7},{7,6},{8,9},{9,8},{10,11... | collective-permute-start | bytes 3145736 | tf_op jit(solution)/shard_map/swap_w0/ppermute | solution.py:40
  77.4 17.9 %collective-permute-start.19 = (bf16[512,1024]{1,0:T(8,128)(2,1)}, bf16[512,1024]{1,0:T(8,128)(2,1)}, u32[]{:S(2)}, u32[]{:S(2)}) collective-permute-start(bf16[512,1024]{1,0:T(8,128)(2,1)} %get-tuple-element.98), channel_id=1, source_target_pairs={{0,1},{1,0},{2,3},{3,2},{4,5},{5,4},{6,7},{7,6},{8,9},{9,8},{10,11... | collective-permute-start | bytes 3145736 | tf_op jit(solution)/shard_map/swap_w0/ppermute | solution.py:40
  85.5 29.1 %collective-permute-start.15 = (bf16[512,1024]{1,0:T(8,128)(2,1)}, bf16[512,1024]{1,0:T(8,128)(2,1)}, u32[]{:S(2)}, u32[]{:S(2)}) collective-permute-start(bf16[512,1024]{1,0:T(8,128)(2,1)} %add_convert_fusion), channel_id=1, source_target_pairs={{0,4},{1,5},{2,6},{3,7},{4,8},{5,9},{6,10},{7,11},{8,12},{9,13},{1... | collective-permute-start | bytes 3145736 | tf_op jit(solution)/shard_map/rs_A/ppermute | solution.py:40
  85.5 29.1 %collective-permute-start.12 = (bf16[512,1024]{1,0:T(8,128)(2,1)}, bf16[512,1024]{1,0:T(8,128)(2,1)}, u32[]{:S(2)}, u32[]{:S(2)}) collective-permute-start(bf16[512,1024]{1,0:T(8,128)(2,1)} %get-tuple-element.82.rest_1_), channel_id=1, source_target_pairs={{0,12},{1,13},{2,14},{3,15},{4,0},{5,1},{6,2},{7,3},{8,4},{9,5},{1... | collective-permute-start | bytes 3145736 | tf_op jit(solution)/shard_map/rs_C/ppermute | solution.py:40
  88.4 26.7 %collective-permute-start.13 = (bf16[512,1024]{1,0:T(8,128)(2,1)}, bf16[512,1024]{1,0:T(8,128)(2,1)}, u32[]{:S(2)}, u32[]{:S(2)}) collective-permute-start(bf16[512,1024]{1,0:T(8,128)(2,1)} %get-tuple-element.83.rest_3_), channel_id=1, source_target_pairs={{0,2},{1,3},{2,0},{3,1},{4,6},{5,7},{6,4},{7,5},{8,10},{9,11},{10,... | collective-permute-start | bytes 3145736 | tf_op jit(solution)/shard_map/rs_B/ppermute | solution.py:40
  93.9 19.2 %collective-permute-start.28 = (f32[1,4096]{1,0:T(1,128)}, f32[1,4096]{1,0:T(1,128)S(1)}, u32[]{:S(2)}, u32[]{:S(2)}) collective-permute-start(f32[1,4096]{1,0:T(1,128)} %gain_grad.3), channel_id=1, source_target_pairs={{0,2},{1,3},{2,0},{3,1},{4,6},{5,7},{6,4},{7,5},{8,10},{9,11},{10,... | collective-permute-start | bytes 49160 | tf_op jit(solution)/shard_map/gain_y/ppermute | solution.py:40
  95.3 24.2 %collective-permute-start.22 = (bf16[512,1024]{1,0:T(8,128)(2,1)}, bf16[512,1024]{1,0:T(8,128)(2,1)}, u32[]{:S(2)}, u32[]{:S(2)}) collective-permute-start(bf16[512,1024]{1,0:T(8,128)(2,1)} %get-tuple-element.103), channel_id=1, source_target_pairs={{0,1},{1,0},{2,3},{3,2},{4,5},{5,4},{6,7},{7,6},{8,9},{9,8},{10,11... | collective-permute-start | bytes 3145736 | tf_op jit(solution)/shard_map/swap_w0/ppermute | solution.py:40
  113.1 8.2 %collective-permute-start.20 = (bf16[512,1024]{1,0:T(8,128)(2,1)}, bf16[512,1024]{1,0:T(8,128)(2,1)}, u32[]{:S(2)}, u32[]{:S(2)}) collective-permute-start(bf16[512,1024]{1,0:T(8,128)(2,1)} %get-tuple-element.99), channel_id=1, source_target_pairs={{0,1},{1,0},{2,3},{3,2},{4,5},{5,4},{6,7},{7,6},{8,9},{9,8},{10,11... | collective-permute-start | bytes 3145736 | tf_op jit(solution)/shard_map/swap_w1/ppermute | solution.py:40
  114.6 6.8 %collective-permute-start.21 = (bf16[512,1024]{1,0:T(8,128)(2,1)}, bf16[512,1024]{1,0:T(8,128)(2,1)}, u32[]{:S(2)}, u32[]{:S(2)}) collective-permute-start(bf16[512,1024]{1,0:T(8,128)(2,1)} %get-tuple-element.100), channel_id=1, source_target_pairs={{0,1},{1,0},{2,3},{3,2},{4,5},{5,4},{6,7},{7,6},{8,9},{9,8},{10,11... | collective-permute-start | bytes 3145736 | tf_op jit(solution)/shard_map/swap_w1/ppermute | solution.py:40
  114.6 9.4 %collective-permute-start.23 = (bf16[512,1024]{1,0:T(8,128)(2,1)}, bf16[512,1024]{1,0:T(8,128)(2,1)}, u32[]{:S(2)}, u32[]{:S(2)}) collective-permute-start(bf16[512,1024]{1,0:T(8,128)(2,1)} %get-tuple-element.104), channel_id=1, source_target_pairs={{0,1},{1,0},{2,3},{3,2},{4,5},{5,4},{6,7},{7,6},{8,9},{9,8},{10,11... | collective-permute-start | bytes 3145736 | tf_op jit(solution)/shard_map/swap_w1/ppermute | solution.py:40
  115.1 6.1 %collective-permute-start.29 = (f32[1,4096]{1,0:T(1,128)S(1)}, f32[1,4096]{1,0:T(1,128)S(1)}, u32[]{:S(2)}, u32[]{:S(2)}) collective-permute-start(f32[1,4096]{1,0:T(1,128)S(1)} %add.36), channel_id=1, source_target_pairs={{0,4},{1,5},{2,6},{3,7},{4,0},{5,1},{6,2},{7,3},{8,12},{9,13},{10,... | collective-permute-start | bytes 49160 | tf_op jit(solution)/shard_map/ppermute | solution.py:45
  119.6 30.0 %collective-permute-start.24 = (bf16[512,1024]{1,0:T(8,128)(2,1)S(1)}, bf16[512,1024]{1,0:T(8,128)(2,1)}, u32[]{:S(2)}, u32[]{:S(2)}) collective-permute-start(bf16[512,1024]{1,0:T(8,128)(2,1)S(1)} %copy-done.3), channel_id=1, source_target_pairs={{0,12},{1,13},{2,14},{3,15},{4,0},{5,1},{6,2},{7,3},{8,4},{9,5},{1... | collective-permute-start | bytes 3145736 | tf_op jit(solution)/shard_map/rs_zm/ppermute | solution.py:40
  121.2 28.4 %collective-permute-start.25 = (bf16[512,1024]{1,0:T(8,128)(2,1)}, bf16[512,1024]{1,0:T(8,128)(2,1)}, u32[]{:S(2)}, u32[]{:S(2)}) collective-permute-start(bf16[512,1024]{1,0:T(8,128)(2,1)} %get-tuple-element.109), channel_id=1, source_target_pairs={{0,2},{1,3},{2,0},{3,1},{4,6},{5,7},{6,4},{7,5},{8,10},{9,11},{10,... | collective-permute-start | bytes 3145736 | tf_op jit(solution)/shard_map/rs_y/ppermute | solution.py:40
  121.3 28.2 %collective-permute-start.26 = (bf16[512,1024]{1,0:T(8,128)(2,1)}, bf16[512,1024]{1,0:T(8,128)(2,1)}, u32[]{:S(2)}, u32[]{:S(2)}) collective-permute-start(bf16[512,1024]{1,0:T(8,128)(2,1)} %get-tuple-element.110), channel_id=1, source_target_pairs={{0,4},{1,5},{2,6},{3,7},{4,8},{5,9},{6,10},{7,11},{8,12},{9,13},{1... | collective-permute-start | bytes 3145736 | tf_op jit(solution)/shard_map/rs_zp/ppermute | solution.py:40
  121.4 27.4 %collective-permute-start.27 = (f32[512,128]{1,0:T(8,128)S(1)}, f32[512,128]{1,0:T(8,128)S(1)}, u32[]{:S(2)}, u32[]{:S(2)}) collective-permute-start(f32[512,128]{1,0:T(8,128)S(1)} %add.33), channel_id=1, source_target_pairs={{0,96},{16,112},{32,64},{48,80},{64,32},{80,48},{96,0},{112,16},{1... | collective-permute-start | bytes 786440 | tf_op jit(solution)/shard_map/ppermute | solution.py:49
  123.9 23.0 %collective-permute-start.30 = (f32[1,4096]{1,0:T(1,128)S(1)}, f32[1,4096]{1,0:T(1,128)S(1)}, u32[]{:S(2)}, u32[]{:S(2)}) collective-permute-start(f32[1,4096]{1,0:T(1,128)S(1)} %add.37), channel_id=1, source_target_pairs={{0,12},{1,13},{2,14},{3,15},{4,8},{5,9},{6,10},{7,11},{8,4},{9,5},... | collective-permute-start | bytes 49160 | tf_op jit(solution)/shard_map/ppermute | solution.py:45
  147.0 7.9 %collective-permute-start.31 = (f32[1,4096]{1,0:T(1,128)S(1)}, f32[1,4096]{1,0:T(1,128)S(1)}, u32[]{:S(2)}, u32[]{:S(2)}) collective-permute-start(f32[1,4096]{1,0:T(1,128)S(1)} %add.38), channel_id=1, source_target_pairs={{0,1},{1,0},{2,3},{3,2},{4,5},{5,4},{6,7},{7,6},{8,9},{9,8},{10,11... | collective-permute-start | bytes 49160 | tf_op jit(solution)/shard_map/gain_c/ppermute | solution.py:40
  (7 other events, 78.1 us)

commit v7 on v6

--- a/solution.py
+++ b/solution.py
@@ -620,7 +620,7 @@
         inner_rate,
         scalars,
         weight,
-        (after(g[0, 0], hidden_grad), from_next, from_side, from_last),
+        (after(g[0, 0], hidden_grad), from_last, from_side, from_next),
         total,
         anchor,
         momentum,

time: 156 us -> 155 us (level)
  starting transfers between devices: 36.1 us -> 34 us
    ppermute x2, starting transfers between devices: 2.76 us -> 0.49 us  [flip_z(): return lax.ppermute(x, 'fsdp', pairs)]
where the time goes in v7:
time: 155 us; the launch traced here: 154 us
  Pallas kernels  94.3 us (61%)
  starting transfers between devices  34 us (22%)
  waiting for transfers between devices  18.4 us (12%)
  other arithmetic  4.17 us (3%)
  local copies, waits for them, and re-layouts  1.69 us (1%)
    pallas_call x2, Pallas kernels, half_call(): pl.pallas_call(functools.partial(half_kernel, depths), grid_spec=pltpu.Pr...  31 us
    ppermute x27, starting transfers between devices, shift(): return lax.ppermute(x, 'fsdp', pairs)  27.1 us
    pallas_call x1, Pallas kernels, grad_call(): pl.pallas_call(functools.partial(grad_kernel, places), grid_spec=pltpu.Pr...  16.8 us
    pallas_call x1, Pallas kernels, hidden_call(): pl.pallas_call(functools.partial(hidden_kernel, depths), grid_spec=pltpu....  13.2 us
    ppermute x27, waiting for transfers between devices, shift(): return lax.ppermute(x, 'fsdp', pairs)  10.8 us
    pallas_call x2, Pallas kernels, gain_call(): pl.pallas_call(functools.partial(gain_kernel, places, before is not None)...  10.7 us
    pallas_call x1, Pallas kernels, norm_call(): pl.pallas_call(norm_kernel, grid_spec=pltpu.PrefetchScalarGridSpec(num_sc...  10.6 us
    ppermute x2, waiting for transfers between devices, flip_z(): return lax.ppermute(x, 'fsdp', pairs)  7.58 us
  transfers between devices with their start and end apart: 32, of which 7 were waited for; matrix products, arithmetic and copies ran while one was open for 3% of the time, Pallas kernels for 61%

profile of v7, /device:TPU:1, one launch (start us, length us, event | category | flops | bytes accessed | tf_op | source)
XLA Modules:
  0.0 154.0 jit_solution(3047686108468980943)
XLA Ops:
  0.6 2.2 %collective-permute-start = (bf16[512,1024]{1,0:T(8,128)(2,1)}, bf16[512,1024]{1,0:T(8,128)(2,1)}, u32[]{:S(2)}, u32[]{:S(2)}) collective-permute-start(bf16[512,1024]{1,0:T(8,128)(2,1)} %bitcast.13), channel_id=1, source_target_pairs={{0,2},{1,3},{2,0},{3,1},{4,6},{5,7},{6,4},{7,5},{8,10},{9,11},{10,... | collective-permute-start | bytes 3145736 | tf_op jit(solution)/shard_map/ag_y/ppermute | solution.py:40
  2.8 3.8 %collective-permute-start.1 = (bf16[512,1024]{1,0:T(8,128)(2,1)}, bf16[512,1024]{1,0:T(8,128)(2,1)}, u32[]{:S(2)}, u32[]{:S(2)}) collective-permute-start(bf16[512,1024]{1,0:T(8,128)(2,1)} %bitcast.14), channel_id=1, source_target_pairs={{0,12},{1,13},{2,14},{3,15},{4,0},{5,1},{6,2},{7,3},{8,4},{9,5},{1... | collective-permute-start | bytes 3145736 | tf_op jit(solution)/shard_map/ag_zm/ppermute | solution.py:40
  7.9 2.3 %outer_term.1 = f32[512,128]{1,0:T(8,128)} custom-call(s32[6]{0:T(128)} %stack.26.s_ref, bf16[512,1024]{1,0:T(8,128)(2,1)} %bitcast.16, f32[8,1,64,128]{3,2,1,0:T(8,128)} %rest_0_.1, f32[8,1,64,128]{3,2,1,0:T(8,128)} %rest_1_.1), custom_call_target="tpu_custom_call" | custom-call | bytes 3300000 | tf_op jit(solution)/shard_map/outer_term/pallas_call | solution.py:459
  10.3 10.6 %norm.1 = (bf16[512,5120]{1,0:T(8,128)(2,1)}, bf16[512,1024]{1,0:T(8,128)(2,1)}, bf16[512,1024]{1,0:T(8,128)(2,1)}, bf16[512,1024]{1,0:T(8,128)(2,1)}, bf16[512,...) custom-call(s32[6]{0:T(128)} %stack.26.s_ref, bf16[512,8192]{1,0:T(8,128)(2,1)} %bitcast.11, ...), custom_call_target="tpu_custom_call" | custom-call | bytes 26400000 | tf_op jit(solution)/shard_map/norm/pallas_call | solution.py:113
  20.9 1.3 collective-permute-start.3
  22.3 3.3 %collective-permute-done.rest_6_.rest_5_ = bf16[512,1024]{1,0:T(8,128)(2,1)} collective-permute-done((bf16[512,1024]{1,0:T(8,128)(2,1)}, bf16[512,1024]{1,0:T(8,128)(2,1)}, u32[]{:S(2)}, u32[]{:S(2)}) %collective-permute-start) | collective-permute-done | bytes 1048608 | tf_op jit(solution)/shard_map/ag_y/ppermute | solution.py:40
  25.6 1.6 %collective-permute-start.5 = (bf16[512,1024]{1,0:T(8,128)(2,1)}, bf16[512,1024]{1,0:T(8,128)(2,1)}, u32[]{:S(2)}, u32[]{:S(2)}) collective-permute-start(bf16[512,1024]{1,0:T(8,128)(2,1)} %get-tuple-element.67), channel_id=1, source_target_pairs={{0,1},{1,0},{2,3},{3,2},{4,5},{5,4},{6,7},{7,6},{8,9},{9,8},{10,11... | collective-permute-start | bytes 3145736 | tf_op jit(solution)/shard_map/swap_x/ppermute | solution.py:40
  27.3 1.1 collective-permute-done.1.rest_7_.rest_6_
  28.4 1.9 %collective-permute-start.6 = (bf16[512,1024]{1,0:T(8,128)(2,1)}, bf16[512,1024]{1,0:T(8,128)(2,1)}, u32[]{:S(2)}, u32[]{:S(2)}) collective-permute-start(bf16[512,1024]{1,0:T(8,128)(2,1)} %get-tuple-element.68), channel_id=1, source_target_pairs={{0,1},{1,0},{2,3},{3,2},{4,5},{5,4},{6,7},{7,6},{8,9},{9,8},{10,11... | collective-permute-start | bytes 3145736 | tf_op jit(solution)/shard_map/swap_x/ppermute | solution.py:40
  30.3 1.2 collective-permute-done.2.rest_4_.rest_5_
  31.5 2.2 %collective-permute-start.7 = (bf16[512,1024]{1,0:T(8,128)(2,1)}, bf16[512,1024]{1,0:T(8,128)(2,1)}, u32[]{:S(2)}, u32[]{:S(2)}) collective-permute-start(bf16[512,1024]{1,0:T(8,128)(2,1)} %get-tuple-element.69), channel_id=1, source_target_pairs={{0,1},{1,0},{2,3},{3,2},{4,5},{5,4},{6,7},{7,6},{8,9},{9,8},{10,11... | collective-permute-start | bytes 3145736 | tf_op jit(solution)/shard_map/swap_x/ppermute | solution.py:40
  35.2 2.6 %collective-permute-start.9 = (f32[512,128]{1,0:T(8,128)S(1)}, f32[512,128]{1,0:T(8,128)S(1)}, u32[]{:S(2)}, u32[]{:S(2)}) collective-permute-start(f32[512,128]{1,0:T(8,128)S(1)} %copy-done.4), channel_id=1, source_target_pairs={{0,16},{16,0},{32,48},{48,32},{64,80},{80,64},{96,112},{112,96},{1... | collective-permute-start | bytes 786440 | tf_op jit(solution)/shard_map/ppermute | solution.py:49
  37.9 16.8 %weight_grad_blocks.1 = (bf16[512,1024]{1,0:T(8,128)(2,1)}, bf16[512,1024]{1,0:T(8,128)(2,1)}, bf16[512,1024]{1,0:T(8,128)(2,1)}, bf16[512,1024]{1,0:T(8,128)(2,...) custom-call(s32[6]{0:T(128)} %stack.26.s_ref, ...), custom_call_target="tpu_custom_call" | custom-call | bytes 52800000 | tf_op jit(solution)/shard_map/weight_grad_blocks/pallas_call | solution.py:186
  54.9 1.3 collective-permute-start.10
  56.2 2.6 %collective-permute-done.8.rest_8_.rest_7_ = bf16[512,1024]{1,0:T(8,128)(2,1)} collective-permute-done((bf16[512,1024]{1,0:T(8,128)(2,1)}, bf16[512,1024]{1,0:T(8,128)(2,1)}, u32[]{:S(2)}, u32[]{:S(2)}) %collective-permute-start.8) | collective-permute-done | bytes 1048608 | tf_op jit(solution)/shard_map/ag_B/ppermute | solution.py:40
  59.6 1.4 collective-permute-done.16.rest_6_.rest_7_
  61.0 15.5 %half_near.1 = (bf16[512,1024]{1,0:T(8,128)(2,1)}, bf16[512,1024]{1,0:T(8,128)(2,1)}, bf16[512,1024]{1,0:T(8,128)(2,1)}, bf16[512,1024]{1,0:T(8,128)(2,1)}, bf16...) custom-call(s32[6]{0:T(128)} %stack.26.s_ref, f32[1,8192]{1,0:T(1,128)} %gain_ref.5, bf16[512,1024]{1,0:T(8,128)(2,1)} %copy-done.1, ...), custom_call_target="tpu_custom_call" | custom-call | bytes 33000000 | tf_op jit(solution)/shard_map/half_near/pallas_call | solution.py:311
  77.5 5.3 %gain_grad.2.rest_8_ = f32[1,4096]{1,0:T(1,128)} custom-call(s32[6]{0:T(128)} %stack.26.s_ref, bf16[512,1024]{1,0:T(8,128)(2,1)} %get-tuple-element.107.rest_0_.a_ref, bf16[512,1024]{1,0:T(8,128)(2,1)} %get-tuple-element.77.rest_1_.a_ref, bf16[512,1024]{1,0:T(8,128)(2,1)} %get-tuple-element.78.rest_2_.c_ref, bf16[512,1024]{1,0:T(8,128)(2,1)} %get-tuple-element.83.rest_3_, ...), custom_call_target="tpu_custom_call" | custom-call | tf_op jit(solution)/shard_map/gain_grad/pallas_call | solution.py:498
  82.9 2.6 %add_convert_fusion = bf16[512,1024]{1,0:T(8,128)(2,1)} fusion(bf16[512,1024]{1,0:T(8,128)(2,1)} %collective-permute-done.14, bf16[512,1024]{1,0:T(8,128)(2,1)S(1)} %copy-done.2), kind=kLoop, calls=%fused_computation | loop fusion | flops 2097152 | bytes 3145728 | tf_op jit(solution)/shard_map/convert_element_type | solution.py:541
  85.5 3.0 %collective-permute-start.12 = (bf16[512,1024]{1,0:T(8,128)(2,1)}, bf16[512,1024]{1,0:T(8,128)(2,1)}, u32[]{:S(2)}, u32[]{:S(2)}) collective-permute-start(bf16[512,1024]{1,0:T(8,128)(2,1)} %get-tuple-element.82.rest_1_), channel_id=1, source_target_pairs={{0,12},{1,13},{2,14},{3,15},{4,0},{5,1},{6,2},{7,3},{8,4},{9,5},{1... | collective-permute-start | bytes 3145736 | tf_op jit(solution)/shard_map/rs_C/ppermute | solution.py:40
  88.6 5.3 %gain_grad.3 = f32[1,4096]{1,0:T(1,128)} custom-call(s32[6]{0:T(128)} %stack.26.s_ref, bf16[512,1024]{1,0:T(8,128)(2,1)} %get-tuple-element.110.rest_0_, bf16[512,1024]{1,0:T(8,128)(2,1)} %get-tuple-element.82.rest_1_, bf16[512,1024]{1,0:T(8,128)(2,1)} %get-tuple-element.80.rest_2_, bf16[512,1024]{1,0:T(8,128)(2,1)} %get-tuple-element.85.rest_3_, ...), custom_call_target="tpu_custom_call" | custom-call | tf_op jit(solution)/shard_map/gain_grad/pallas_call | solution.py:498
  93.9 1.4 collective-permute-start.28
  95.3 1.3 collective-permute-start.22
  96.6 15.5 %half_far.1 = (bf16[512,1024]{1,0:T(8,128)(2,1)}, bf16[512,1024]{1,0:T(8,128)(2,1)}, bf16[512,1024]{1,0:T(8,128)(2,1)}, bf16[512,1024]{1,0:T(8,128)(2,1)}, bf16[...) custom-call(s32[6]{0:T(128)} %stack.26.s_ref, f32[1,8192]{1,0:T(1,128)} %gain_ref.5, bf16[512,1024]{1,0:T(8,128)(2,1)} %copy-done.1, ...), custom_call_target="tpu_custom_call" | custom-call | bytes 33000000 | tf_op jit(solution)/shard_map/half_far/pallas_call | solution.py:311
  113.1 1.5 collective-permute-start.20
  115.2 4.3 %relay_sums.1 = (bf16[512,1024]{1,0:T(8,128)(2,1)}, bf16[512,1024]{1,0:T(8,128)(2,1)}) custom-call(bf16[512,1024]{1,0:T(8,128)(2,1)} %get-tuple-element.77.rest_1_.a_ref, bf16[512,1024]{1,0:T(8,128)(2,1)} %collective-permute-done.12.b_ref, bf16[512,1024]{1,0:T(8,128)(2,1)} %get-tuple-element.78.rest_2_.c_ref, ...), custom_call_target="tpu_custom_call" | custom-call | bytes 9900000 | tf_op jit(solution)/shard_map/relay_sums/pallas_call | solution.py:521
  119.6 1.5 collective-permute-start.24
  121.3 1.2 collective-permute-start.26
  122.5 2.5 %collective-permute-start.27 = (f32[512,128]{1,0:T(8,128)S(1)}, f32[512,128]{1,0:T(8,128)S(1)}, u32[]{:S(2)}, u32[]{:S(2)}) collective-permute-start(f32[512,128]{1,0:T(8,128)S(1)} %add.33), channel_id=1, source_target_pairs={{0,96},{16,112},{32,64},{48,80},{64,32},{80,48},{96,0},{112,16},{1... | collective-permute-start | bytes 786440 | tf_op jit(solution)/shard_map/ppermute | solution.py:49
  125.4 13.2 %hidden_grad.1 = (bf16[512,1024]{1,0:T(8,128)(2,1)}, bf16[512,8192]{1,0:T(8,128)(2,1)}) custom-call(s32[6]{0:T(128)} %stack.26.s_ref, bf16[512,8192]{1,0:T(8,128)(2,1)} %bitcast.12, bf16[512,1024]{1,0:T(8,128)(2,1)} %get-tuple-element.65.rest_1_.c_ref, f32[512,128]{1,0:T(8,128)} %get-tuple-element.88.inv_ref, bf16[512,1024]{1,0:T(8,128)(2,1)} %get-tuple-element.89.rest_0_, ...), custom_call_target="tpu_custom_call" | custom-call | bytes 330000000 | tf_op jit(solution)/shard_map/hidden_grad/pallas_call | solution.py:366
  138.7 7.6 %collective-permute-done.30 = f32[1,4096]{1,0:T(1,128)S(1)} collective-permute-done((f32[1,4096]{1,0:T(1,128)S(1)}, f32[1,4096]{1,0:T(1,128)S(1)}, u32[]{:S(2)}, u32[]{:S(2)}) %collective-permute-start.30) | collective-permute-done | bytes 16416 | tf_op jit(solution)/shard_map/ppermute | solution.py:45
  147.8 5.3 %update.1 = (bf16[512,1024]{1,0:T(8,128)(2,1)}, f32[8,1,64,128]{3,2,1,0:T(8,128)}, f32[8,1,64,128]{3,2,1,0:T(8,128)}) custom-call(s32[6]{0:T(128)} %stack.26.s_ref, bf16[512,1024]{1,0:T(8,128)(2,1)} %bitcast.19, bf16[512,1024]{1,0:T(8,128)(2,1)} %get-tuple-element.107.rest_0_.a_ref, bf16[512,1024]{1,0:T(8,128)(2,1)} %collective-permute-done.24.b_ref, ...), custom_call_target="tpu_custom_call" | custom-call | bytes 9900000 | tf_op jit(solution)/shard_map/update/pallas_call | solution.py:420
  (71 shorter events, 9.2 us)
Async XLA Ops:
  0.6 25.0 %collective-permute-start = (bf16[512,1024]{1,0:T(8,128)(2,1)}, bf16[512,1024]{1,0:T(8,128)(2,1)}, u32[]{:S(2)}, u32[]{:S(2)}) collective-permute-start(bf16[512,1024]{1,0:T(8,128)(2,1)} %bitcast.13), channel_id=1, source_target_pairs={{0,2},{1,3},{2,0},{3,1},{4,6},{5,7},{6,4},{7,5},{8,10},{9,11},{10,... | collective-permute-start | bytes 3145736 | tf_op jit(solution)/shard_map/ag_y/ppermute | solution.py:40
  2.8 25.6 %collective-permute-start.1 = (bf16[512,1024]{1,0:T(8,128)(2,1)}, bf16[512,1024]{1,0:T(8,128)(2,1)}, u32[]{:S(2)}, u32[]{:S(2)}) collective-permute-start(bf16[512,1024]{1,0:T(8,128)(2,1)} %bitcast.14), channel_id=1, source_target_pairs={{0,12},{1,13},{2,14},{3,15},{4,0},{5,1},{6,2},{7,3},{8,4},{9,5},{1... | collective-permute-start | bytes 3145736 | tf_op jit(solution)/shard_map/ag_zm/ppermute | solution.py:40
  6.6 24.9 %collective-permute-start.2 = (bf16[512,1024]{1,0:T(8,128)(2,1)}, bf16[512,1024]{1,0:T(8,128)(2,1)}, u32[]{:S(2)}, u32[]{:S(2)}) collective-permute-start(bf16[512,1024]{1,0:T(8,128)(2,1)} %bitcast.15), channel_id=1, source_target_pairs={{0,4},{1,5},{2,6},{3,7},{4,8},{5,9},{6,10},{7,11},{8,12},{9,13},{1... | collective-permute-start | bytes 3145736 | tf_op jit(solution)/shard_map/ag_zp/ppermute | solution.py:40
  20.9 12.8 %collective-permute-start.3 = (bf16[512,1024]{1,0:T(8,128)(2,1)}, bf16[512,1024]{1,0:T(8,128)(2,1)S(1)}, u32[]{:S(2)}, u32[]{:S(2)}) collective-permute-start(bf16[512,1024]{1,0:T(8,128)(2,1)} %get-tuple-element.65.rest_1_.c_ref), channel_id=1, source_target_pairs={{0,1},{1,0},{2,3},{3,2},{4,5},{5,4},{6,7},{7,6},{8,9},{9,8},{10,11... | collective-permute-start | bytes 3145736 | tf_op jit(solution)/shard_map/swap_x/ppermute | solution.py:40
  22.2 11.6 %collective-permute-start.4 = (bf16[512,1024]{1,0:T(8,128)(2,1)}, bf16[512,1024]{1,0:T(8,128)(2,1)S(1)}, u32[]{:S(2)}, u32[]{:S(2)}) collective-permute-start(bf16[512,1024]{1,0:T(8,128)(2,1)} %get-tuple-element.66), channel_id=1, source_target_pairs={{0,1},{1,0},{2,3},{3,2},{4,5},{5,4},{6,7},{7,6},{8,9},{9,8},{10,11... | collective-permute-start | bytes 3145736 | tf_op jit(solution)/shard_map/swap_x/ppermute | solution.py:40
  25.6 9.6 %collective-permute-start.5 = (bf16[512,1024]{1,0:T(8,128)(2,1)}, bf16[512,1024]{1,0:T(8,128)(2,1)}, u32[]{:S(2)}, u32[]{:S(2)}) collective-permute-start(bf16[512,1024]{1,0:T(8,128)(2,1)} %get-tuple-element.67), channel_id=1, source_target_pairs={{0,1},{1,0},{2,3},{3,2},{4,5},{5,4},{6,7},{7,6},{8,9},{9,8},{10,11... | collective-permute-start | bytes 3145736 | tf_op jit(solution)/shard_map/swap_x/ppermute | solution.py:40
  28.4 9.5 %collective-permute-start.6 = (bf16[512,1024]{1,0:T(8,128)(2,1)}, bf16[512,1024]{1,0:T(8,128)(2,1)}, u32[]{:S(2)}, u32[]{:S(2)}) collective-permute-start(bf16[512,1024]{1,0:T(8,128)(2,1)} %get-tuple-element.68), channel_id=1, source_target_pairs={{0,1},{1,0},{2,3},{3,2},{4,5},{5,4},{6,7},{7,6},{8,9},{9,8},{10,11... | collective-permute-start | bytes 3145736 | tf_op jit(solution)/shard_map/swap_x/ppermute | solution.py:40
  31.5 6.3 %collective-permute-start.7 = (bf16[512,1024]{1,0:T(8,128)(2,1)}, bf16[512,1024]{1,0:T(8,128)(2,1)}, u32[]{:S(2)}, u32[]{:S(2)}) collective-permute-start(bf16[512,1024]{1,0:T(8,128)(2,1)} %get-tuple-element.69), channel_id=1, source_target_pairs={{0,1},{1,0},{2,3},{3,2},{4,5},{5,4},{6,7},{7,6},{8,9},{9,8},{10,11... | collective-permute-start | bytes 3145736 | tf_op jit(solution)/shard_map/swap_x/ppermute | solution.py:40
  33.7 25.0 %collective-permute-start.8 = (bf16[512,1024]{1,0:T(8,128)(2,1)}, bf16[512,1024]{1,0:T(8,128)(2,1)}, u32[]{:S(2)}, u32[]{:S(2)}) collective-permute-start(bf16[512,1024]{1,0:T(8,128)(2,1)} %collective-permute-done.rest_6_.rest_5_), channel_id=1, source_target_pairs={{0,12},{1,13},{2,14},{3,15},{4,0},{5,1},{6,2},{7,3},{8,4},{9,5},{1... | collective-permute-start | bytes 3145736 | tf_op jit(solution)/shard_map/ag_B/ppermute | solution.py:40
  34.7 26.3 %collective-permute-start.16 = (bf16[512,1024]{1,0:T(8,128)(2,1)}, bf16[512,1024]{1,0:T(8,128)(2,1)}, u32[]{:S(2)}, u32[]{:S(2)}) collective-permute-start(bf16[512,1024]{1,0:T(8,128)(2,1)} %collective-permute-done.2.rest_4_.rest_5_), channel_id=1, source_target_pairs={{0,4},{1,5},{2,6},{3,7},{4,8},{5,9},{6,10},{7,11},{8,12},{9,13},{1... | collective-permute-start | bytes 3145736 | tf_op jit(solution)/shard_map/ag_A/ppermute | solution.py:40
  35.2 19.5 %collective-permute-start.9 = (f32[512,128]{1,0:T(8,128)S(1)}, f32[512,128]{1,0:T(8,128)S(1)}, u32[]{:S(2)}, u32[]{:S(2)}) collective-permute-start(f32[512,128]{1,0:T(8,128)S(1)} %copy-done.4), channel_id=1, source_target_pairs={{0,16},{16,0},{32,48},{48,32},{64,80},{80,64},{96,112},{112,96},{1... | collective-permute-start | bytes 786440 | tf_op jit(solution)/shard_map/ppermute | solution.py:49
  54.8 28.1 %collective-permute-start.14 = (bf16[512,1024]{1,0:T(8,128)(2,1)}, bf16[512,1024]{1,0:T(8,128)(2,1)}, u32[]{:S(2)}, u32[]{:S(2)}) collective-permute-start(bf16[512,1024]{1,0:T(8,128)(2,1)} %get-tuple-element.85.rest_3_), channel_id=1, source_target_pairs={{0,2},{1,3},{2,0},{3,1},{4,6},{5,7},{6,4},{7,5},{8,10},{9,11},{10,... | collective-permute-start | bytes 3145736 | tf_op jit(solution)/shard_map/rs_D/ppermute | solution.py:40
  54.9 22.5 %collective-permute-start.10 = (f32[512,128]{1,0:T(8,128)S(1)}, f32[512,128]{1,0:T(8,128)S(1)}, u32[]{:S(2)}, u32[]{:S(2)}) collective-permute-start(f32[512,128]{1,0:T(8,128)S(1)} %add.32), channel_id=1, source_target_pairs={{0,32},{16,48},{32,0},{48,16},{64,96},{80,112},{96,64},{112,80},{1... | collective-permute-start | bytes 786440 | tf_op jit(solution)/shard_map/ppermute | solution.py:49
  58.7 26.7 %collective-permute-start.11 = (bf16[512,1024]{1,0:T(8,128)(2,1)}, bf16[512,1024]{1,0:T(8,128)(2,1)}, u32[]{:S(2)}, u32[]{:S(2)}) collective-permute-start(bf16[512,1024]{1,0:T(8,128)(2,1)} %collective-permute-done.8.rest_8_.rest_7_), channel_id=1, source_target_pairs={{0,12},{1,13},{2,14},{3,15},{4,0},{5,1},{6,2},{7,3},{8,4},{9,5},{1... | collective-permute-start | bytes 3145736 | tf_op jit(solution)/shard_map/ag_D/ppermute | solution.py:40
  61.0 27.4 %collective-permute-start.17 = (bf16[512,1024]{1,0:T(8,128)(2,1)}, bf16[512,1024]{1,0:T(8,128)(2,1)}, u32[]{:S(2)}, u32[]{:S(2)}) collective-permute-start(bf16[512,1024]{1,0:T(8,128)(2,1)} %collective-permute-done.rest_6_.rest_5_), channel_id=1, source_target_pairs={{0,4},{1,5},{2,6},{3,7},{4,8},{5,9},{6,10},{7,11},{8,12},{9,13},{1... | collective-permute-start | bytes 3145736 | tf_op jit(solution)/shard_map/ag_C/ppermute | solution.py:40
  76.5 17.4 %collective-permute-start.18 = (bf16[512,1024]{1,0:T(8,128)(2,1)}, bf16[512,1024]{1,0:T(8,128)(2,1)}, u32[]{:S(2)}, u32[]{:S(2)}) collective-permute-start(bf16[512,1024]{1,0:T(8,128)(2,1)} %get-tuple-element.74), channel_id=1, source_target_pairs={{0,1},{1,0},{2,3},{3,2},{4,5},{5,4},{6,7},{7,6},{8,9},{9,8},{10,11... | collective-permute-start | bytes 3145736 | tf_op jit(solution)/shard_map/swap_w0/ppermute | solution.py:40
  77.4 17.9 %collective-permute-start.19 = (bf16[512,1024]{1,0:T(8,128)(2,1)}, bf16[512,1024]{1,0:T(8,128)(2,1)}, u32[]{:S(2)}, u32[]{:S(2)}) collective-permute-start(bf16[512,1024]{1,0:T(8,128)(2,1)} %get-tuple-element.98), channel_id=1, source_target_pairs={{0,1},{1,0},{2,3},{3,2},{4,5},{5,4},{6,7},{7,6},{8,9},{9,8},{10,11... | collective-permute-start | bytes 3145736 | tf_op jit(solution)/shard_map/swap_w0/ppermute | solution.py:40
  85.5 29.1 %collective-permute-start.15 = (bf16[512,1024]{1,0:T(8,128)(2,1)}, bf16[512,1024]{1,0:T(8,128)(2,1)}, u32[]{:S(2)}, u32[]{:S(2)}) collective-permute-start(bf16[512,1024]{1,0:T(8,128)(2,1)} %add_convert_fusion), channel_id=1, source_target_pairs={{0,4},{1,5},{2,6},{3,7},{4,8},{5,9},{6,10},{7,11},{8,12},{9,13},{1... | collective-permute-start | bytes 3145736 | tf_op jit(solution)/shard_map/rs_A/ppermute | solution.py:40
  85.5 29.1 %collective-permute-start.12 = (bf16[512,1024]{1,0:T(8,128)(2,1)}, bf16[512,1024]{1,0:T(8,128)(2,1)}, u32[]{:S(2)}, u32[]{:S(2)}) collective-permute-start(bf16[512,1024]{1,0:T(8,128)(2,1)} %get-tuple-element.82.rest_1_), channel_id=1, source_target_pairs={{0,12},{1,13},{2,14},{3,15},{4,0},{5,1},{6,2},{7,3},{8,4},{9,5},{1... | collective-permute-start | bytes 3145736 | tf_op jit(solution)/shard_map/rs_C/ppermute | solution.py:40
  88.4 26.7 %collective-permute-start.13 = (bf16[512,1024]{1,0:T(8,128)(2,1)}, bf16[512,1024]{1,0:T(8,128)(2,1)}, u32[]{:S(2)}, u32[]{:S(2)}) collective-permute-start(bf16[512,1024]{1,0:T(8,128)(2,1)} %get-tuple-element.83.rest_3_), channel_id=1, source_target_pairs={{0,2},{1,3},{2,0},{3,1},{4,6},{5,7},{6,4},{7,5},{8,10},{9,11},{10,... | collective-permute-start | bytes 3145736 | tf_op jit(solution)/shard_map/rs_B/ppermute | solution.py:40
  93.9 19.2 %collective-permute-start.28 = (f32[1,4096]{1,0:T(1,128)}, f32[1,4096]{1,0:T(1,128)S(1)}, u32[]{:S(2)}, u32[]{:S(2)}) collective-permute-start(f32[1,4096]{1,0:T(1,128)} %gain_grad.3), channel_id=1, source_target_pairs={{0,2},{1,3},{2,0},{3,1},{4,6},{5,7},{6,4},{7,5},{8,10},{9,11},{10,... | collective-permute-start | bytes 49160 | tf_op jit(solution)/shard_map/gain_y/ppermute | solution.py:40
  95.3 24.2 %collective-permute-start.22 = (bf16[512,1024]{1,0:T(8,128)(2,1)}, bf16[512,1024]{1,0:T(8,128)(2,1)}, u32[]{:S(2)}, u32[]{:S(2)}) collective-permute-start(bf16[512,1024]{1,0:T(8,128)(2,1)} %get-tuple-element.103), channel_id=1, source_target_pairs={{0,1},{1,0},{2,3},{3,2},{4,5},{5,4},{6,7},{7,6},{8,9},{9,8},{10,11... | collective-permute-start | bytes 3145736 | tf_op jit(solution)/shard_map/swap_w0/ppermute | solution.py:40
  113.1 8.1 %collective-permute-start.20 = (bf16[512,1024]{1,0:T(8,128)(2,1)}, bf16[512,1024]{1,0:T(8,128)(2,1)}, u32[]{:S(2)}, u32[]{:S(2)}) collective-permute-start(bf16[512,1024]{1,0:T(8,128)(2,1)} %get-tuple-element.99), channel_id=1, source_target_pairs={{0,1},{1,0},{2,3},{3,2},{4,5},{5,4},{6,7},{7,6},{8,9},{9,8},{10,11... | collective-permute-start | bytes 3145736 | tf_op jit(solution)/shard_map/swap_w1/ppermute | solution.py:40
  114.6 7.9 %collective-permute-start.21 = (bf16[512,1024]{1,0:T(8,128)(2,1)}, bf16[512,1024]{1,0:T(8,128)(2,1)}, u32[]{:S(2)}, u32[]{:S(2)}) collective-permute-start(bf16[512,1024]{1,0:T(8,128)(2,1)} %get-tuple-element.100), channel_id=1, source_target_pairs={{0,1},{1,0},{2,3},{3,2},{4,5},{5,4},{6,7},{7,6},{8,9},{9,8},{10,11... | collective-permute-start | bytes 3145736 | tf_op jit(solution)/shard_map/swap_w1/ppermute | solution.py:40
  114.6 10.4 %collective-permute-start.23 = (bf16[512,1024]{1,0:T(8,128)(2,1)}, bf16[512,1024]{1,0:T(8,128)(2,1)}, u32[]{:S(2)}, u32[]{:S(2)}) collective-permute-start(bf16[512,1024]{1,0:T(8,128)(2,1)} %get-tuple-element.104), channel_id=1, source_target_pairs={{0,1},{1,0},{2,3},{3,2},{4,5},{5,4},{6,7},{7,6},{8,9},{9,8},{10,11... | collective-permute-start | bytes 3145736 | tf_op jit(solution)/shard_map/swap_w1/ppermute | solution.py:40
  115.1 6.0 %collective-permute-start.29 = (f32[1,4096]{1,0:T(1,128)S(1)}, f32[1,4096]{1,0:T(1,128)S(1)}, u32[]{:S(2)}, u32[]{:S(2)}) collective-permute-start(f32[1,4096]{1,0:T(1,128)S(1)} %add.36), channel_id=1, source_target_pairs={{0,4},{1,5},{2,6},{3,7},{4,0},{5,1},{6,2},{7,3},{8,12},{9,13},{10,... | collective-permute-start | bytes 49160 | tf_op jit(solution)/shard_map/ppermute | solution.py:45
  119.6 28.3 %collective-permute-start.24 = (bf16[512,1024]{1,0:T(8,128)(2,1)}, bf16[512,1024]{1,0:T(8,128)(2,1)}, u32[]{:S(2)}, u32[]{:S(2)}) collective-permute-start(bf16[512,1024]{1,0:T(8,128)(2,1)} %get-tuple-element.108), channel_id=1, source_target_pairs={{0,4},{1,5},{2,6},{3,7},{4,8},{5,9},{6,10},{7,11},{8,12},{9,13},{1... | collective-permute-start | bytes 3145736 | tf_op jit(solution)/shard_map/rs_zp/ppermute | solution.py:40
  121.1 26.7 %collective-permute-start.25 = (bf16[512,1024]{1,0:T(8,128)(2,1)}, bf16[512,1024]{1,0:T(8,128)(2,1)}, u32[]{:S(2)}, u32[]{:S(2)}) collective-permute-start(bf16[512,1024]{1,0:T(8,128)(2,1)} %get-tuple-element.109), channel_id=1, source_target_pairs={{0,2},{1,3},{2,0},{3,1},{4,6},{5,7},{6,4},{7,5},{8,10},{9,11},{10,... | collective-permute-start | bytes 3145736 | tf_op jit(solution)/shard_map/rs_y/ppermute | solution.py:40
  121.3 26.6 %collective-permute-start.26 = (bf16[512,1024]{1,0:T(8,128)(2,1)S(1)}, bf16[512,1024]{1,0:T(8,128)(2,1)}, u32[]{:S(2)}, u32[]{:S(2)}) collective-permute-start(bf16[512,1024]{1,0:T(8,128)(2,1)S(1)} %copy-done.3), channel_id=1, source_target_pairs={{0,12},{1,13},{2,14},{3,15},{4,0},{5,1},{6,2},{7,3},{8,4},{9,5},{1... | collective-permute-start | bytes 3145736 | tf_op jit(solution)/shard_map/rs_zm/ppermute | solution.py:40
  122.5 24.6 %collective-permute-start.27 = (f32[512,128]{1,0:T(8,128)S(1)}, f32[512,128]{1,0:T(8,128)S(1)}, u32[]{:S(2)}, u32[]{:S(2)}) collective-permute-start(f32[512,128]{1,0:T(8,128)S(1)} %add.33), channel_id=1, source_target_pairs={{0,96},{16,112},{32,64},{48,80},{64,32},{80,48},{96,0},{112,16},{1... | collective-permute-start | bytes 786440 | tf_op jit(solution)/shard_map/ppermute | solution.py:49
  125.0 21.2 %collective-permute-start.30 = (f32[1,4096]{1,0:T(1,128)S(1)}, f32[1,4096]{1,0:T(1,128)S(1)}, u32[]{:S(2)}, u32[]{:S(2)}) collective-permute-start(f32[1,4096]{1,0:T(1,128)S(1)} %add.37), channel_id=1, source_target_pairs={{0,12},{1,13},{2,14},{3,15},{4,8},{5,9},{6,10},{7,11},{8,4},{9,5},... | collective-permute-start | bytes 49160 | tf_op jit(solution)/shard_map/ppermute | solution.py:45
  146.3 6.8 %collective-permute-start.31 = (f32[1,4096]{1,0:T(1,128)S(1)}, f32[1,4096]{1,0:T(1,128)S(1)}, u32[]{:S(2)}, u32[]{:S(2)}) collective-permute-start(f32[1,4096]{1,0:T(1,128)S(1)} %add.38), channel_id=1, source_target_pairs={{0,1},{1,0},{2,3},{3,2},{4,5},{5,4},{6,7},{7,6},{8,9},{9,8},{10,11... | collective-permute-start | bytes 49160 | tf_op jit(solution)/shard_map/gain_c/ppermute | solution.py:40
  (7 other events, 79.2 us)
